TPU v7x, 32 devices: a whole 2x2x4 slice. The times are simulated.
32 devices in a mesh: groups: 2 (over y), ctx: 4 (over z), dp: 2 (over x), inner: 2 (over core).
Axes of the slice: x: 2, y: 2, z: 4, core: 2. Of those that a mesh axis runs over, the one named last changes fastest.
Arguments:
- grad_out: bfloat16 [4096, 8192], P(('groups', 'ctx'), ('dp', 'inner')), parts along dimension 0, may hold values from -6 to 6
- saved_x: bfloat16 [4096, 8192], P(('groups', 'ctx'), ('dp', 'inner')), parts along dimension 0, may hold values from -6 to 6
- saved_b: bfloat16 [4096, 2048], P(('groups', 'ctx'), ('dp', 'inner')), parts along dimension 0, may hold values from -1.5 to 1.5
- saved_c: bfloat16 [4096, 2048], P(('groups', 'ctx'), ('dp', 'inner')), parts along dimension 0, may hold values from -1.5 to 1.5
- step_size: bfloat16 [4096, 128], P(('groups', 'ctx'), ('dp', 'inner')), parts along dimension 0, may hold values from 0.0055242717 to 0.022097087
- decay_rate: float32 [128], P(('dp', 'inner')), may hold values from -2.71529 to -0.022097087
- skip_gain: float32 [128], P(('dp', 'inner')), may hold values from 0.5 to 1.5
Outputs:
- grad_x: bfloat16 [4096, 8192], P(('groups', 'ctx'), ('dp', 'inner')), parts along dimension 0
- grad_b: bfloat16 [4096, 2048], P(('groups', 'ctx'), ('dp', 'inner')), parts along dimension 0
- grad_c: bfloat16 [4096, 2048], P(('groups', 'ctx'), ('dp', 'inner')), parts along dimension 0
There are 2 independent parts, one for each index of `groups`. A program takes and returns all parts, laid end to end along the dimension named above; an argument that names none is the same for every part. Nothing has to cross between parts.
All inputs are finite; a program needn't handle non-finite values.
Results may differ from a plain program's by a relative error of at most 0.0063.
Values may be sent and summed in bfloat16 or wider, within the bound.
No kernel may reach another device: no remote copies, remote signals or barrier semaphores. Data moves between devices by JAX's collectives and lax.ppermute only.
A program may use at most 128 MiB of HBM per device.

v0:
```python
from functools import partial
import math

import jax
import jax.numpy as jnp
from jax import lax
from jax.sharding import PartitionSpec as P

P_SIZE = 64
N = 256
SEG = 256


def product(form, left, right):
    return jnp.einsum(form, left, right, preferred_element_type=jnp.float32)


def prepare(step_rows, head_rates, seg_len):
    total, groups, per_group = step_rows.shape
    as_float = step_rows.astype(jnp.float32).reshape(total // seg_len, seg_len, groups, per_group)
    step_sizes = jnp.transpose(as_float, (0, 2, 3, 1))
    cum_decay = jnp.cumsum(step_sizes * head_rates[None, :, :, None], axis=-1)
    return (step_sizes, cum_decay)


def summaries(grad_seg, x_seg, b_seg, c_seg, step_sizes, cum_decay):
    last_cum = cum_decay[..., -1:]
    tail_weight = jnp.moveaxis(jnp.exp(last_cum - cum_decay) * step_sizes, 3, 1)[..., None]
    head_weight = jnp.moveaxis(jnp.exp(cum_decay), 3, 1)[..., None]
    b_weighted = (tail_weight * b_seg[:, :, :, None, :]).astype(jnp.bfloat16)
    c_weighted = (head_weight * c_seg[:, :, :, None, :]).astype(jnp.bfloat16)
    fwd_local = product("ckgjp,ckgjn->cgjpn", x_seg, b_weighted)
    back_local = product("ckgjp,ckgjn->cgjpn", grad_seg, c_weighted)
    return (jnp.exp(last_cum[..., 0]), fwd_local, back_local)


def entering(decays, local_states, reverse):

    def advance(carry, pieces):
        running, state = carry
        decay_now, local_now = pieces
        return (
            (running * decay_now, decay_now[..., None, None] * state + local_now),
            (state, running),
        )

    start = (
        jnp.ones(decays.shape[1:], jnp.float32),
        jnp.zeros(local_states.shape[1:], jnp.float32),
    )
    (total, final), (before, prefix) = lax.scan(
        advance, start, (decays, local_states), reverse=reverse
    )
    return (before, prefix, total, final)


def block_grads(pieces, head_gains):
    grad_seg, x_seg, b_seg, c_seg, step_sizes, cum_decay, fwd_in, back_in = pieces
    seg_len = grad_seg.shape[1]
    places = jnp.arange(seg_len)
    lower_mask = places[:, None] >= places[None, :]
    cum_gap = cum_decay[..., :, None] - cum_decay[..., None, :]
    seg_decay = jnp.where(lower_mask, jnp.exp(jnp.where(lower_mask, cum_gap, 0.0)), 0.0)
    scores = product("ctgn,csgn->cgts", c_seg, b_seg)
    mixing = (seg_decay * scores[:, :, None]).astype(jnp.bfloat16)
    dot_rows = product("ctgjp,csgjp->cgjts", grad_seg, x_seg)
    weighted = (seg_decay * dot_rows * step_sizes[..., None, :]).astype(jnp.bfloat16)
    x_local = product("cgjts,ctgjp->csgjp", mixing, grad_seg)
    b_local = product("cgjts,ctgn->csgjn", weighted, c_seg)
    c_local = product("cgjts,csgn->ctgjn", weighted, b_seg)
    last_cum = cum_decay[..., -1:]
    tail_weight = jnp.moveaxis(jnp.exp(last_cum - cum_decay) * step_sizes, 3, 1)[..., None]
    head_weight = jnp.moveaxis(jnp.exp(cum_decay), 3, 1)[..., None]
    step_rows = jnp.moveaxis(step_sizes, 3, 1)[..., None]
    back_half = back_in.astype(jnp.bfloat16)
    fwd_half = fwd_in.astype(jnp.bfloat16)
    x_carried = product("csgn,cgjpn->csgjp", b_seg, back_half) * tail_weight
    b_carried = product("csgjp,cgjpn->csgjn", x_seg, back_half) * tail_weight
    c_carried = product("ctgjp,cgjpn->ctgjn", grad_seg, fwd_half) * head_weight
    grad_x = (
        step_rows * x_local + x_carried + head_gains[:, :, None] * grad_seg.astype(jnp.float32)
    ).astype(jnp.bfloat16)
    head_b = (b_local + b_carried).astype(jnp.bfloat16)
    head_c = (c_local + c_carried).astype(jnp.bfloat16)
    return (grad_x, head_b, head_c)


def run_blocks(arrays, head_gains):
    seg_count = arrays[0].shape[0]
    items = arrays[0].shape[2] * arrays[0].shape[3]
    per_turn = math.gcd(seg_count, max(1, 16 // items))
    turn_count = seg_count // per_turn
    split_up = tuple((array.reshape((turn_count, per_turn) + array.shape[1:]) for array in arrays))
    results = lax.map(partial(block_grads, head_gains=head_gains), split_up)
    return tuple((result.reshape((seg_count,) + result.shape[2:]) for result in results))


def on_device(grad_out, saved_x, saved_b, saved_c, step_size, decay_rate, skip_gain):
    tokens, row_width = grad_out.shape
    head_count = step_size.shape[1]
    groups = saved_b.shape[1] // N
    per_group = head_count // groups
    ctx_count = lax.axis_size("ctx")
    ctx_rank = lax.axis_index("ctx")
    own_heads = head_count // ctx_count
    all_tokens = tokens * ctx_count
    moved_grad, moved_x, moved_step = (
        lax.all_to_all(
            grad_out.reshape(tokens, head_count, P_SIZE),
            "ctx",
            split_axis=1,
            concat_axis=0,
            tiled=True,
        ),
        lax.all_to_all(
            saved_x.reshape(tokens, head_count, P_SIZE),
            "ctx",
            split_axis=1,
            concat_axis=0,
            tiled=True,
        ),
        lax.all_to_all(
            step_size.reshape(tokens, head_count, 1), "ctx", split_axis=1, concat_axis=0, tiled=True
        ),
    )
    full_b, full_c = (
        lax.all_gather(saved_b, "ctx", axis=0, tiled=True),
        lax.all_gather(saved_c, "ctx", axis=0, tiled=True),
    )
    first_head = ctx_rank * own_heads
    group_id = first_head // per_group
    own_b = lax.dynamic_slice_in_dim(full_b, group_id * N, N, 1)
    own_c = lax.dynamic_slice_in_dim(full_c, group_id * N, N, 1)
    head_rates = lax.dynamic_slice_in_dim(decay_rate, first_head, own_heads, 0).reshape(
        1, own_heads
    )
    head_gains = lax.dynamic_slice_in_dim(skip_gain, first_head, own_heads, 0).reshape(1, own_heads)
    seg_count = all_tokens // SEG
    grad_seg = moved_grad.reshape(seg_count, SEG, 1, own_heads, P_SIZE)
    x_seg = moved_x.reshape(seg_count, SEG, 1, own_heads, P_SIZE)
    b_seg = own_b.reshape(seg_count, SEG, 1, N)
    c_seg = own_c.reshape(seg_count, SEG, 1, N)
    step_sizes, cum_decay = prepare(moved_step.reshape(all_tokens, 1, own_heads), head_rates, SEG)
    decays, fwd_local, back_local = summaries(grad_seg, x_seg, b_seg, c_seg, step_sizes, cum_decay)
    fwd_in = entering(decays, fwd_local, False)[0]
    back_in = entering(decays, back_local, True)[0]
    grad_x, head_b, head_c = run_blocks(
        (grad_seg, x_seg, b_seg, c_seg, step_sizes, cum_decay, fwd_in, back_in), head_gains
    )
    grad_x = grad_x.reshape(all_tokens, own_heads, P_SIZE)
    head_b = head_b.reshape(all_tokens, own_heads, N)
    head_c = head_c.reshape(all_tokens, own_heads, N)
    back_x = lax.all_to_all(grad_x, "ctx", split_axis=0, concat_axis=1, tiled=True)
    term_b = jnp.sum(head_b.astype(jnp.float32), axis=1)
    term_c = jnp.sum(head_c.astype(jnp.float32), axis=1)
    zero_cols = jnp.zeros((all_tokens, groups * N), jnp.float32)
    place_b = lax.dynamic_update_slice_in_dim(zero_cols, term_b, group_id * N, 1)
    place_c = lax.dynamic_update_slice_in_dim(zero_cols, term_c, group_id * N, 1)
    sum_b, sum_c = (
        lax.psum_scatter(place_b, "ctx", scatter_dimension=0, tiled=True),
        lax.psum_scatter(place_c, "ctx", scatter_dimension=0, tiled=True),
    )
    return (
        back_x.reshape(tokens, row_width),
        sum_b.astype(jnp.bfloat16),
        sum_c.astype(jnp.bfloat16),
    )


def solution(mesh):
    return jax.shard_map(
        on_device,
        mesh=mesh,
        in_specs=(
            P(("groups", "ctx"), ("dp", "inner")),
            P(("groups", "ctx"), ("dp", "inner")),
            P(("groups", "ctx"), ("dp", "inner")),
            P(("groups", "ctx"), ("dp", "inner")),
            P(("groups", "ctx"), ("dp", "inner")),
            P(("dp", "inner")),
            P(("dp", "inner")),
        ),
        out_specs=(
            P(("groups", "ctx"), ("dp", "inner")),
            P(("groups", "ctx"), ("dp", "inner")),
            P(("groups", "ctx"), ("dp", "inner")),
        ),
        check_vma=False,
    )
```

profile of v0, /device:TPU:0, one launch (start us, length us, event | category | flops | bytes accessed | tf_op | source)
XLA Modules:
  0.0 536.2 jit_solution(3399859155721091180)
XLA Ops:
  10.0 6.3 %all-to-all-start = ((bf16[4,2,2048]{2,1,0:T(2,128)(2,1)}), bf16[4,2,2048]{2,1,0:T(2,128)(2,1)S(1)}, u32[]{:S(2)}, u32[]{:S(2)}) async-start(bf16[4,2,2048]{2,1,0:T(2,128)(2,1)} %reshape.408), calls=%async_computation | async-start | bytes 65536 | tf_op jit(solution)/shard_map/all_to_all | solution.py:122
  26.3 4.0 copy.156
  30.3 76.4 %all-to-all-done.1 = bf16[512,32,64]{0,2,1:T(8,128)(2,1)S(1)} async-done(((bf16[512,32,64]{0,2,1:T(8,128)(2,1)}), bf16[512,32,64]{0,2,1:T(8,128)(2,1)S(1)}, u32[]{:S(2)}, u32[]{:S(2)}) %all-to-all-start.1) | async-done | bytes 2097184 | tf_op jit(solution)/shard_map/all_to_all | solution.py:108
  108.0 4.4 all-to-all-start.2
  113.6 4.5 reduce-window.6
  118.9 4.6 copy.217
  123.4 4.0 reshape.389
  127.5 4.1 reshape.403
  131.6 62.4 %all-to-all-done.2 = bf16[512,32,64]{0,2,1:T(8,128)(2,1)} async-done(((bf16[512,32,64]{0,2,1:T(8,128)(2,1)}), bf16[512,32,64]{0,2,1:T(8,128)(2,1)}, u32[]{:S(2)}, u32[]{:S(2)}) %all-to-all-start.2) | async-done | bytes 2097184 | tf_op jit(solution)/shard_map/all_to_all | solution.py:115
  193.9 4.5 copy.216
  198.5 4.0 reshape.392
  202.4 4.2 reshape.404
  209.5 4.4 fusion.58
  215.5 15.4 %while.46 = (s32[]{:T(128)}, f32[1,8,64,256]{3,2,1,0:T(8,128)S(1)}, bf16[8,1,8,64,256]{4,3,2,1,0:T(8,128)(2,1)}, f32[8,1,8]{2,1,0:T(1,128)S(1)}, f32[8,1,8,64,256]{4,3,2,1,0:T(8,128)}, /*index=5*/s32[]{:T(128)}, s32[]{:T(128)}) while((s32[]{:T(128)}, f32[1,8,64,256]{3,2,1,0:T(8,128)S(1)}, bf16[8,1,8,64,256]{4,3,2,1,0:T(8,128)(2,1)}, ...), condition=%wide.region_3.4_spmd.clone, body=%wide.region_2.3_spmd.clone.sunk | while | flops 524291 | bytes 2360000 | solution.py:51
  233.8 4.4 fusion.59
  239.9 15.4 %while.45 = (s32[]{:T(128)}, f32[1,8,64,256]{3,2,1,0:T(8,128)S(1)}, bf16[8,1,8,64,256]{4,3,2,1,0:T(8,128)(2,1)}, f32[8,1,8]{2,1,0:T(1,128)S(1)}, f32[8,1,8,64,25...) while((s32[]{:T(128)}, f32[1,8,64,256]{3,2,1,0:T(8,128)S(1)}, ...), condition=%wide.region_5.6_spmd.clone, body=%wide.region_4.5_spmd.clone.sunk | while | flops 524292 | bytes 2359512 | solution.py:51
  255.3 56.9 %while.44 = (s32[]{:T(128)}, bf16[4,2,256,1,8,64]{2,5,4,1,3,0:T(8,128)(2,1)}, bf16[4,2,256,1,8,256]{2,5,4,1,3,0:T(8,128)(2,1)}, bf16[4,2,256,1,8,256]{2,5,4,1,3,...) while((s32[]{:T(128)}, ...), condition=%wide.region_7.8_spmd, body=%wide.region_6.7_spmd.sunk | while | flops 1831673856 | bytes 47945080 | solution.py:94
  312.2 10.3 %convert_reduce_fusion = (f32[4,2,256,256]{2,3,1,0:T(8,128)}, f32[4,2,256,256]{2,3,1,0:T(8,128)S(1)}) fusion(bf16[4,2,256,1,8,256]{2,5,4,1,3,0:T(8,128)(2,1)} %get-tuple-element.206, bf16[4,2,256,1,8,256]{2,5,4,1,3,0:T(8,128)(2,1)} %get-tuple-element.205), kind=kLoop, calls=%fused_computation.77 | loop fusion | flops 15728640 | bytes 20971520 | tf_op jit(solution)/shard_map/reduce_sum | solution.py:155
  335.9 5.2 copy.187
  341.1 4.9 reshape.410
  346.0 99.7 %all_to_all.54 = bf16[4,2,131072]{2,1,0:T(2,128)(2,1)} all-to-all(bf16[4,2,131072]{2,1,0:T(2,128)(2,1)S(1)} %reshape.410), channel_id=1, replica_groups=mesh['groups'=2,'ctx'=4,'dp'=2,'inner'=2] {'ctx'}, dimensions={0} | all-to-all | bytes 4194304 | tf_op jit(solution)/shard_map/all_to_all | solution.py:153
  445.7 5.8 %reshape.411 = bf16[2048,8,64]{2,1,0:T(8,128)(2,1)} reshape(bf16[4,2,131072]{2,1,0:T(2,128)(2,1)} %all_to_all.54) | data formatting | bytes 4194304
  451.5 5.2 copy.188
  464.5 63.1 %reduce-scatter.3.cloned.1.call-done = f32[512,512]{1,0:T(8,128)} async-done(((f32[2048,512]{1,0:T(8,128)}), f32[512,512]{1,0:T(8,128)}) %reduce-scatter.3.cloned.1.call-update) | async-done | bytes 1048592 | tf_op jit(solution)/shard_map/reduce_scatter | solution.py:160
  (180 shorter events, 135.1 us)
Async XLA Ops:
  10.0 12.0 %all-to-all-start = ((bf16[4,2,2048]{2,1,0:T(2,128)(2,1)}), bf16[4,2,2048]{2,1,0:T(2,128)(2,1)S(1)}, u32[]{:S(2)}, u32[]{:S(2)}) async-start(bf16[4,2,2048]{2,1,0:T(2,128)(2,1)} %reshape.408), calls=%async_computation | async-start | bytes 65536 | tf_op jit(solution)/shard_map/all_to_all | solution.py:122
  21.9 84.7 %all-to-all-start.1 = ((bf16[512,32,64]{0,2,1:T(8,128)(2,1)}), bf16[512,32,64]{0,2,1:T(8,128)(2,1)S(1)}, u32[]{:S(2)}, u32[]{:S(2)}) async-start(bf16[512,32,64]{0,2,1:T(8,128)(2,1)} %bitcast.329), calls=%async_computation.1 | async-start | bytes 4194304 | tf_op jit(solution)/shard_map/all_to_all | solution.py:108
  25.5 181.1 %all-gather.5.cloned.1.call-start = ((), (), s32[]{:S(2)}) async-start(), calls=%async_computation.7 | async-start | bytes 2621440 | tf_op jit(solution)/shard_map/all_gather | solution.py:127
  106.7 1.3 copy-start.1
  106.7 6.6 %copy-start.6 = (f32[32]{0:T(128)S(1)}, f32[32]{0:T(128)}, u32[]{:S(2)}) copy-start(f32[32]{0:T(128)} %param.18) | copy-start | bytes 388
  106.7 6.7 %copy-start.7 = (f32[32]{0:T(128)S(1)}, f32[32]{0:T(128)}, u32[]{:S(2)}) copy-start(f32[32]{0:T(128)} %param.19) | copy-start | bytes 388
  108.0 86.0 %all-to-all-start.2 = ((bf16[512,32,64]{0,2,1:T(8,128)(2,1)}), bf16[512,32,64]{0,2,1:T(8,128)(2,1)}, u32[]{:S(2)}, u32[]{:S(2)}) async-start(bf16[512,32,64]{0,2,1:T(8,128)(2,1)} %bitcast.328), calls=%async_computation.2 | async-start | bytes 4194304 | tf_op jit(solution)/shard_map/all_to_all | solution.py:115
  112.4 118.5 %all-gather.3.cloned.1.call-start = ((), (), s32[]{:S(2)}) async-start(), calls=%async_computation.6 | async-start | bytes 2621440 | tf_op jit(solution)/shard_map/all_gather | solution.py:128
  113.2 349.3 %reduce-scatter.5.cloned.1.call-start = ((), (), s32[]{:S(2)}) async-start(), calls=%async_computation.9 | async-start | bytes 5242880 | tf_op jit(solution)/shard_map/reduce_scatter | solution.py:161
  207.9 1.6 copy-start.5
  232.3 1.6 copy-start.4
  259.3 1.6 copy-start
  273.5 1.6 copy-start
  287.6 1.6 copy-start
  301.7 1.6 copy-start
  325.4 2.5 copy-start.3
  329.5 198.2 %reduce-scatter.3.cloned.1.call-start = ((), (), s32[]{:S(2)}) async-start(), calls=%async_computation.8 | async-start | bytes 5242880 | tf_op jit(solution)/shard_map/reduce_scatter | solution.py:160
  331.6 2.8 copy-start.2
Sparse Core Ops, SparseCore 0:
  27.9 74.9 all-gather.4
  114.8 74.5 all-gather.2
  329.6 108.1 reduce-scatter.4
  440.1 87.4 reduce-scatter.2
where the time goes:
time: 539 us; the launch traced here: 536 us
  waiting for transfers between devices  205 us (38%)
  blocking collectives  99.7 us (18%)
  local copies, waits for them, and re-layouts  96.8 us (18%)
  matrix products  54 us (10%)
  other arithmetic  51.4 us (10%)
  starting transfers between devices  14.5 us (3%)
  between operations  14 us (3%)
    all_to_all x1, blocking collectives, on_device(): lax.all_to_all(grad_x, 'ctx', split_axis=0, concat_axis=1, tiled=True)  99.7 us
    all_to_all x1, waiting for transfers between devices, on_device(): lax.all_to_all(grad_out.reshape(tokens, head_count, P_SIZE), 'ctx', split...  76.4 us
    reduce_scatter x1, waiting for transfers between devices, on_device(): lax.psum_scatter(place_b, 'ctx', scatter_dimension=0, tiled=True)  63.1 us
    all_to_all x1, waiting for transfers between devices, on_device(): lax.all_to_all(saved_x.reshape(tokens, head_count, P_SIZE), 'ctx', split_...  62.4 us
    dot_general x34, matrix products, product(): return jnp.einsum(form, left, right, preferred_element_type=jnp.float32)  54 us
    unnamed x23, local copies, waits for them, and re-layouts  27.9 us
    add x16, other arithmetic, advance(): decay_now[..., None, None] * state + local_now  18.5 us
    dynamic_update_slice x16, other arithmetic, entering(): lax.scan(advance, start, (decays, local_states), reverse=reverse)  12 us
  transfers between devices with their start and end apart: 7, of which 4 were waited for; matrix products, arithmetic and copies ran while one was open for 18% of the time, Pallas kernels for 0%

commit v1 on v0

v1 whole, which is shorter than its diff:
```python
from functools import partial

import jax
import jax.numpy as jnp
from jax import lax
from jax.experimental import pallas as pl
from jax.experimental.pallas import tpu as pltpu
from jax.sharding import PartitionSpec as P

P_SIZE = 64
N = 256
CHUNK = 512
CHUNK_HEADS = CHUNK // P_SIZE
F32 = jnp.float32
BF16 = jnp.bfloat16
MIB = 1024 * 1024


def dot(left, right, left_dim, right_dim):
    return lax.dot_general(
        left, right, (((left_dim,), (right_dim,)), ((), ())), preferred_element_type=F32
    )


def head_spread(pair, chunk, head_count):
    rows = lax.broadcasted_iota(jnp.int32, (2 * head_count, CHUNK), 0)
    cols = lax.broadcasted_iota(jnp.int32, (2 * head_count, CHUNK), 1)
    head = jnp.where(rows >= head_count, rows - head_count, rows)
    pick = (head == chunk * CHUNK_HEADS + cols // P_SIZE).astype(F32).astype(BF16)
    return dot(pair, pick, 1, 0)


def two_terms(value, head_count):
    high = value.astype(BF16)
    low = (value - high.astype(F32)).astype(BF16)
    lane = lax.broadcasted_iota(jnp.int32, value.shape, 1)
    return jnp.where(lane < head_count, high.astype(F32), low.astype(F32)).astype(BF16)


def local_kernel(step, rate, dy, x, b, c, dyw, xw, fwd, back, decay, wx, wd):
    chunk = pl.program_id(0)
    tokens, pair_width = step.shape
    head_count = pair_width // 2

    @pl.when(chunk == 0)
    def _():
        rows = lax.broadcasted_iota(jnp.int32, (tokens, tokens), 0)
        cols = lax.broadcasted_iota(jnp.int32, (tokens, tokens), 1)
        lower = (rows >= cols).astype(F32).astype(BF16)
        cum = dot(lower, step[...], 1, 0) * rate[...]
        wd[...] = two_terms(jnp.exp(cum), head_count)
        wx[...] = two_terms(jnp.exp(-cum) * step[...].astype(F32), head_count)

    spread_d = head_spread(wd[...], chunk, head_count)
    last = spread_d[tokens - 1 : tokens, :]
    decay[...] = last
    dyw[...] = (spread_d * dy[...].astype(F32)).astype(BF16)
    xw[...] = (head_spread(wx[...], chunk, head_count) * x[...].astype(F32)).astype(BF16)
    fwd[0] = dot(b[...], xw[...], 0, 0) * last
    back[0] = dot(c[...], dyw[...], 0, 0)


def within_kernel(dyw, xw, b, c, dy, wx, gain, grad_x, grad_b, grad_c):
    group = pl.program_id(0)
    tokens = b.shape[0]
    head_count = wx.shape[1] // 2
    rows = lax.broadcasted_iota(jnp.int32, (tokens, tokens), 0)
    cols = lax.broadcasted_iota(jnp.int32, (tokens, tokens), 1)
    lower = rows >= cols
    scores = jnp.where(lower, dot(c[...], b[...], 1, 1), 0.0).astype(BF16)
    weighted = jnp.where(lower, dot(dyw[...], xw[...], 1, 1), 0.0).astype(BF16)
    grad_b[...] = dot(weighted, c[...], 0, 0)
    grad_c[...] = dot(weighted, b[...], 1, 0)
    per_group = dyw.shape[1] // CHUNK
    for part in range(per_group):
        span = pl.ds(part * CHUNK, CHUNK)
        spread = head_spread(wx[...], group * per_group + part, head_count)
        grad_x[:, span] = spread * dot(scores, dyw[:, span], 0, 0) + gain[:, span] * dy[
            :, span
        ].astype(F32)


def carried_kernel(places, fwd_in, back_in, dyw, xw, b, decay, wx, part_x, part_b, part_c, grad_x, grad_b, grad_c, sum_b, sum_c, *, per_group):
    chunk = pl.program_id(0)
    head_count = wx.shape[1] // 2
    inside = lax.rem(chunk, per_group)

    @pl.when(inside == 0)
    def _():
        sum_b[...] = part_b[...]
        sum_c[...] = part_c[...]

    back = (back_in[0].astype(F32) * decay[...]).astype(BF16)
    spread = head_spread(wx[...], chunk, head_count)
    grad_x[...] = (part_x[...] + spread * dot(b[...], back, 1, 0)).astype(BF16)
    sum_b[...] += dot(xw[...], back, 1, 1)
    sum_c[...] += dot(dyw[...], fwd_in[0], 1, 1)

    @pl.when(inside == per_group - 1)
    def _():
        grad_b[...] = sum_b[...].astype(BF16)
        grad_c[...] = sum_c[...].astype(BF16)


def on_device(grad_out, saved_x, saved_b, saved_c, step_size, decay_rate, skip_gain):
    tokens, row_width = grad_out.shape
    head_count = step_size.shape[1]
    groups = saved_b.shape[1] // N
    chunks = row_width // CHUNK
    per_group = chunks // groups
    group_width = row_width // groups
    ranks = lax.axis_size("ctx")
    rank = lax.axis_index("ctx")
    step_pair = jnp.concatenate([step_size, step_size], axis=1)
    rate_pair = jnp.concatenate([decay_rate, decay_rate]).reshape(1, 2 * head_count)
    gain_row = jnp.repeat(skip_gain, P_SIZE).reshape(1, row_width)

    whole = pl.BlockSpec((tokens, 2 * head_count), lambda c: (0, 0))
    chunk_cols = pl.BlockSpec((tokens, CHUNK), lambda c: (0, c))
    chunk_row = pl.BlockSpec((1, CHUNK), lambda c: (0, c))
    chunk_group = pl.BlockSpec((tokens, N), lambda c: (0, c // per_group))
    chunk_state = pl.BlockSpec((1, N, CHUNK), lambda c: (c, 0, 0))
    dyw, xw, fwd_local, back_local, decay, wx = pl.pallas_call(
        local_kernel,
        grid=(chunks,),
        in_specs=[
            whole,
            pl.BlockSpec((1, 2 * head_count), lambda c: (0, 0)),
            chunk_cols,
            chunk_cols,
            chunk_group,
            chunk_group,
        ],
        out_specs=[chunk_cols, chunk_cols, chunk_state, chunk_state, chunk_row, whole],
        out_shape=[
            jax.ShapeDtypeStruct((tokens, row_width), BF16),
            jax.ShapeDtypeStruct((tokens, row_width), BF16),
            jax.ShapeDtypeStruct((chunks, N, CHUNK), F32),
            jax.ShapeDtypeStruct((chunks, N, CHUNK), F32),
            jax.ShapeDtypeStruct((1, row_width), F32),
            jax.ShapeDtypeStruct((tokens, 2 * head_count), BF16),
        ],
        scratch_shapes=[pltpu.VMEM((tokens, 2 * head_count), BF16)],
        compiler_params=pltpu.CompilerParams(vmem_limit_bytes=28 * MIB),
        cost_estimate=pl.CostEstimate(
            flops=2 * tokens * row_width * (2 * N + 512),
            bytes_accessed=12 * tokens * row_width,
            transcendentals=0,
        ),
        name="local_states",
    )(step_pair, rate_pair, grad_out, saved_x, saved_b, saved_c)

    group_cols = pl.BlockSpec((tokens, group_width), lambda g: (0, g))
    group_own = pl.BlockSpec((tokens, N), lambda g: (0, g))
    part_x, part_b, part_c = pl.pallas_call(
        within_kernel,
        grid=(groups,),
        in_specs=[
            group_cols,
            group_cols,
            group_own,
            group_own,
            group_cols,
            pl.BlockSpec((tokens, 2 * head_count), lambda g: (0, 0)),
            pl.BlockSpec((1, group_width), lambda g: (0, g)),
        ],
        out_specs=[group_cols, group_own, group_own],
        out_shape=[
            jax.ShapeDtypeStruct((tokens, row_width), F32),
            jax.ShapeDtypeStruct((tokens, groups * N), F32),
            jax.ShapeDtypeStruct((tokens, groups * N), F32),
        ],
        compiler_params=pltpu.CompilerParams(vmem_limit_bytes=28 * MIB),
        cost_estimate=pl.CostEstimate(
            flops=4 * tokens * tokens * (row_width + 2 * groups * N),
            bytes_accessed=12 * tokens * row_width,
            transcendentals=0,
        ),
        name="within_device",
    )(dyw, xw, saved_b, saved_c, grad_out, wx, gain_row)

    def at(states, place):
        place = jnp.clip(place, 0, chunks - 1)
        return lax.dynamic_index_in_dim(states, place, 0, False)

    decay_rows = decay.reshape(chunks, 1, CHUNK)
    fwd_now = jnp.zeros((N, CHUNK), BF16)
    back_now = jnp.zeros((N, CHUNK), BF16)
    fwd_got, back_got = [], []
    for turn in range(chunks + ranks - 2):
        fwd_place, back_place = turn - rank, turn - (ranks - 1 - rank)
        fwd_send = (fwd_now.astype(F32) * at(decay_rows, fwd_place) + at(fwd_local, fwd_place)).astype(BF16)
        back_send = (back_now.astype(F32) * at(decay_rows, back_place) + at(back_local, back_place)).astype(BF16)
        pairs = [(r, r + 1) for r in range(ranks - 1) if 0 <= turn - r < chunks]
        fwd_now = lax.ppermute(fwd_send, "ctx", pairs)
        back_now = lax.ppermute(back_send, "ctx", [(ranks - 1 - s, ranks - 1 - d) for s, d in pairs])
        fwd_got.append(fwd_now)
        back_got.append(back_now)
    fwd_all = jnp.stack(fwd_got)
    back_all = jnp.stack(back_got)
    places = jnp.stack([jnp.maximum(rank - 1, 0), jnp.maximum(ranks - 2 - rank, 0)]).astype(jnp.int32)
    turns = chunks + ranks - 2

    def spec(shape, index):
        return pl.BlockSpec(shape, lambda c, places: index(c))

    return pl.pallas_call(
        partial(carried_kernel, per_group=per_group),
        grid_spec=pltpu.PrefetchScalarGridSpec(
            num_scalar_prefetch=1,
            grid=(chunks,),
            in_specs=[
                pl.BlockSpec((1, N, CHUNK), lambda c, places: (jnp.minimum(c + places[0], turns - 1), 0, 0)),
                pl.BlockSpec((1, N, CHUNK), lambda c, places: (jnp.minimum(c + places[1], turns - 1), 0, 0)),
                spec((tokens, CHUNK), lambda c: (0, c)),
                spec((tokens, CHUNK), lambda c: (0, c)),
                spec((tokens, N), lambda c: (0, c // per_group)),
                spec((1, CHUNK), lambda c: (0, c)),
                spec((tokens, 2 * head_count), lambda c: (0, 0)),
                spec((tokens, CHUNK), lambda c: (0, c)),
                spec((tokens, N), lambda c: (0, c // per_group)),
                spec((tokens, N), lambda c: (0, c // per_group)),
            ],
            out_specs=[
                spec((tokens, CHUNK), lambda c: (0, c)),
                spec((tokens, N), lambda c: (0, c // per_group)),
                spec((tokens, N), lambda c: (0, c // per_group)),
            ],
            scratch_shapes=[pltpu.VMEM((tokens, N), F32), pltpu.VMEM((tokens, N), F32)],
        ),
        out_shape=[
            jax.ShapeDtypeStruct((tokens, row_width), BF16),
            jax.ShapeDtypeStruct((tokens, groups * N), BF16),
            jax.ShapeDtypeStruct((tokens, groups * N), BF16),
        ],
        compiler_params=pltpu.CompilerParams(vmem_limit_bytes=28 * MIB),
        cost_estimate=pl.CostEstimate(
            flops=6 * tokens * row_width * N,
            bytes_accessed=14 * tokens * row_width,
            transcendentals=0,
        ),
        name="carried_states",
    )(places, fwd_all, back_all, dyw, xw, saved_b, decay, wx, part_x, part_b, part_c)


def solution(mesh):
    rows_cols = P(("groups", "ctx"), ("dp", "inner"))
    return jax.shard_map(
        on_device,
        mesh=mesh,
        in_specs=(rows_cols,) * 5 + (P(("dp", "inner")),) * 2,
        out_specs=(rows_cols,) * 3,
        check_vma=False,
    )
```

time: 539 us -> 95.9 us (0.18)
  waiting for transfers between devices: 205 us -> 25 us
  blocking collectives: 99.7 us -> 0 us
  local copies, waits for them, and re-layouts: 96.8 us -> 22 us
  matrix products: 54 us -> 0 us
  other arithmetic: 51.4 us -> 7.81 us
  Pallas kernels: 0 us -> 15 us
  between operations: 14 us -> 1.12 us
  starting transfers between devices: 14.5 us -> 24.1 us
    all_to_all x3 -> x0, waiting for transfers between devices: 141 us -> none  [the longest x1 76.4 us: on_device(): lax.all_to_all(grad_out.reshape(tokens, head_count, P_SIZE), 'ctx', split...]
    all_to_all x1 -> x0, blocking collectives: 99.7 us -> none  [on_device(): lax.all_to_all(grad_x, 'ctx', split_axis=0, concat_axis=1, tiled=True)]
    reduce_scatter x2 -> x0, waiting for transfers between devices: 63.1 us -> none  [the longest x1 63.1 us: on_device(): lax.psum_scatter(place_b, 'ctx', scatter_dimension=0, tiled=True)]
    dot_general x34 -> x0, matrix products: 54 us -> none  [product(): return jnp.einsum(form, left, right, preferred_element_type=jnp.float32)]
    ppermute x0 -> x12, waiting for transfers between devices: none -> 25 us  [the longest x6 16.8 us: on_device(): lax.ppermute(back_send, 'ctx', [(ranks - 1 - s, ranks - 1 - d) for s, d i...]
    another operation x10 -> x3, local copies, waits for them, and re-layouts: 24.7 us -> 0.12 us  [the longest x1 0.08 us: on_device(): gain_row = jnp.repeat(skip_gain, P_SIZE).reshape(1, row_width)]
    ppermute x0 -> x12, starting transfers between devices: none -> 24.1 us  [the longest x6 16.7 us: on_device(): fwd_now = lax.ppermute(fwd_send, 'ctx', pairs)]
    add x16 -> x0, other arithmetic: 18.5 us -> none  [advance(): decay_now[..., None, None] * state + local_now]
  transfers between devices with their start and end apart: 7 -> 12, of which waited for: 4 -> 6; matrix products, arithmetic and copies ran while one was open for 18% -> 5% of each run, Pallas kernels for 0% -> 5%
where the time goes in v1:
time: 95.9 us; the launch traced here: 95 us
  waiting for transfers between devices  25 us (26%)
  starting transfers between devices  24.1 us (25%)
  local copies, waits for them, and re-layouts  22 us (23%)
  Pallas kernels  15 us (16%)
  other arithmetic  7.81 us (8%)
  between operations  1.12 us (1%)
    unnamed x69, local copies, waits for them, and re-layouts  21.2 us
    ppermute x6, waiting for transfers between devices, on_device(): lax.ppermute(back_send, 'ctx', [(ranks - 1 - s, ranks - 1 - d) for s, d i...  16.8 us
    ppermute x6, starting transfers between devices, on_device(): fwd_now = lax.ppermute(fwd_send, 'ctx', pairs)  16.7 us
    ppermute x6, waiting for transfers between devices, on_device(): fwd_now = lax.ppermute(fwd_send, 'ctx', pairs)  8.19 us
    ppermute x6, starting transfers between devices, on_device(): lax.ppermute(back_send, 'ctx', [(ranks - 1 - s, ranks - 1 - d) for s, d i...  7.47 us
    pallas_call x1, Pallas kernels, on_device(): pl.pallas_call(partial(carried_kernel, per_group=per_group), grid_spec=pl...  5.66 us
    pallas_call x1, Pallas kernels, on_device(): pl.pallas_call(within_kernel, grid=(groups,), in_specs=[group_cols, group...  5.06 us
    pallas_call x1, Pallas kernels, on_device(): pl.pallas_call(local_kernel, grid=(chunks,), in_specs=[whole, pl.BlockSpe...  4.27 us
  transfers between devices with their start and end apart: 12, of which 6 were waited for; matrix products, arithmetic and copies ran while one was open for 5% of the time, Pallas kernels for 5%

profile of v1, /device:TPU:0, one launch (start us, length us, event | category | flops | bytes accessed | tf_op | source)
XLA Modules:
  0.0 95.0 jit_solution(10232610772823871646)
XLA Ops:
  3.5 1.6 %copy-done.15 = bf16[512,2048]{1,0:T(8,128)(2,1)S(1)} copy-done((bf16[512,2048]{1,0:T(8,128)(2,1)S(1)}, bf16[512,2048]{1,0:T(8,128)(2,1)}, u32[]{:S(2)}) %copy-start.15) | copy-done | bytes 2097176
  5.1 1.6 %copy-done.16 = bf16[512,2048]{1,0:T(8,128)(2,1)S(1)} copy-done((bf16[512,2048]{1,0:T(8,128)(2,1)S(1)}, bf16[512,2048]{1,0:T(8,128)(2,1)}, u32[]{:S(2)}) %copy-start.16) | copy-done | bytes 2097176
  7.7 4.3 %local_states.1 = (bf16[512,2048]{1,0:T(8,128)(2,1)S(1)}, bf16[512,2048]{1,0:T(8,128)(2,1)S(1)}, f32[4,256,512]{2,1,0:T(8,128)S(1)}, f32[4,256,512]{2,1,0:T(8,12...) custom-call(bf16[512,64]{1,0:T(8,128)(2,1)S(1)} %pad_maximum_fusion.step, ...), custom_call_target="tpu_custom_call" | custom-call | flops 2147483648 | bytes 12582912 | tf_op jit(solution)/shard_map/local_states/pallas_call | solution.py:123
  13.3 1.4 %copy-done.4 = bf16[512,2048]{1,0:T(8,128)(2,1)} copy-done((bf16[512,2048]{1,0:T(8,128)(2,1)}, bf16[512,2048]{1,0:T(8,128)(2,1)S(1)}, u32[]{:S(2)}) %copy-start.4) | copy-done | bytes 2097176
  14.7 1.4 %copy-done.7 = bf16[512,2048]{1,0:T(8,128)(2,1)} copy-done((bf16[512,2048]{1,0:T(8,128)(2,1)}, bf16[512,2048]{1,0:T(8,128)(2,1)S(1)}, u32[]{:S(2)}) %copy-start.7) | copy-done | bytes 2097176
  18.0 1.8 %fusion.11 = bf16[256,512]{1,0:T(8,128)(2,1)} fusion(f32[4,256,512]{2,1,0:T(8,128)} %copy-done, s32[]{:T(128)S(6)} %min.49, f32[512]{0:T(512)S(1)} %bitcast.99), kind=kLoop, calls=%fused_computation.23 | loop fusion | flops 262144 | bytes 788484 | tf_op jit(solution)/shard_map/convert_element_type | solution.py:192
  19.8 4.9 %collective-permute-start = (bf16[256,512]{1,0:T(8,128)(2,1)}, bf16[256,512]{1,0:T(8,128)(2,1)S(1)}, u32[]{:S(2)}, u32[]{:S(2)}) collective-permute-start(bf16[256,512]{1,0:T(8,128)(2,1)} %fusion.11), channel_id=1, source_target_pairs={{0,4},{1,5},{2,6},{3,7},{16,20},{17,21},{18,22},{19,23}} | collective-permute-start | bytes 786440 | tf_op jit(solution)/shard_map/ppermute | solution.py:195
  25.5 1.4 %collective-permute-start.6 = (bf16[256,512]{1,0:T(8,128)(2,1)}, bf16[256,512]{1,0:T(8,128)(2,1)}, u32[]{:S(2)}, u32[]{:S(2)}) collective-permute-start(bf16[256,512]{1,0:T(8,128)(2,1)} %fusion.5), channel_id=1, source_target_pairs={{12,8},{13,9},{14,10},{15,11},{28,24},{29,25},{30,26},{31,27}} | collective-permute-start | bytes 786440 | tf_op jit(solution)/shard_map/ppermute | solution.py:196
  27.0 1.6 %copy-done.5 = bf16[512,2048]{1,0:T(8,128)(2,1)S(1)} copy-done((bf16[512,2048]{1,0:T(8,128)(2,1)S(1)}, bf16[512,2048]{1,0:T(8,128)(2,1)}, u32[]{:S(2)}) %copy-start.5) | copy-done | bytes 2097176
  28.6 1.6 %copy-done.8 = bf16[512,2048]{1,0:T(8,128)(2,1)S(1)} copy-done((bf16[512,2048]{1,0:T(8,128)(2,1)S(1)}, bf16[512,2048]{1,0:T(8,128)(2,1)}, u32[]{:S(2)}) %copy-start.8) | copy-done | bytes 2097176
  31.2 1.6 %copy-done.17 = bf16[512,2048]{1,0:T(8,128)(2,1)S(1)} copy-done((bf16[512,2048]{1,0:T(8,128)(2,1)S(1)}, bf16[512,2048]{1,0:T(8,128)(2,1)}, u32[]{:S(2)}) %copy-start.17) | copy-done | bytes 2097176
  33.8 5.1 %within_device.1 = (f32[512,2048]{1,0:T(8,128)S(1)}, f32[512,512]{1,0:T(8,128)S(1)}, f32[512,512]{1,0:T(8,128)S(1)}) custom-call(bf16[512,2048]{1,0:T(8,128)(2,1)S(1)} %copy-done.5, bf16[512,2048]{1,0:T(8,128)(2,1)S(1)} %copy-done.8, bf16[512,512]{1,0:T(8,128)(2,1)S(1)} %copy-done.13, bf16[512,512]{1,0:T(8,128)(2,1)S(1)} %copy-done.19, ...), custom_call_target="tpu_custom_call" | custom-call | flops 3221225472 | bytes 12582912 | tf_op jit(solution)/shard_map/within_device/pallas_call | solution.py:155
  38.9 2.0 %copy-done.2 = f32[512,2048]{1,0:T(8,128)} copy-done((f32[512,2048]{1,0:T(8,128)}, f32[512,2048]{1,0:T(8,128)S(1)}, u32[]{:S(2)}) %copy-start.2) | copy-done | bytes 4194328
  47.3 2.8 %collective-permute-done.1 = bf16[256,512]{1,0:T(8,128)(2,1)S(1)} collective-permute-done((bf16[256,512]{1,0:T(8,128)(2,1)S(1)}, bf16[256,512]{1,0:T(8,128)(2,1)S(1)}, u32[]{:S(2)}, u32[]{:S(2)}) %collective-permute-start.1) | collective-permute-done | bytes 262176 | tf_op jit(solution)/shard_map/ppermute | solution.py:195
  50.2 4.4 %collective-permute-start.2 = (bf16[256,512]{1,0:T(8,128)(2,1)S(1)}, bf16[256,512]{1,0:T(8,128)(2,1)S(1)}, u32[]{:S(2)}, u32[]{:S(2)}) collective-permute-start(bf16[256,512]{1,0:T(8,128)(2,1)S(1)} %fusion.9), channel_id=1, source_target_pairs={{0,4},{4,8},{8,12},{1,5},{5,9},{9,13},{2,6},{6,10},{10,14},{3,7},{... | collective-permute-start | bytes 786440 | tf_op jit(solution)/shard_map/ppermute | solution.py:195
  56.0 3.2 %collective-permute-done.2 = bf16[256,512]{1,0:T(8,128)(2,1)S(1)} collective-permute-done((bf16[256,512]{1,0:T(8,128)(2,1)S(1)}, bf16[256,512]{1,0:T(8,128)(2,1)S(1)}, u32[]{:S(2)}, u32[]{:S(2)}) %collective-permute-start.2) | collective-permute-done | bytes 262176 | tf_op jit(solution)/shard_map/ppermute | solution.py:195
  59.3 4.5 %collective-permute-start.3 = (bf16[256,512]{1,0:T(8,128)(2,1)S(1)}, bf16[256,512]{1,0:T(8,128)(2,1)S(1)}, u32[]{:S(2)}, u32[]{:S(2)}) collective-permute-start(bf16[256,512]{1,0:T(8,128)(2,1)S(1)} %fusion.8), channel_id=1, source_target_pairs={{0,4},{4,8},{8,12},{1,5},{5,9},{9,13},{2,6},{6,10},{10,14},{3,7},{... | collective-permute-start | bytes 786440 | tf_op jit(solution)/shard_map/ppermute | solution.py:195
  64.0 1.4 %collective-permute-start.9 = (bf16[256,512]{1,0:T(8,128)(2,1)S(1)}, bf16[256,512]{1,0:T(8,128)(2,1)S(1)}, u32[]{:S(2)}, u32[]{:S(2)}) collective-permute-start(bf16[256,512]{1,0:T(8,128)(2,1)S(1)} %fusion.2), channel_id=1, source_target_pairs={{12,8},{8,4},{4,0},{13,9},{9,5},{5,1},{14,10},{10,6},{6,2},{15,11}... | collective-permute-start | bytes 786440 | tf_op jit(solution)/shard_map/ppermute | solution.py:196
  65.5 2.2 %collective-permute-done.3 = bf16[256,512]{1,0:T(8,128)(2,1)S(1)} collective-permute-done((bf16[256,512]{1,0:T(8,128)(2,1)S(1)}, bf16[256,512]{1,0:T(8,128)(2,1)S(1)}, u32[]{:S(2)}, u32[]{:S(2)}) %collective-permute-start.3) | collective-permute-done | bytes 262176 | tf_op jit(solution)/shard_map/ppermute | solution.py:195
  68.5 3.9 %collective-permute-done.9 = bf16[256,512]{1,0:T(8,128)(2,1)S(1)} collective-permute-done((bf16[256,512]{1,0:T(8,128)(2,1)S(1)}, bf16[256,512]{1,0:T(8,128)(2,1)S(1)}, u32[]{:S(2)}, u32[]{:S(2)}) %collective-permute-start.9) | collective-permute-done | bytes 262176 | tf_op jit(solution)/shard_map/ppermute | solution.py:196
  72.5 1.4 %collective-permute-start.10 = (bf16[256,512]{1,0:T(8,128)(2,1)S(1)}, bf16[256,512]{1,0:T(8,128)(2,1)S(1)}, u32[]{:S(2)}, u32[]{:S(2)}) collective-permute-start(bf16[256,512]{1,0:T(8,128)(2,1)S(1)} %fusion.1), channel_id=1, source_target_pairs={{8,4},{4,0},{9,5},{5,1},{10,6},{6,2},{11,7},{7,3},{24,20},{20,16},... | collective-permute-start | bytes 786440 | tf_op jit(solution)/shard_map/ppermute | solution.py:196
  74.9 6.0 %collective-permute-done.10 = bf16[256,512]{1,0:T(8,128)(2,1)S(1)} collective-permute-done((bf16[256,512]{1,0:T(8,128)(2,1)S(1)}, bf16[256,512]{1,0:T(8,128)(2,1)S(1)}, u32[]{:S(2)}, u32[]{:S(2)}) %collective-permute-start.10) | collective-permute-done | bytes 262176 | tf_op jit(solution)/shard_map/ppermute | solution.py:196
  82.3 6.9 %collective-permute-done.11 = bf16[256,512]{1,0:T(8,128)(2,1)S(1)} collective-permute-done((bf16[256,512]{1,0:T(8,128)(2,1)S(1)}, bf16[256,512]{1,0:T(8,128)(2,1)S(1)}, u32[]{:S(2)}, u32[]{:S(2)}) %collective-permute-start.11) | collective-permute-done | bytes 262176 | tf_op jit(solution)/shard_map/ppermute | solution.py:196
  89.3 5.7 %carried_states.1 = (bf16[512,2048]{1,0:T(8,128)(2,1)}, bf16[512,512]{1,0:T(8,128)(2,1)}, bf16[512,512]{1,0:T(8,128)(2,1)}) custom-call(s32[2]{0:T(128)S(1)} %pad_add_fusion.places, bf16[6,256,512]{2,1,0:T(8,128)(2,1)S(1)} %bitcast_dynamic-update-slice_fusion.6.fwd_in, bf16[6,256,512]{2,1,0:T(8,128)(2,1)S(1)} %bitcast_dynamic-update-slice_fusion.back_in, ...), custom_call_target="tpu_custom_call" | custom-call | flops 1610612736 | bytes 14680064 | tf_op jit(solution)/shard_map/carried_states/pallas_call | solution.py:207
  (95 shorter events, 21.3 us)
Async XLA Ops:
  16.1 10.7 %copy-start.28 = (f32[32]{0:T(128)S(1)}, f32[32]{0:T(128)}, u32[]{:S(2)}) copy-start(f32[32]{0:T(128)} %param.13) | copy-start | bytes 388
  19.8 22.2 %collective-permute-start = (bf16[256,512]{1,0:T(8,128)(2,1)}, bf16[256,512]{1,0:T(8,128)(2,1)S(1)}, u32[]{:S(2)}, u32[]{:S(2)}) collective-permute-start(bf16[256,512]{1,0:T(8,128)(2,1)} %fusion.11), channel_id=1, source_target_pairs={{0,4},{1,5},{2,6},{3,7},{16,20},{17,21},{18,22},{19,23}} | collective-permute-start | bytes 786440 | tf_op jit(solution)/shard_map/ppermute | solution.py:195
  25.5 19.1 %collective-permute-start.6 = (bf16[256,512]{1,0:T(8,128)(2,1)}, bf16[256,512]{1,0:T(8,128)(2,1)}, u32[]{:S(2)}, u32[]{:S(2)}) collective-permute-start(bf16[256,512]{1,0:T(8,128)(2,1)} %fusion.5), channel_id=1, source_target_pairs={{12,8},{13,9},{14,10},{15,11},{28,24},{29,25},{30,26},{31,27}} | collective-permute-start | bytes 786440 | tf_op jit(solution)/shard_map/ppermute | solution.py:196
  43.2 6.8 %collective-permute-start.1 = (bf16[256,512]{1,0:T(8,128)(2,1)S(1)}, bf16[256,512]{1,0:T(8,128)(2,1)S(1)}, u32[]{:S(2)}, u32[]{:S(2)}) collective-permute-start(bf16[256,512]{1,0:T(8,128)(2,1)S(1)} %fusion.10), channel_id=1, source_target_pairs={{0,4},{4,8},{1,5},{5,9},{2,6},{6,10},{3,7},{7,11},{16,20},{20,24},... | collective-permute-start | bytes 786440 | tf_op jit(solution)/shard_map/ppermute | solution.py:195
  44.6 10.0 %copy-start.26 = (f32[1,1,512]{2,0,1:T(1,128)S(1)}, f32[1,1,512]{2,0,1:T(1,128)}, u32[]{:S(2)}) copy-start(f32[1,1,512]{2,0,1:T(1,128)} %get-tuple-element.24) | copy-start | bytes 6148
  45.6 9.0 %collective-permute-start.7 = (bf16[256,512]{1,0:T(8,128)(2,1)S(1)}, bf16[256,512]{1,0:T(8,128)(2,1)S(1)}, u32[]{:S(2)}, u32[]{:S(2)}) collective-permute-start(bf16[256,512]{1,0:T(8,128)(2,1)S(1)} %fusion.4), channel_id=1, source_target_pairs={{12,8},{8,4},{13,9},{9,5},{14,10},{10,6},{15,11},{11,7},{28,24},{2... | collective-permute-start | bytes 786440 | tf_op jit(solution)/shard_map/ppermute | solution.py:196
  50.1 9.1 %copy-start.25 = (f32[1,1,512]{2,0,1:T(1,128)S(1)}, f32[1,1,512]{2,0,1:T(1,128)}, u32[]{:S(2)}) copy-start(f32[1,1,512]{2,0,1:T(1,128)} %get-tuple-element.29) | copy-start | bytes 6148
  50.2 9.1 %collective-permute-start.2 = (bf16[256,512]{1,0:T(8,128)(2,1)S(1)}, bf16[256,512]{1,0:T(8,128)(2,1)S(1)}, u32[]{:S(2)}, u32[]{:S(2)}) collective-permute-start(bf16[256,512]{1,0:T(8,128)(2,1)S(1)} %fusion.9), channel_id=1, source_target_pairs={{0,4},{4,8},{8,12},{1,5},{5,9},{9,13},{2,6},{6,10},{10,14},{3,7},{... | collective-permute-start | bytes 786440 | tf_op jit(solution)/shard_map/ppermute | solution.py:195
  54.6 9.3 %copy-start.24 = (f32[1,1,512]{2,0,1:T(1,128)S(1)}, f32[1,1,512]{2,0,1:T(1,128)}, u32[]{:S(2)}) copy-start(f32[1,1,512]{2,0,1:T(1,128)} %get-tuple-element.23) | copy-start | bytes 6148
  54.7 9.2 %collective-permute-start.8 = (bf16[256,512]{1,0:T(8,128)(2,1)S(1)}, bf16[256,512]{1,0:T(8,128)(2,1)S(1)}, u32[]{:S(2)}, u32[]{:S(2)}) collective-permute-start(bf16[256,512]{1,0:T(8,128)(2,1)S(1)} %fusion.3), channel_id=1, source_target_pairs={{12,8},{8,4},{4,0},{13,9},{9,5},{5,1},{14,10},{10,6},{6,2},{15,11}... | collective-permute-start | bytes 786440 | tf_op jit(solution)/shard_map/ppermute | solution.py:196
  59.2 8.5 %copy-start.23 = (f32[1,1,512]{2,0,1:T(1,128)S(1)}, f32[1,1,512]{2,0,1:T(1,128)}, u32[]{:S(2)}) copy-start(f32[1,1,512]{2,0,1:T(1,128)} %get-tuple-element.28) | copy-start | bytes 6148
  59.2 30.1 %copy-start.14 = (bf16[512,512]{1,0:T(8,128)(2,1)S(1)}, bf16[512,512]{1,0:T(8,128)(2,1)}, u32[]{:S(2)}) copy-start(bf16[512,512]{1,0:T(8,128)(2,1)} %b.5) | copy-start | bytes 1572868
  59.3 8.4 %collective-permute-start.3 = (bf16[256,512]{1,0:T(8,128)(2,1)S(1)}, bf16[256,512]{1,0:T(8,128)(2,1)S(1)}, u32[]{:S(2)}, u32[]{:S(2)}) collective-permute-start(bf16[256,512]{1,0:T(8,128)(2,1)S(1)} %fusion.8), channel_id=1, source_target_pairs={{0,4},{4,8},{8,12},{1,5},{5,9},{9,13},{2,6},{6,10},{10,14},{3,7},{... | collective-permute-start | bytes 786440 | tf_op jit(solution)/shard_map/ppermute | solution.py:195
  63.9 8.5 %copy-start.22 = (f32[1,1,512]{2,0,1:T(1,128)S(1)}, f32[1,1,512]{2,0,1:T(1,128)}, u32[]{:S(2)}) copy-start(f32[1,1,512]{2,0,1:T(1,128)} %get-tuple-element.22) | copy-start | bytes 6148
  63.9 25.4 %copy-start.11 = (f32[512,512]{1,0:T(8,128)S(1)}, f32[512,512]{1,0:T(8,128)}, u32[]{:S(2)}) copy-start(f32[512,512]{1,0:T(8,128)} %copy-done.10) | copy-start | bytes 3145732
  64.0 8.4 %collective-permute-start.9 = (bf16[256,512]{1,0:T(8,128)(2,1)S(1)}, bf16[256,512]{1,0:T(8,128)(2,1)S(1)}, u32[]{:S(2)}, u32[]{:S(2)}) collective-permute-start(bf16[256,512]{1,0:T(8,128)(2,1)S(1)} %fusion.2), channel_id=1, source_target_pairs={{12,8},{8,4},{4,0},{13,9},{9,5},{5,1},{14,10},{10,6},{6,2},{15,11}... | collective-permute-start | bytes 786440 | tf_op jit(solution)/shard_map/ppermute | solution.py:196
  65.4 23.9 %copy-start.9 = (bf16[512,2048]{1,0:T(8,128)(2,1)S(1)}, bf16[512,2048]{1,0:T(8,128)(2,1)}, u32[]{:S(2)}) copy-start(bf16[512,2048]{1,0:T(8,128)(2,1)} %copy-done.7) | copy-start | bytes 6291460
  67.8 6.2 %collective-permute-start.4 = (bf16[256,512]{1,0:T(8,128)(2,1)S(1)}, bf16[256,512]{1,0:T(8,128)(2,1)S(1)}, u32[]{:S(2)}, u32[]{:S(2)}) collective-permute-start(bf16[256,512]{1,0:T(8,128)(2,1)S(1)} %fusion.7), channel_id=1, source_target_pairs={{4,8},{8,12},{5,9},{9,13},{6,10},{10,14},{7,11},{11,15},{20,24},{2... | collective-permute-start | bytes 786440 | tf_op jit(solution)/shard_map/ppermute | solution.py:195
  72.4 8.5 %copy-start.20 = (f32[1,1,512]{2,0,1:T(1,128)S(1)}, f32[1,1,512]{2,0,1:T(1,128)}, u32[]{:S(2)}) copy-start(f32[1,1,512]{2,0,1:T(1,128)} %get-tuple-element.21) | copy-start | bytes 6148
  72.4 16.9 %copy-start.6 = (bf16[512,2048]{1,0:T(8,128)(2,1)S(1)}, bf16[512,2048]{1,0:T(8,128)(2,1)}, u32[]{:S(2)}) copy-start(bf16[512,2048]{1,0:T(8,128)(2,1)} %copy-done.4) | copy-start | bytes 6291460
  72.5 8.4 %collective-permute-start.10 = (bf16[256,512]{1,0:T(8,128)(2,1)S(1)}, bf16[256,512]{1,0:T(8,128)(2,1)S(1)}, u32[]{:S(2)}, u32[]{:S(2)}) collective-permute-start(bf16[256,512]{1,0:T(8,128)(2,1)S(1)} %fusion.1), channel_id=1, source_target_pairs={{8,4},{4,0},{9,5},{5,1},{10,6},{6,2},{11,7},{7,3},{24,20},{20,16},... | collective-permute-start | bytes 786440 | tf_op jit(solution)/shard_map/ppermute | solution.py:196
  74.0 15.3 %copy-start.3 = (f32[512,2048]{1,0:T(8,128)S(1)}, f32[512,2048]{1,0:T(8,128)}, u32[]{:S(2)}) copy-start(f32[512,2048]{1,0:T(8,128)} %copy-done.2) | copy-start | bytes 12582916
  74.1 15.2 %collective-permute-start.5 = (bf16[256,512]{1,0:T(8,128)(2,1)S(1)}, bf16[256,512]{1,0:T(8,128)(2,1)S(1)}, u32[]{:S(2)}, u32[]{:S(2)}) collective-permute-start(bf16[256,512]{1,0:T(8,128)(2,1)S(1)} %fusion.6), channel_id=1, source_target_pairs={{8,12},{9,13},{10,14},{11,15},{24,28},{25,29},{26,30},{27,31}} | collective-permute-start | bytes 786440 | tf_op jit(solution)/shard_map/ppermute | solution.py:195
  81.0 8.3 %collective-permute-start.11 = (bf16[256,512]{1,0:T(8,128)(2,1)S(1)}, bf16[256,512]{1,0:T(8,128)(2,1)S(1)}, u32[]{:S(2)}, u32[]{:S(2)}) collective-permute-start(bf16[256,512]{1,0:T(8,128)(2,1)S(1)} %fusion), channel_id=1, source_target_pairs={{4,0},{5,1},{6,2},{7,3},{20,16},{21,17},{22,18},{23,19}} | collective-permute-start | bytes 786440 | tf_op jit(solution)/shard_map/ppermute | solution.py:196
  (17 other events, 41.7 us)

commit v2 on v0

v2 whole, which is shorter than its diff:
```python
from functools import partial

import jax
import jax.numpy as jnp
from jax import lax
from jax.experimental import pallas as pl
from jax.experimental.pallas import tpu as pltpu
from jax.sharding import PartitionSpec as P

P_SIZE = 64
N = 256
CHUNK = 512
CHUNK_HEADS = CHUNK // P_SIZE
F32 = jnp.float32
BF16 = jnp.bfloat16
PARAMS = pltpu.CompilerParams(vmem_limit_bytes=16 * 1024 * 1024)
RELAY_PARAMS = pltpu.CompilerParams(vmem_limit_bytes=4 * 1024 * 1024)
ANYWHERE = pl.BlockSpec(memory_space=pl.ANY)
IN_VMEM = pl.BlockSpec(memory_space=pltpu.VMEM)


def dot(left, right, left_dim, right_dim):
    return lax.dot_general(
        left, right, (((left_dim,), (right_dim,)), ((), ())), preferred_element_type=F32
    )


def terms(value, count):
    parts = []
    for _ in range(count):
        part = value.astype(BF16)
        parts.append(part)
        value = value - part.astype(F32)
    return parts


def head_spread(parts, chunk):
    head_count = parts[0].shape[0]
    rows = lax.broadcasted_iota(jnp.int32, (head_count, CHUNK), 0)
    cols = lax.broadcasted_iota(jnp.int32, (head_count, CHUNK), 1)
    pick = (rows == chunk * CHUNK_HEADS + cols // P_SIZE).astype(F32).astype(BF16)
    total = dot(parts[0], pick, 0, 0)
    for part in parts[1:]:
        total += dot(part, pick, 0, 0)
    return total


def lower_mask(tokens):
    rows = lax.broadcasted_iota(jnp.int32, (tokens, tokens), 0)
    cols = lax.broadcasted_iota(jnp.int32, (tokens, tokens), 1)
    return rows >= cols


def columns(row):
    size = row.shape[1]
    rows = lax.broadcasted_iota(jnp.int32, (size, size), 0)
    cols = lax.broadcasted_iota(jnp.int32, (size, size), 1)
    return jnp.sum(jnp.where(rows == cols, row, 0.0), axis=1, keepdims=True)


def local_kernel(*refs, first, last, per_group):
    if first == 0:
        step, rate, dy, x, b, c = refs[:6]
        dyw, xw, fwd, back, decay, wd, wx, fwd_send, back_send = refs[6:15]
    else:
        wd, wx, dy, x, b, c = refs[:6]
        dyw, xw, fwd, back, decay = refs[6:11]
    dy_in, x_in, b_in, c_in, sems = refs[-5:]
    tokens = dy_in.shape[0]
    low_group = first // per_group
    copies = []
    for place, (source, target, low) in enumerate(
        (
            (dy, dy_in, first * CHUNK),
            (c, c_in, low_group * N),
            (x, x_in, first * CHUNK),
            (b, b_in, low_group * N),
        )
    ):
        copies.append(
            pltpu.make_async_copy(
                source.at[:, pl.ds(low, target.shape[1])], target, sems.at[place]
            )
        )
        copies[-1].start()
    if first == 0:
        rows = lax.broadcasted_iota(jnp.int32, (tokens, tokens), 0)
        cols = lax.broadcasted_iota(jnp.int32, (tokens, tokens), 1)
        upper = (rows <= cols).astype(F32).astype(BF16)
        cum = dot(step[...], upper, 1, 0) * columns(rate[...])
        wd[0], wd[1] = terms(jnp.exp(cum), 2)
        wx[0], wx[1] = terms(jnp.exp(-cum) * step[...].astype(F32), 2)
    for place in range(4):
        copies[place].wait()
    for chunk in range(first, last):
        span = pl.ds((chunk - first) * CHUNK, CHUNK)
        group = pl.ds((chunk // per_group - low_group) * N, N)
        spread = head_spread((wd[0], wd[1]), chunk)
        end = spread[tokens - 1 : tokens, :]
        decay[chunk - first] = end
        dyw[:, span] = (spread * dy_in[:, span].astype(F32)).astype(BF16)
        spread = head_spread((wx[0], wx[1]), chunk)
        xw[:, span] = (spread * x_in[:, span].astype(F32)).astype(BF16)
        back[chunk - first] = dot(c_in[:, group], dyw[:, span], 0, 0)
        fwd[chunk - first] = dot(b_in[:, group], xw[:, span], 0, 0) * end
    if first == 0:
        fwd_send[...] = fwd[0].astype(BF16)
        back_send[...] = back[0].astype(BF16)


def piece(refs, chunk):
    if chunk == 0:
        return refs[0][...]
    return refs[1][:, pl.ds((chunk - 1) * CHUNK, CHUNK)]


def within_kernel(*refs, group, per_group):
    dyw, xw = refs[0:2], refs[2:4]
    b, c, dy, wx, gain, grad_x, grad_b, grad_c = refs[4:]
    lower = lower_mask(b.shape[0])
    own = pl.ds(group * N, N)
    chunks = range(group * per_group, (group + 1) * per_group)
    scores = jnp.where(lower, dot(c[:, own], b[:, own], 1, 1), 0.0).astype(BF16)
    weighted = sum(dot(piece(dyw, chunk), piece(xw, chunk), 1, 1) for chunk in chunks)
    weighted = jnp.where(lower, weighted, 0.0).astype(BF16)
    grad_b[...] = dot(weighted, c[:, own], 0, 0)
    grad_c[...] = dot(weighted, b[:, own], 1, 0)
    gains = terms(jnp.broadcast_to(columns(gain[...]), (gain.shape[1], 128)), 3)
    for part, chunk in enumerate(chunks):
        spread = head_spread((wx[0], wx[1]), chunk)
        rows = dy[:, pl.ds(chunk * CHUNK, CHUNK)].astype(F32)
        skip = head_spread(gains, chunk)[0:1, :] * rows
        grad_x[:, pl.ds(part * CHUNK, CHUNK)] = (
            spread * dot(scores, piece(dyw, chunk), 0, 0) + skip
        )


def ahead(step, ranks):
    rank = lax.axis_index("ctx")
    return rank if step > 0 else ranks - 1 - rank


def relay_kernel(got, states_0, states, decay_0, decay, out, *, turn, step, ranks):
    place = turn - ahead(step, ranks)
    later = jnp.clip(place - 1, 0, states.shape[0] - 1)
    state = jnp.where(place <= 0, states_0[0], states[later])
    shrink = jnp.where(place <= 0, decay_0[0], decay[later])
    out[...] = (got[...].astype(F32) * shrink + state).astype(BF16)


def chosen(candidates, step, ranks):
    source = ahead(step, ranks) - 1
    value = candidates[0][...]
    for place in range(1, len(candidates)):
        value = jnp.where(source == place, candidates[place][...], value)
    return value


def carried_kernel(*refs, chunk, per_group, last, ranks):
    fwd_in = chosen(refs[: ranks - 1], 1, ranks)
    back_in = chosen(refs[ranks - 1 : 2 * ranks - 2], -1, ranks)
    refs = refs[2 * ranks - 2 :]
    dyw, xw, b, decay, wx, part_x, part_b, part_c = refs[:8]
    group, inside = chunk // per_group, chunk % per_group
    grad_x, grad_b, grad_c = refs[-7 if last else -5 :][:3]
    x_out = refs[-4] if last else refs[-2]
    sems = refs[-1]
    place = max(chunk - 1, 0)
    span = pl.ds(place * CHUNK, CHUNK)
    own = pl.ds(group * N, N)
    copies = []

    def send(source, target, place):
        copies.append(pltpu.make_async_copy(source, target, sems.at[place]))
        copies[-1].start()

    back = (back_in.astype(F32) * decay[place]).astype(BF16)
    spread = head_spread((wx[0], wx[1]), chunk)
    carried = spread * dot(b[:, own], back, 1, 0)
    x_out[...] = (part_x[:, pl.ds(inside * CHUNK, CHUNK)] + carried).astype(BF16)
    send(x_out, grad_x.at[:, pl.ds(chunk * CHUNK, CHUNK)], 0)
    total_b = part_b[...] + dot(xw[:, span], back, 1, 1)
    if last:
        b_out, c_out = refs[-3:-1]
        b_out[...] = total_b.astype(BF16)
        send(b_out, grad_b.at[:, own], 1)
    else:
        grad_b[...] = total_b
    total_c = part_c[...] + dot(dyw[:, span], fwd_in, 1, 1)
    if last:
        c_out[...] = total_c.astype(BF16)
        send(c_out, grad_c.at[:, own], 2)
    else:
        grad_c[...] = total_c
    for copy in copies:
        copy.wait()


def cost(flops, bytes_accessed):
    return pl.CostEstimate(flops=flops, bytes_accessed=bytes_accessed, transcendentals=0)


def on_device(grad_out, saved_x, saved_b, saved_c, step_size, decay_rate, skip_gain):
    tokens, row_width = grad_out.shape
    head_count = step_size.shape[1]
    groups = saved_b.shape[1] // N
    chunks = row_width // CHUNK
    per_group = chunks // groups
    group_width = row_width // groups
    ranks = lax.axis_size("ctx")
    rate_row = decay_rate.reshape(1, head_count)
    gain_row = skip_gain.reshape(1, head_count)
    stay = partial(pltpu.with_memory_space_constraint, memory_space=pltpu.HBM)
    sources = [stay(array) for array in (grad_out, saved_x, saved_b, saved_c)]

    weight_shapes = [pltpu.VMEM((2, head_count, tokens), BF16)] * 2
    send_shapes = [jax.ShapeDtypeStruct((N, CHUNK), BF16)] * 2

    def local_states(first, last, inputs, extra_shapes):
        wide = (last - first) * CHUNK
        out_shape = [
            pltpu.VMEM((tokens, wide), BF16),
            pltpu.VMEM((tokens, wide), BF16),
            pltpu.VMEM((last - first, N, CHUNK), F32),
            pltpu.VMEM((last - first, N, CHUNK), F32),
            pltpu.VMEM((last - first, 1, CHUNK), F32),
        ] + extra_shapes
        tall = ((last - 1) // per_group - first // per_group + 1) * N
        return pl.pallas_call(
            partial(local_kernel, first=first, last=last, per_group=per_group),
            in_specs=[IN_VMEM] * 2 + [ANYWHERE] * 4,
            out_specs=[IN_VMEM] * len(out_shape),
            out_shape=out_shape,
            scratch_shapes=[
                pltpu.VMEM((tokens, wide), BF16),
                pltpu.VMEM((tokens, wide), BF16),
                pltpu.VMEM((tokens, tall), BF16),
                pltpu.VMEM((tokens, tall), BF16),
                pltpu.SemaphoreType.DMA((4,)),
            ],
            compiler_params=PARAMS,
            cost_estimate=cost(4 * tokens * wide * (N + 512), 6 * tokens * wide),
            name=f"states_{first}",
        )(*inputs)

    *head, wd, wx, fwd_send, back_send = local_states(
        0, 1, [step_size.T, rate_row] + sources, weight_shapes + send_shapes
    )
    tail = local_states(1, chunks, [wd, wx] + sources, [])

    def within(group, wx):
        return pl.pallas_call(
            partial(within_kernel, group=group, per_group=per_group),
            in_specs=[IN_VMEM] * 9,
            out_specs=[IN_VMEM] * 3,
            out_shape=[
                pltpu.VMEM((tokens, group_width), F32),
                pltpu.VMEM((tokens, N), F32),
                pltpu.VMEM((tokens, N), F32),
            ],
            compiler_params=PARAMS,
            cost_estimate=cost(
                4 * tokens * tokens * (group_width + 2 * N), 10 * tokens * group_width
            ),
            name=f"within_{group}",
        )(head[0], tail[0], head[1], tail[1], saved_b, saved_c, grad_out, wx, gain_row)

    def relay(turn, step, got):
        kind = 2 if step > 0 else 3
        return pl.pallas_call(
            partial(relay_kernel, turn=turn, step=step, ranks=ranks),
            in_specs=[IN_VMEM] * 5,
            out_specs=IN_VMEM,
            out_shape=pltpu.VMEM((N, CHUNK), BF16),
            compiler_params=RELAY_PARAMS,
            cost_estimate=cost(4 * N * CHUNK, 8 * N * CHUNK),
            name=f"relay_{turn}_{kind}",
        )(got, head[kind], tail[kind], head[4], tail[4])

    def carried(chunk, fwd_in, back_in, part_x, part_b, part_c, grads):
        own = head if chunk == 0 else tail
        last = chunk % per_group == per_group - 1
        out_shape = [jax.ShapeDtypeStruct((tokens, row_width), BF16)]
        out_specs = [ANYWHERE]
        scratch = [pltpu.VMEM((tokens, CHUNK), BF16)]
        if last:
            out_shape += [jax.ShapeDtypeStruct((tokens, groups * N), BF16)] * 2
            out_specs += [ANYWHERE] * 2
            scratch += [pltpu.VMEM((tokens, N), BF16)] * 2
        else:
            out_shape += [pltpu.VMEM((tokens, N), F32)] * 2
            out_specs += [IN_VMEM] * 2
        inputs = [*fwd_in, *back_in, own[0], own[1], saved_b, own[4], wx, part_x, part_b, part_c]
        aliases = {}
        if grads[0] is not None:
            aliases[len(inputs)] = 0
            inputs.append(grads[0])
        if last and grads[1] is not None:
            for place in (1, 2):
                aliases[len(inputs)] = place
                inputs.append(grads[place])
        results = pl.pallas_call(
            partial(
                carried_kernel, chunk=chunk, per_group=per_group, last=last, ranks=ranks
            ),
            in_specs=[IN_VMEM] * (2 * ranks + 6) + [ANYWHERE] * len(aliases),
            out_specs=out_specs,
            out_shape=out_shape,
            scratch_shapes=scratch + [pltpu.SemaphoreType.DMA((3,))],
            input_output_aliases=aliases,
            compiler_params=PARAMS,
            cost_estimate=cost(6 * tokens * CHUNK * N, 14 * tokens * CHUNK),
            name=f"carried_{chunk}",
        )(*inputs)
        if last:
            return None, list(results)
        return results[1:], [results[0]] + list(grads[1:])

    fwd_got, back_got, parts = [], [], {}
    sums, grads = None, [None, None, None]
    turns = chunks + ranks - 2
    for turn in range(turns + 1):
        if 0 < turn < turns:
            fwd_send = relay(turn, 1, fwd_got[-1])
            back_send = relay(turn, -1, back_got[-1])
        if turn < turns:
            pairs = [(r, r + 1) for r in range(ranks - 1) if 0 <= turn - r < chunks]
            fwd_now = lax.ppermute(fwd_send, "ctx", pairs)
            back_now = lax.ppermute(
                back_send, "ctx", [(ranks - 1 - s, ranks - 1 - d) for s, d in pairs]
            )
        for group in range(groups):
            if turn == 1 + group:
                wx_now = lax.optimization_barrier((wx, fwd_got[-1], back_got[-1]))[0]
                parts[group] = within(group, wx_now)
                fwd_now, parts[group] = lax.optimization_barrier((fwd_now, parts[group]))
        chunk = turn - (ranks - 1)
        if 0 <= chunk < chunks:
            fwd_in = fwd_got[chunk : chunk + ranks - 1]
            back_in = back_got[chunk : chunk + ranks - 1]
            part_x, part_b, part_c = parts[chunk // per_group]
            if chunk % per_group > 0:
                part_b, part_c = sums
            sums, grads = carried(chunk, fwd_in, back_in, part_x, part_b, part_c, grads)
            if turn < turns:
                grads[0], fwd_now = lax.optimization_barrier((grads[0], fwd_now))
        fwd_got.append(fwd_now)
        back_got.append(back_now)
    return tuple(grads)


def solution(mesh):
    rows_cols = P(("groups", "ctx"), ("dp", "inner"))
    return jax.shard_map(
        on_device,
        mesh=mesh,
        in_specs=(rows_cols,) * 5 + (P(("dp", "inner")),) * 2,
        out_specs=(rows_cols,) * 3,
        check_vma=False,
    )
```

time: 539 us -> 65.3 us (0.12)
  waiting for transfers between devices: 205 us -> 16.3 us
  blocking collectives: 99.7 us -> 0 us
  local copies, waits for them, and re-layouts: 96.8 us -> 1.43 us
  matrix products: 54 us -> 0 us
  other arithmetic: 51.4 us -> 0 us
  Pallas kernels: 0 us -> 19.9 us
  between operations: 14 us -> 0.96 us
  starting transfers between devices: 14.5 us -> 26.3 us
    all_to_all x3 -> x0, waiting for transfers between devices: 141 us -> none  [the longest x1 76.4 us: on_device(): lax.all_to_all(grad_out.reshape(tokens, head_count, P_SIZE), 'ctx', split...]
    all_to_all x1 -> x0, blocking collectives: 99.7 us -> none  [on_device(): lax.all_to_all(grad_x, 'ctx', split_axis=0, concat_axis=1, tiled=True)]
    reduce_scatter x2 -> x0, waiting for transfers between devices: 63.1 us -> none  [the longest x1 63.1 us: on_device(): lax.psum_scatter(place_b, 'ctx', scatter_dimension=0, tiled=True)]
    dot_general x34 -> x0, matrix products: 54 us -> none  [product(): return jnp.einsum(form, left, right, preferred_element_type=jnp.float32)]
    unnamed x23 -> x12, local copies, waits for them, and re-layouts: 27.9 us -> 1.43 us
    ppermute x0 -> x12, starting transfers between devices: none -> 26.3 us  [the longest x6 19.8 us: on_device(): fwd_now = lax.ppermute(fwd_send, 'ctx', pairs)]
    another operation x10 -> x0, local copies, waits for them, and re-layouts: 24.7 us -> none
    pallas_call x0 -> x18, Pallas kernels: none -> 19.9 us  [the longest x2 7.35 us: local_states(): pl.pallas_call(partial(local_kernel, first=first, last=last, per_group=pe...]
  transfers between devices with their start and end apart: 7 -> 12, of which waited for: 4 -> 5; matrix products, arithmetic and copies ran while one was open for 18% -> 0% of each run, Pallas kernels for 0% -> 24%
where the time goes in v2:
time: 65.3 us; the launch traced here: 64.9 us
  starting transfers between devices  26.3 us (40%)
  Pallas kernels  19.9 us (30%)
  waiting for transfers between devices  16.3 us (25%)
  local copies, waits for them, and re-layouts  1.43 us (2%)
  between operations  0.96 us (1%)
    ppermute x6, starting transfers between devices, on_device(): fwd_now = lax.ppermute(fwd_send, 'ctx', pairs)  19.8 us
    ppermute x6, waiting for transfers between devices, on_device(): lax.ppermute(back_send, 'ctx', [(ranks - 1 - s, ranks - 1 - d) for s, d i...  14.1 us
    pallas_call x2, Pallas kernels, local_states(): pl.pallas_call(partial(local_kernel, first=first, last=last, per_group=pe...  7.35 us
    pallas_call x4, Pallas kernels, carried(): pl.pallas_call(partial(carried_kernel, chunk=chunk, per_group=per_group,...  6.55 us
    ppermute x6, starting transfers between devices, on_device(): lax.ppermute(back_send, 'ctx', [(ranks - 1 - s, ranks - 1 - d) for s, d i...  6.52 us
    pallas_call x2, Pallas kernels, within(): pl.pallas_call(partial(within_kernel, group=group, per_group=per_group),...  5.09 us
    ppermute x6, waiting for transfers between devices, on_device(): fwd_now = lax.ppermute(fwd_send, 'ctx', pairs)  2.2 us
    unnamed x12, local copies, waits for them, and re-layouts  1.43 us
  transfers between devices with their start and end apart: 12, of which 5 were waited for; matrix products, arithmetic and copies ran while one was open for 0% of the time, Pallas kernels for 24%

profile of v2, /device:TPU:0, one launch (start us, length us, event | category | flops | bytes accessed | tf_op | source)
XLA Modules:
  0.0 64.9 jit_solution(2739411084246166875)
XLA Ops:
  0.6 0.7 %copy-done.3 = bf16[512,32]{0,1:T(8,128)(2,1)S(1)} copy-done((bf16[512,32]{0,1:T(8,128)(2,1)S(1)}, bf16[512,32]{0,1:T(8,128)(2,1)}, u32[]{:S(2)}) %copy-start.3) | copy-done | bytes 32792
  2.0 2.4 %states_0.1 = (bf16[512,512]{1,0:T(8,128)(2,1)S(1)}, bf16[512,512]{1,0:T(8,128)(2,1)S(1)}, f32[1,256,512]{2,1,0:T(8,128)S(1)}, f32[1,256,512]{2,1,0:T(8,128)S(1)...) custom-call(bf16[32,512]{1,0:T(8,128)(2,1)S(1)} %bitcast.3, ...), custom_call_target="tpu_custom_call" | custom-call | flops 805306368 | bytes 1572864 | tf_op jit(solution)/shard_map/states_0/pallas_call | solution.py:229
  4.5 4.9 %collective-permute-start = (bf16[256,512]{1,0:T(8,128)(2,1)S(1)}, bf16[256,512]{1,0:T(8,128)(2,1)S(1)}, u32[]{:S(2)}, u32[]{:S(2)}) collective-permute-start(bf16[256,512]{1,0:T(8,128)(2,1)S(1)} %get-tuple-element.48), channel_id=1, source_target_pairs={{0,4},{1,5},{2,6},{3,7},{16,20},{17,21},{18,22},{19,23}} | collective-permute-start | bytes 786440 | tf_op jit(solution)/shard_map/ppermute | solution.py:328
  10.1 4.9 %states_1.1 = (bf16[512,1536]{1,0:T(8,128)(2,1)S(1)}, bf16[512,1536]{1,0:T(8,128)(2,1)S(1)}, f32[3,256,512]{2,1,0:T(8,128)S(1)}, f32[3,256,512]{2,1,0:T(8,128)S(1)}, f32[3,1,512]{2,1,0:T(1,128)S(1)}) custom-call(bf16[2,32,512]{2,1,0:T(8,128)(2,1)S(1)} %get-tuple-element.50.refs_0_, bf16[2,32,512]{2,1,0:T(8,128)(2,1)S(1)} %get-tuple-element.67.refs_1_.refs_7_.refs_10_, ...), custom_call_target="tpu_custom_call" | custom-call | flops 2415919104 | bytes 4718592 | tf_op jit(solution)/shard_map/states_1/pallas_call | solution.py:229
  15.2 4.5 %collective-permute-start.1 = (bf16[256,512]{1,0:T(8,128)(2,1)S(1)}, bf16[256,512]{1,0:T(8,128)(2,1)S(1)}, u32[]{:S(2)}, u32[]{:S(2)}) collective-permute-start(bf16[256,512]{1,0:T(8,128)(2,1)S(1)} %relay_1_2.1), channel_id=1, source_target_pairs={{0,4},{4,8},{1,5},{5,9},{2,6},{6,10},{3,7},{7,11},{16,20},{20,24},... | collective-permute-start | bytes 786440 | tf_op jit(solution)/shard_map/ppermute | solution.py:328
  19.9 0.7 %collective-permute-start.4 = (bf16[256,512]{1,0:T(8,128)(2,1)S(1)}, bf16[256,512]{1,0:T(8,128)(2,1)S(1)}, u32[]{:S(2)}, u32[]{:S(2)}) collective-permute-start(bf16[256,512]{1,0:T(8,128)(2,1)S(1)} %relay_1_3.1), channel_id=1, source_target_pairs={{12,8},{8,4},{13,9},{9,5},{14,10},{10,6},{15,11},{11,7},{28,24},{2... | collective-permute-start | bytes 786440 | tf_op jit(solution)/shard_map/ppermute | solution.py:329
  20.6 2.5 %within_0.1 = (f32[512,1024]{1,0:T(8,128)S(1)}, f32[512,256]{1,0:T(8,128)S(1)}, f32[512,256]{1,0:T(8,128)S(1)}) custom-call(bf16[512,512]{1,0:T(8,128)(2,1)S(1)} %get-tuple-element.55.refs_0_.refs_6_, bf16[512,1536]{1,0:T(8,128)(2,1)S(1)} %get-tuple-element.56.refs_1_.refs_6_, bf16[512,512]{1,0:T(8,128)(2,1)S(1)} %get-tuple-element.57.refs_2_.refs_7_, ...), custom_call_target="tpu_custom_call" | custom-call | flops 1610612736 | bytes 5242880 | tf_op jit(solution)/shard_map/within_0/pallas_call | solution.py:252
  23.1 1.3 %collective-permute-done.1.got.refs_1_.refs_0_ = bf16[256,512]{1,0:T(8,128)(2,1)S(1)} collective-permute-done((bf16[256,512]{1,0:T(8,128)(2,1)S(1)}, bf16[256,512]{1,0:T(8,128)(2,1)S(1)}, u32[]{:S(2)}, u32[]{:S(2)}) %collective-permute-start.1) | collective-permute-done | bytes 262176 | tf_op jit(solution)/shard_map/ppermute | solution.py:328
  24.5 4.4 %collective-permute-start.3 = (bf16[256,512]{1,0:T(8,128)(2,1)S(1)}, bf16[256,512]{1,0:T(8,128)(2,1)S(1)}, u32[]{:S(2)}, u32[]{:S(2)}) collective-permute-start(bf16[256,512]{1,0:T(8,128)(2,1)S(1)} %relay_2_2.1), channel_id=1, source_target_pairs={{0,4},{4,8},{8,12},{1,5},{5,9},{9,13},{2,6},{6,10},{10,14},{3,7},{... | collective-permute-start | bytes 786440 | tf_op jit(solution)/shard_map/ppermute | solution.py:328
  29.0 1.3 %collective-permute-start.5 = (bf16[256,512]{1,0:T(8,128)(2,1)S(1)}, bf16[256,512]{1,0:T(8,128)(2,1)S(1)}, u32[]{:S(2)}, u32[]{:S(2)}) collective-permute-start(bf16[256,512]{1,0:T(8,128)(2,1)S(1)} %relay_2_3.1), channel_id=1, source_target_pairs={{12,8},{8,4},{4,0},{13,9},{9,5},{5,1},{14,10},{10,6},{6,2},{15,11}... | collective-permute-start | bytes 786440 | tf_op jit(solution)/shard_map/ppermute | solution.py:329
  30.3 2.5 %within_1.1 = (f32[512,1024]{1,0:T(8,128)S(1)}, f32[512,256]{1,0:T(8,128)S(1)}, f32[512,256]{1,0:T(8,128)S(1)}) custom-call(bf16[512,512]{1,0:T(8,128)(2,1)S(1)} %get-tuple-element.55.refs_0_.refs_6_, bf16[512,1536]{1,0:T(8,128)(2,1)S(1)} %get-tuple-element.56.refs_1_.refs_6_, bf16[512,512]{1,0:T(8,128)(2,1)S(1)} %get-tuple-element.57.refs_2_.refs_7_, ...), custom_call_target="tpu_custom_call" | custom-call | flops 1610612736 | bytes 5242880 | tf_op jit(solution)/shard_map/within_1/pallas_call | solution.py:252
  33.0 4.6 %collective-permute-start.6 = (bf16[256,512]{1,0:T(8,128)(2,1)S(1)}, bf16[256,512]{1,0:T(8,128)(2,1)S(1)}, u32[]{:S(2)}, u32[]{:S(2)}) collective-permute-start(bf16[256,512]{1,0:T(8,128)(2,1)S(1)} %relay_3_2.1), channel_id=1, source_target_pairs={{0,4},{4,8},{8,12},{1,5},{5,9},{9,13},{2,6},{6,10},{10,14},{3,7},{... | collective-permute-start | bytes 786440 | tf_op jit(solution)/shard_map/ppermute | solution.py:328
  37.7 1.3 %collective-permute-start.7 = (bf16[256,512]{1,0:T(8,128)(2,1)S(1)}, bf16[256,512]{1,0:T(8,128)(2,1)S(1)}, u32[]{:S(2)}, u32[]{:S(2)}) collective-permute-start(bf16[256,512]{1,0:T(8,128)(2,1)S(1)} %relay_3_3.1), channel_id=1, source_target_pairs={{12,8},{8,4},{4,0},{13,9},{9,5},{5,1},{14,10},{10,6},{6,2},{15,11}... | collective-permute-start | bytes 786440 | tf_op jit(solution)/shard_map/ppermute | solution.py:329
  39.0 1.5 %carried_0.1 = (bf16[512,2048]{1,0:T(8,128)(2,1)}, f32[512,256]{1,0:T(8,128)S(1)}, f32[512,256]{1,0:T(8,128)S(1)}) custom-call(bf16[256,512]{1,0:T(8,128)(2,1)S(1)} %collective-permute-done.got.refs_0_, bf16[256,512]{1,0:T(8,128)(2,1)S(1)} %collective-permute-done.1.got.refs_1_.refs_0_, ...), custom_call_target="tpu_custom_call" | custom-call | flops 402653184 | bytes 3670016 | tf_op jit(solution)/shard_map/carried_0/pallas_call | solution.py:302
  40.5 0.9 %collective-permute-done.6.refs_2_.got.refs_1_.refs_0_ = bf16[256,512]{1,0:T(8,128)(2,1)S(1)} collective-permute-done((bf16[256,512]{1,0:T(8,128)(2,1)S(1)}, bf16[256,512]{1,0:T(8,128)(2,1)S(1)}, u32[]{:S(2)}, u32[]{:S(2)}) %collective-permute-start.6) | collective-permute-done | bytes 262176 | tf_op jit(solution)/shard_map/ppermute | solution.py:328
  41.5 0.7 %collective-permute-start.8 = (bf16[256,512]{1,0:T(8,128)(2,1)S(1)}, bf16[256,512]{1,0:T(8,128)(2,1)S(1)}, u32[]{:S(2)}, u32[]{:S(2)}) collective-permute-start(bf16[256,512]{1,0:T(8,128)(2,1)S(1)} %relay_4_2.1), channel_id=1, source_target_pairs={{4,8},{8,12},{5,9},{9,13},{6,10},{10,14},{7,11},{11,15},{20,24},{2... | collective-permute-start | bytes 786440 | tf_op jit(solution)/shard_map/ppermute | solution.py:328
  42.2 3.8 %collective-permute-done.7.refs_5_.got.refs_4_.refs_3_ = bf16[256,512]{1,0:T(8,128)(2,1)S(1)} collective-permute-done((bf16[256,512]{1,0:T(8,128)(2,1)S(1)}, bf16[256,512]{1,0:T(8,128)(2,1)S(1)}, u32[]{:S(2)}, u32[]{:S(2)}) %collective-permute-start.7) | collective-permute-done | bytes 262176 | tf_op jit(solution)/shard_map/ppermute | solution.py:329
  46.1 1.3 %collective-permute-start.9 = (bf16[256,512]{1,0:T(8,128)(2,1)S(1)}, bf16[256,512]{1,0:T(8,128)(2,1)S(1)}, u32[]{:S(2)}, u32[]{:S(2)}) collective-permute-start(bf16[256,512]{1,0:T(8,128)(2,1)S(1)} %relay_4_3.1), channel_id=1, source_target_pairs={{8,4},{4,0},{9,5},{5,1},{10,6},{6,2},{11,7},{7,3},{24,20},{20,16},... | collective-permute-start | bytes 786440 | tf_op jit(solution)/shard_map/ppermute | solution.py:329
  47.4 1.8 %carried_1.1 = (bf16[512,2048]{1,0:T(8,128)(2,1)}, bf16[512,512]{1,0:T(8,128)(2,1)}, bf16[512,512]{1,0:T(8,128)(2,1)}) custom-call(bf16[256,512]{1,0:T(8,128)(2,1)S(1)} %collective-permute-done.1.got.refs_1_.refs_0_, bf16[256,512]{1,0:T(8,128)(2,1)S(1)} %collective-permute-done.3.refs_2_.got.refs_1_.refs_0_, ...), custom_call_target="tpu_custom_call", output_to_operand_aliasing={{0}: (14, {})} | custom-call | flops 402653184 | bytes 3670016 | tf_op jit(solution)/shard_map/carried_1/pallas_call | solution.py:302
  49.9 4.8 %collective-permute-done.9.refs_5_.got.refs_4_ = bf16[256,512]{1,0:T(8,128)(2,1)S(1)} collective-permute-done((bf16[256,512]{1,0:T(8,128)(2,1)S(1)}, bf16[256,512]{1,0:T(8,128)(2,1)S(1)}, u32[]{:S(2)}, u32[]{:S(2)}) %collective-permute-start.9) | collective-permute-done | bytes 262176 | tf_op jit(solution)/shard_map/ppermute | solution.py:329
  54.9 1.3 %collective-permute-start.11 = (bf16[256,512]{1,0:T(8,128)(2,1)S(1)}, bf16[256,512]{1,0:T(8,128)(2,1)S(1)}, u32[]{:S(2)}, u32[]{:S(2)}) collective-permute-start(bf16[256,512]{1,0:T(8,128)(2,1)S(1)} %relay_5_3.1), channel_id=1, source_target_pairs={{4,0},{5,1},{6,2},{7,3},{20,16},{21,17},{22,18},{23,19}} | collective-permute-start | bytes 786440 | tf_op jit(solution)/shard_map/ppermute | solution.py:329
  56.2 1.5 %carried_2.1 = (bf16[512,2048]{1,0:T(8,128)(2,1)}, f32[512,256]{1,0:T(8,128)S(1)}, f32[512,256]{1,0:T(8,128)S(1)}) custom-call(bf16[256,512]{1,0:T(8,128)(2,1)S(1)} %collective-permute-done.3.refs_2_.got.refs_1_.refs_0_, bf16[256,512]{1,0:T(8,128)(2,1)S(1)} %collective-permute-done.6.refs_2_.got.refs_1_.refs_0_, ...), custom_call_target="tpu_custom_call", output_to_operand_aliasing={{0}: (14, {})} | custom-call | flops 402653184 | bytes 3670016 | tf_op jit(solution)/shard_map/carried_2/pallas_call | solution.py:302
  57.7 5.4 %collective-permute-done.11.refs_5_ = bf16[256,512]{1,0:T(8,128)(2,1)S(1)} collective-permute-done((bf16[256,512]{1,0:T(8,128)(2,1)S(1)}, bf16[256,512]{1,0:T(8,128)(2,1)S(1)}, u32[]{:S(2)}, u32[]{:S(2)}) %collective-permute-start.11) | collective-permute-done | bytes 262176 | tf_op jit(solution)/shard_map/ppermute | solution.py:329
  63.1 1.8 %carried_3.1 = (bf16[512,2048]{1,0:T(8,128)(2,1)}, bf16[512,512]{1,0:T(8,128)(2,1)}, bf16[512,512]{1,0:T(8,128)(2,1)}) custom-call(bf16[256,512]{1,0:T(8,128)(2,1)S(1)} %collective-permute-done.6.refs_2_.got.refs_1_.refs_0_, ...), custom_call_target="tpu_custom_call", output_to_operand_aliasing={{0}: (14, {}), {1}: (15, {}), {2}: (16, {})} | custom-call | flops 402653184 | bytes 3670016 | tf_op jit(solution)/shard_map/carried_3/pallas_call | solution.py:302
  (30 shorter events, 3.0 us)
Async XLA Ops:
  0.6 0.8 %copy-start.3 = (bf16[512,32]{0,1:T(8,128)(2,1)S(1)}, bf16[512,32]{0,1:T(8,128)(2,1)}, u32[]{:S(2)}) copy-start(bf16[512,32]{0,1:T(8,128)(2,1)} %param.11) | copy-start | bytes 98308
  1.4 0.7 %copy-start.5 = (f32[32]{0:T(128)S(1)}, f32[32]{0:T(128)}, u32[]{:S(2)}) copy-start(f32[32]{0:T(128)} %param.12) | copy-start | bytes 388
  4.5 10.6 %collective-permute-start = (bf16[256,512]{1,0:T(8,128)(2,1)S(1)}, bf16[256,512]{1,0:T(8,128)(2,1)S(1)}, u32[]{:S(2)}, u32[]{:S(2)}) collective-permute-start(bf16[256,512]{1,0:T(8,128)(2,1)S(1)} %get-tuple-element.48), channel_id=1, source_target_pairs={{0,4},{1,5},{2,6},{3,7},{16,20},{17,21},{18,22},{19,23}} | collective-permute-start | bytes 786440 | tf_op jit(solution)/shard_map/ppermute | solution.py:328
  9.4 10.3 %collective-permute-start.2 = (bf16[256,512]{1,0:T(8,128)(2,1)S(1)}, bf16[256,512]{1,0:T(8,128)(2,1)S(1)}, u32[]{:S(2)}, u32[]{:S(2)}) collective-permute-start(bf16[256,512]{1,0:T(8,128)(2,1)S(1)} %get-tuple-element.59), channel_id=1, source_target_pairs={{12,8},{13,9},{14,10},{15,11},{28,24},{29,25},{30,26},{31,27}} | collective-permute-start | bytes 786440 | tf_op jit(solution)/shard_map/ppermute | solution.py:329
  15.1 5.5 %copy-start = (bf16[512,512]{1,0:T(8,128)(2,1)S(1)}, bf16[512,512]{1,0:T(8,128)(2,1)}, u32[]{:S(2)}) copy-start(bf16[512,512]{1,0:T(8,128)(2,1)} %refs_8_.7) | copy-start | bytes 1572868
  15.1 5.5 %copy-start.1 = (bf16[512,2048]{1,0:T(8,128)(2,1)S(1)}, bf16[512,2048]{1,0:T(8,128)(2,1)}, u32[]{:S(2)}) copy-start(bf16[512,2048]{1,0:T(8,128)(2,1)} %refs_6_.3) | copy-start | bytes 6291460
  15.1 5.5 %copy-start.2 = (bf16[512,512]{1,0:T(8,128)(2,1)S(1)}, bf16[512,512]{1,0:T(8,128)(2,1)}, u32[]{:S(2)}) copy-start(bf16[512,512]{1,0:T(8,128)(2,1)} %refs_5_.7) | copy-start | bytes 1572868
  15.1 5.5 %copy-start.4 = (f32[32]{0:T(128)S(1)}, f32[32]{0:T(128)}, u32[]{:S(2)}) copy-start(f32[32]{0:T(128)} %param.13) | copy-start | bytes 388
  15.2 9.2 %collective-permute-start.1 = (bf16[256,512]{1,0:T(8,128)(2,1)S(1)}, bf16[256,512]{1,0:T(8,128)(2,1)S(1)}, u32[]{:S(2)}, u32[]{:S(2)}) collective-permute-start(bf16[256,512]{1,0:T(8,128)(2,1)S(1)} %relay_1_2.1), channel_id=1, source_target_pairs={{0,4},{4,8},{1,5},{5,9},{2,6},{6,10},{3,7},{7,11},{16,20},{20,24},... | collective-permute-start | bytes 786440 | tf_op jit(solution)/shard_map/ppermute | solution.py:328
  19.9 9.1 %collective-permute-start.4 = (bf16[256,512]{1,0:T(8,128)(2,1)S(1)}, bf16[256,512]{1,0:T(8,128)(2,1)S(1)}, u32[]{:S(2)}, u32[]{:S(2)}) collective-permute-start(bf16[256,512]{1,0:T(8,128)(2,1)S(1)} %relay_1_3.1), channel_id=1, source_target_pairs={{12,8},{8,4},{13,9},{9,5},{14,10},{10,6},{15,11},{11,7},{28,24},{2... | collective-permute-start | bytes 786440 | tf_op jit(solution)/shard_map/ppermute | solution.py:329
  24.5 8.4 %collective-permute-start.3 = (bf16[256,512]{1,0:T(8,128)(2,1)S(1)}, bf16[256,512]{1,0:T(8,128)(2,1)S(1)}, u32[]{:S(2)}, u32[]{:S(2)}) collective-permute-start(bf16[256,512]{1,0:T(8,128)(2,1)S(1)} %relay_2_2.1), channel_id=1, source_target_pairs={{0,4},{4,8},{8,12},{1,5},{5,9},{9,13},{2,6},{6,10},{10,14},{3,7},{... | collective-permute-start | bytes 786440 | tf_op jit(solution)/shard_map/ppermute | solution.py:328
  29.0 8.5 %collective-permute-start.5 = (bf16[256,512]{1,0:T(8,128)(2,1)S(1)}, bf16[256,512]{1,0:T(8,128)(2,1)S(1)}, u32[]{:S(2)}, u32[]{:S(2)}) collective-permute-start(bf16[256,512]{1,0:T(8,128)(2,1)S(1)} %relay_2_3.1), channel_id=1, source_target_pairs={{12,8},{8,4},{4,0},{13,9},{9,5},{5,1},{14,10},{10,6},{6,2},{15,11}... | collective-permute-start | bytes 786440 | tf_op jit(solution)/shard_map/ppermute | solution.py:329
  33.0 8.4 %collective-permute-start.6 = (bf16[256,512]{1,0:T(8,128)(2,1)S(1)}, bf16[256,512]{1,0:T(8,128)(2,1)S(1)}, u32[]{:S(2)}, u32[]{:S(2)}) collective-permute-start(bf16[256,512]{1,0:T(8,128)(2,1)S(1)} %relay_3_2.1), channel_id=1, source_target_pairs={{0,4},{4,8},{8,12},{1,5},{5,9},{9,13},{2,6},{6,10},{10,14},{3,7},{... | collective-permute-start | bytes 786440 | tf_op jit(solution)/shard_map/ppermute | solution.py:328
  37.7 8.3 %collective-permute-start.7 = (bf16[256,512]{1,0:T(8,128)(2,1)S(1)}, bf16[256,512]{1,0:T(8,128)(2,1)S(1)}, u32[]{:S(2)}, u32[]{:S(2)}) collective-permute-start(bf16[256,512]{1,0:T(8,128)(2,1)S(1)} %relay_3_3.1), channel_id=1, source_target_pairs={{12,8},{8,4},{4,0},{13,9},{9,5},{5,1},{14,10},{10,6},{6,2},{15,11}... | collective-permute-start | bytes 786440 | tf_op jit(solution)/shard_map/ppermute | solution.py:329
  41.5 7.6 %collective-permute-start.8 = (bf16[256,512]{1,0:T(8,128)(2,1)S(1)}, bf16[256,512]{1,0:T(8,128)(2,1)S(1)}, u32[]{:S(2)}, u32[]{:S(2)}) collective-permute-start(bf16[256,512]{1,0:T(8,128)(2,1)S(1)} %relay_4_2.1), channel_id=1, source_target_pairs={{4,8},{8,12},{5,9},{9,13},{6,10},{10,14},{7,11},{11,15},{20,24},{2... | collective-permute-start | bytes 786440 | tf_op jit(solution)/shard_map/ppermute | solution.py:328
  46.1 8.7 %collective-permute-start.9 = (bf16[256,512]{1,0:T(8,128)(2,1)S(1)}, bf16[256,512]{1,0:T(8,128)(2,1)S(1)}, u32[]{:S(2)}, u32[]{:S(2)}) collective-permute-start(bf16[256,512]{1,0:T(8,128)(2,1)S(1)} %relay_4_3.1), channel_id=1, source_target_pairs={{8,4},{4,0},{9,5},{5,1},{10,6},{6,2},{11,7},{7,3},{24,20},{20,16},... | collective-permute-start | bytes 786440 | tf_op jit(solution)/shard_map/ppermute | solution.py:329
  49.2 8.4 %collective-permute-start.10 = (bf16[256,512]{1,0:T(8,128)(2,1)S(1)}, bf16[256,512]{1,0:T(8,128)(2,1)S(1)}, u32[]{:S(2)}, u32[]{:S(2)}) collective-permute-start(bf16[256,512]{1,0:T(8,128)(2,1)S(1)} %relay_5_2.1), channel_id=1, source_target_pairs={{8,12},{9,13},{10,14},{11,15},{24,28},{25,29},{26,30},{27,31}} | collective-permute-start | bytes 786440 | tf_op jit(solution)/shard_map/ppermute | solution.py:328
  54.9 8.3 %collective-permute-start.11 = (bf16[256,512]{1,0:T(8,128)(2,1)S(1)}, bf16[256,512]{1,0:T(8,128)(2,1)S(1)}, u32[]{:S(2)}, u32[]{:S(2)}) collective-permute-start(bf16[256,512]{1,0:T(8,128)(2,1)S(1)} %relay_5_3.1), channel_id=1, source_target_pairs={{4,0},{5,1},{6,2},{7,3},{20,16},{21,17},{22,18},{23,19}} | collective-permute-start | bytes 786440 | tf_op jit(solution)/shard_map/ppermute | solution.py:329

commit v3 on v2

v3 whole, which is shorter than its diff:
```python
from functools import partial

import jax
import jax.numpy as jnp
from jax import lax
from jax.experimental import pallas as pl
from jax.experimental.pallas import tpu as pltpu
from jax.sharding import PartitionSpec as P

P_SIZE = 64
N = 256
CHUNK = 512
CHUNK_HEADS = CHUNK // P_SIZE
F32 = jnp.float32
BF16 = jnp.bfloat16
PARAMS = pltpu.CompilerParams(vmem_limit_bytes=16 * 1024 * 1024)
RELAY_PARAMS = pltpu.CompilerParams(vmem_limit_bytes=4 * 1024 * 1024)
ANYWHERE = pl.BlockSpec(memory_space=pl.ANY)
IN_VMEM = pl.BlockSpec(memory_space=pltpu.VMEM)


def dot(left, right, left_dim, right_dim):
    return lax.dot_general(
        left, right, (((left_dim,), (right_dim,)), ((), ())), preferred_element_type=F32
    )


def terms(value, count):
    parts = []
    for _ in range(count):
        part = value.astype(BF16)
        parts.append(part)
        value = value - part.astype(F32)
    return parts


def head_spread(parts, chunk):
    head_count = parts[0].shape[0]
    rows = lax.broadcasted_iota(jnp.int32, (head_count, CHUNK), 0)
    cols = lax.broadcasted_iota(jnp.int32, (head_count, CHUNK), 1)
    pick = (rows == chunk * CHUNK_HEADS + cols // P_SIZE).astype(F32).astype(BF16)
    total = dot(parts[0], pick, 0, 0)
    for part in parts[1:]:
        total += dot(part, pick, 0, 0)
    return total


def lower_mask(tokens):
    rows = lax.broadcasted_iota(jnp.int32, (tokens, tokens), 0)
    cols = lax.broadcasted_iota(jnp.int32, (tokens, tokens), 1)
    return rows >= cols


def columns(row):
    size = row.shape[1]
    rows = lax.broadcasted_iota(jnp.int32, (size, size), 0)
    cols = lax.broadcasted_iota(jnp.int32, (size, size), 1)
    return jnp.sum(jnp.where(rows == cols, row, 0.0), axis=1, keepdims=True)


def heading(even_links, ranks):
    rank = lax.axis_index("ctx")
    forward = (lax.rem(rank, 2) == 0) == even_links
    return forward, jnp.where(forward, rank, ranks - 1 - rank)


def local_kernel(*refs, first, last, per_group, ranks):
    if first == 0:
        step_hbm, rate_hbm, dy, x, b, c = refs[:6]
        dyw, xw, states, decay, wd, wx, send = refs[6:13]
        step, rate, dy_in, x_in, b_in, c_in, sems = refs[13:]
    else:
        wd, wx, dy, x, b, c = refs[:6]
        dyw, xw, states, decay = refs[6:10]
        dy_in, x_in, b_in, c_in, sems = refs[10:]
    tokens = dy_in.shape[0]
    low_group = first // per_group

    def fetch(source, target, place):
        copy = pltpu.make_async_copy(source, target, sems.at[place])
        copy.start()
        return copy

    def part(source, target, low, place):
        return fetch(source.at[:, pl.ds(low, target.shape[1])], target, place)

    if first == 0:
        small = [fetch(step_hbm, step, 4), fetch(rate_hbm, rate, 5)]
    copies = [
        part(dy, dy_in, first * CHUNK, 0),
        part(c, c_in, low_group * N, 1),
        part(x, x_in, first * CHUNK, 2),
        part(b, b_in, low_group * N, 3),
    ]
    if first == 0:
        rows = lax.broadcasted_iota(jnp.int32, (tokens, tokens), 0)
        cols = lax.broadcasted_iota(jnp.int32, (tokens, tokens), 1)
        upper = (rows <= cols).astype(F32).astype(BF16)
        for copy in small:
            copy.wait()
        cum = dot(step[...], upper, 1, 0) * columns(rate[...])
        wd[0], wd[1] = terms(jnp.exp(cum), 2)
        wx[0], wx[1] = terms(jnp.exp(-cum) * step[...].astype(F32), 2)
    for copy in copies:
        copy.wait()
    for chunk in range(first, last):
        place = chunk - first
        span = pl.ds(place * CHUNK, CHUNK)
        group = pl.ds((chunk // per_group - low_group) * N, N)
        spread = head_spread((wd[0], wd[1]), chunk)
        end = spread[tokens - 1 : tokens, :]
        decay[place] = end
        dyw[:, span] = (spread * dy_in[:, span].astype(F32)).astype(BF16)
        spread = head_spread((wx[0], wx[1]), chunk)
        xw[:, span] = (spread * x_in[:, span].astype(F32)).astype(BF16)
        states[place, 1] = dot(c_in[:, group], dyw[:, span], 0, 0)
        states[place, 0] = dot(b_in[:, group], xw[:, span], 0, 0) * end
    if first == 0:
        forward, _ = heading(True, ranks)
        send[...] = states[0, jnp.where(forward, 0, 1)].astype(BF16)


def piece(refs, chunk, starts):
    place = max(i for i, start in enumerate(starts) if start <= chunk)
    return refs[place][:, pl.ds((chunk - starts[place]) * CHUNK, CHUNK)]


def within_kernel(*refs, group, per_group, starts):
    count = len(starts)
    dyw, xw, refs = refs[:count], refs[count : 2 * count], refs[2 * count :]
    b, c, dy, wx, gain, grad_x, grad_b, grad_c = refs
    lower = lower_mask(b.shape[0])
    own = pl.ds(group * N, N)
    chunks = range(group * per_group, (group + 1) * per_group)
    scores = jnp.where(lower, dot(c[:, own], b[:, own], 1, 1), 0.0).astype(BF16)
    weighted = sum(
        dot(piece(dyw, chunk, starts), piece(xw, chunk, starts), 1, 1) for chunk in chunks
    )
    weighted = jnp.where(lower, weighted, 0.0).astype(BF16)
    grad_b[...] = dot(weighted, c[:, own], 0, 0)
    grad_c[...] = dot(weighted, b[:, own], 1, 0)
    gains = terms(jnp.broadcast_to(columns(gain[...]), (gain.shape[1], 128)), 3)
    for part, chunk in enumerate(chunks):
        spread = head_spread((wx[0], wx[1]), chunk)
        rows = dy[:, pl.ds(chunk * CHUNK, CHUNK)].astype(F32)
        skip = head_spread(gains, chunk)[0:1, :] * rows
        grad_x[:, pl.ds(part * CHUNK, CHUNK)] = (
            spread * dot(scores, piece(dyw, chunk, starts), 0, 0) + skip
        )


def relay_kernel(*refs, turn, even_links, ranks, starts):
    out, refs = refs[-1], refs[:-1]
    count = len(starts)
    states, decays, got = refs[:count], refs[count : 2 * count], refs[2 * count :]
    forward, lag = heading(even_links, ranks)
    kind = jnp.where(forward, 0, 1)
    chunk = turn - lag
    state = shrink = None
    for start, state_ref, decay_ref in zip(starts, states, decays):
        place = jnp.clip(chunk - start, 0, state_ref.shape[0] - 1)
        if state is None:
            state, shrink = state_ref[place, kind], decay_ref[place]
        else:
            state = jnp.where(chunk >= start, state_ref[place, kind], state)
            shrink = jnp.where(chunk >= start, decay_ref[place], shrink)
    if got:
        state = got[0][...].astype(F32) * shrink + state
    out[...] = state.astype(BF16)


def chosen(candidates, source):
    value = jnp.zeros(candidates[0].shape, BF16)
    for place, candidate in enumerate(candidates):
        value = jnp.where(source == place, candidate[...], value)
    return value


def carried_kernel(*refs, chunk, per_group, last, ranks, start):
    rank = lax.axis_index("ctx")
    fwd_in = chosen(refs[: ranks - 1], rank - 1)
    back_in = chosen(refs[: ranks - 1], ranks - 2 - rank)
    refs = refs[ranks - 1 :]
    dyw, xw, b, decay, wx, part_x, part_b, part_c = refs[:8]
    group, inside = chunk // per_group, chunk % per_group
    grad_x, grad_b, grad_c = refs[-7 if last else -5 :][:3]
    x_out = refs[-4] if last else refs[-2]
    sems = refs[-1]
    place = chunk - start
    span = pl.ds(place * CHUNK, CHUNK)
    own = pl.ds(group * N, N)
    copies = []

    def send(source, target, place):
        copies.append(pltpu.make_async_copy(source, target, sems.at[place]))
        copies[-1].start()

    back = (back_in.astype(F32) * decay[place]).astype(BF16)
    spread = head_spread((wx[0], wx[1]), chunk)
    carried = spread * dot(b[:, own], back, 1, 0)
    x_out[...] = (part_x[:, pl.ds(inside * CHUNK, CHUNK)] + carried).astype(BF16)
    send(x_out, grad_x.at[:, pl.ds(chunk * CHUNK, CHUNK)], 0)
    total_b = part_b[...] + dot(xw[:, span], back, 1, 1)
    if last:
        b_out, c_out = refs[-3:-1]
        b_out[...] = total_b.astype(BF16)
        send(b_out, grad_b.at[:, own], 1)
    else:
        grad_b[...] = total_b
    total_c = part_c[...] + dot(dyw[:, span], fwd_in, 1, 1)
    if last:
        c_out[...] = total_c.astype(BF16)
        send(c_out, grad_c.at[:, own], 2)
    else:
        grad_c[...] = total_c
    for copy in copies:
        copy.wait()


def cost(flops, bytes_accessed):
    return pl.CostEstimate(flops=flops, bytes_accessed=bytes_accessed, transcendentals=0)


def on_device(grad_out, saved_x, saved_b, saved_c, step_size, decay_rate, skip_gain):
    tokens, row_width = grad_out.shape
    head_count = step_size.shape[1]
    groups = saved_b.shape[1] // N
    chunks = row_width // CHUNK
    per_group = chunks // groups
    group_width = row_width // groups
    ranks = lax.axis_size("ctx")
    gain_row = skip_gain.reshape(1, head_count)
    stay = partial(pltpu.with_memory_space_constraint, memory_space=pltpu.HBM)
    sources = [stay(array) for array in (grad_out, saved_x, saved_b, saved_c)]
    starts = [start for start in (0, 1) if start < chunks]
    stops = starts[1:] + [chunks]

    def local_states(first, last, inputs, in_spec, extra_shapes, extra_scratch):
        wide = (last - first) * CHUNK
        out_shape = [
            pltpu.VMEM((tokens, wide), BF16),
            pltpu.VMEM((tokens, wide), BF16),
            pltpu.VMEM((last - first, 2, N, CHUNK), F32),
            pltpu.VMEM((last - first, 1, CHUNK), F32),
        ] + extra_shapes
        tall = ((last - 1) // per_group - first // per_group + 1) * N
        return pl.pallas_call(
            partial(local_kernel, first=first, last=last, per_group=per_group, ranks=ranks),
            in_specs=[in_spec] * 2 + [ANYWHERE] * 4,
            out_specs=[IN_VMEM] * len(out_shape),
            out_shape=out_shape,
            scratch_shapes=extra_scratch
            + [
                pltpu.VMEM((tokens, wide), BF16),
                pltpu.VMEM((tokens, wide), BF16),
                pltpu.VMEM((tokens, tall), BF16),
                pltpu.VMEM((tokens, tall), BF16),
                pltpu.SemaphoreType.DMA((6,)),
            ],
            compiler_params=PARAMS,
            cost_estimate=cost(4 * tokens * wide * (N + 512), 6 * tokens * wide),
            name=f"states_{first}",
        )(*inputs)

    *head, wd, wx, first_send = local_states(
        0,
        stops[0],
        [stay(step_size.T), stay(decay_rate.reshape(1, head_count))] + sources,
        ANYWHERE,
        [pltpu.VMEM((2, head_count, tokens), BF16)] * 2 + [pltpu.VMEM((N, CHUNK), BF16)],
        [pltpu.VMEM((head_count, tokens), BF16), pltpu.VMEM((1, head_count), F32)],
    )
    pieces = [head]

    def more_states(wd):
        place = len(pieces)
        pieces.append(
            local_states(
                starts[place], stops[place], [wd, wx] + sources, IN_VMEM, [], []
            )
        )

    def within(group, wx):
        return pl.pallas_call(
            partial(within_kernel, group=group, per_group=per_group, starts=starts),
            in_specs=[IN_VMEM] * (2 * len(starts) + 5),
            out_specs=[IN_VMEM] * 3,
            out_shape=[
                pltpu.VMEM((tokens, group_width), F32),
                pltpu.VMEM((tokens, N), F32),
                pltpu.VMEM((tokens, N), F32),
            ],
            compiler_params=PARAMS,
            cost_estimate=cost(
                4 * tokens * tokens * (group_width + 2 * N), 10 * tokens * group_width
            ),
            name=f"within_{group}",
        )(
            *[piece[0] for piece in pieces],
            *[piece[1] for piece in pieces],
            saved_b,
            saved_c,
            grad_out,
            wx,
            gain_row,
        )

    def relay(turn, even_links, got):
        top = turn if even_links else turn - 1
        count = sum(start <= top for start in starts)
        got = [] if got is None else [got]
        return pl.pallas_call(
            partial(
                relay_kernel,
                turn=turn,
                even_links=even_links,
                ranks=ranks,
                starts=starts[:count],
            ),
            in_specs=[IN_VMEM] * (2 * count + len(got)),
            out_specs=IN_VMEM,
            out_shape=pltpu.VMEM((N, CHUNK), BF16),
            compiler_params=RELAY_PARAMS,
            cost_estimate=cost(4 * N * CHUNK, 8 * N * CHUNK),
            name=f"relay_{turn}",
        )(
            *[piece[2] for piece in pieces[:count]],
            *[piece[3] for piece in pieces[:count]],
            *got,
        )

    def carried(chunk, candidates, part_x, part_b, part_c, grads):
        place = max(i for i, start in enumerate(starts) if start <= chunk)
        own = pieces[place]
        last = chunk % per_group == per_group - 1
        out_shape = [jax.ShapeDtypeStruct((tokens, row_width), BF16)]
        out_specs = [ANYWHERE]
        scratch = [pltpu.VMEM((tokens, CHUNK), BF16)]
        if last:
            out_shape += [jax.ShapeDtypeStruct((tokens, groups * N), BF16)] * 2
            out_specs += [ANYWHERE] * 2
            scratch += [pltpu.VMEM((tokens, N), BF16)] * 2
        else:
            out_shape += [pltpu.VMEM((tokens, N), F32)] * 2
            out_specs += [IN_VMEM] * 2
        inputs = [*candidates, own[0], own[1], saved_b, own[3], wx, part_x, part_b, part_c]
        aliases = {}
        if grads[0] is not None:
            aliases[len(inputs)] = 0
            inputs.append(grads[0])
        if last and grads[1] is not None:
            for slot in (1, 2):
                aliases[len(inputs)] = slot
                inputs.append(grads[slot])
        results = pl.pallas_call(
            partial(
                carried_kernel,
                chunk=chunk,
                per_group=per_group,
                last=last,
                ranks=ranks,
                start=starts[place],
            ),
            in_specs=[IN_VMEM] * (ranks + 7) + [ANYWHERE] * len(aliases),
            out_specs=out_specs,
            out_shape=out_shape,
            scratch_shapes=scratch + [pltpu.SemaphoreType.DMA((3,))],
            input_output_aliases=aliases,
            compiler_params=PARAMS,
            cost_estimate=cost(6 * tokens * CHUNK * N, 14 * tokens * CHUNK),
            name=f"carried_{chunk}",
        )(*inputs)
        if last:
            return None, list(results)
        return results[1:], [results[0]] + list(grads[1:])

    def links(turn, even_links):
        pairs = []
        for low in range(0 if even_links else 1, ranks - 1, 2):
            if 0 <= turn - low < chunks:
                pairs.append((low, low + 1))
            if 0 <= turn - (ranks - 2 - low) < chunks:
                pairs.append((low + 1, low))
        return pairs

    turns = chunks + ranks - 2
    order = []
    for base in range(turns):
        for turn in (base, base + 1):
            even_links = base % 2 == 0
            if turn < turns and links(turn, even_links):
                order.append((turn, even_links))
    got, parts = {}, {}
    sums, grads = None, [None, None, None]
    groups_left, chunks_left = list(range(groups)), list(range(chunks))

    def carry():
        nonlocal sums, grads
        chunk = chunks_left.pop(0)
        candidates = [got[chunk + hop, hop % 2 == 0] for hop in range(ranks - 1)]
        part_x, part_b, part_c = parts[chunk // per_group]
        if chunk % per_group > 0:
            part_b, part_c = sums
        sums, grads = carried(chunk, candidates, part_x, part_b, part_c, grads)

    for position, (turn, even_links) in enumerate(order):
        before = got.get((turn - 1, not even_links))
        if position == 1 and len(pieces) < len(starts):
            more_states(wd)
        send = first_send if position == 0 else relay(turn, even_links, before)
        key = (turn, even_links)
        got[key] = lax.ppermute(send, "ctx", links(turn, even_links))
        ready = order[: position - 1]
        following = order[position - 1] if position else None
        if position == 1:
            while len(pieces) < len(starts):
                more_states(lax.optimization_barrier((wd, send))[0])
                pieces[-1], got[following] = lax.optimization_barrier(
                    (pieces[-1], got[following])
                )
        elif position % 2 == 0 and position > 0:
            if groups_left:
                group = groups_left.pop(0)
                parts[group] = within(group, lax.optimization_barrier((wx, before))[0])
                parts[group], got[following] = lax.optimization_barrier(
                    (parts[group], got[following])
                )
            elif chunks_left and (chunks_left[0] + ranks - 2, True) in ready:
                carry()
                grads[0], got[following] = lax.optimization_barrier((grads[0], got[following]))
    while groups_left:
        group = groups_left.pop(0)
        parts[group] = within(group, wx)
    while chunks_left:
        carry()
    return tuple(grads)


def solution(mesh):
    rows_cols = P(("groups", "ctx"), ("dp", "inner"))
    return jax.shard_map(
        on_device,
        mesh=mesh,
        in_specs=(rows_cols,) * 5 + (P(("dp", "inner")),) * 2,
        out_specs=(rows_cols,) * 3,
        check_vma=False,
    )
```

time: 65.3 us -> 56.9 us (0.87)
  starting transfers between devices: 26.3 us -> 20 us
  local copies, waits for them, and re-layouts: 1.43 us -> 0.03 us
  waiting for transfers between devices: 16.3 us -> 15.6 us
    ppermute x12 -> x10, starting transfers between devices: 26.3 us -> 20 us  [on_device(): got[key] = lax.ppermute(send, 'ctx', links(turn, even_links))]
    unnamed x12 -> x8, local copies, waits for them, and re-layouts: 1.43 us -> 0.03 us
    ppermute x12 -> x10, waiting for transfers between devices: 16.3 us -> 15.6 us  [on_device(): got[key] = lax.ppermute(send, 'ctx', links(turn, even_links))]
    pallas_call x12 -> x11, Pallas kernels: 6.01 us -> 5.95 us  [the longest x2 5.09 us: within(): pl.pallas_call(partial(within_kernel, group=group, per_group=per_group, s...]
  transfers between devices with their start and end apart: 12 -> 10, of which waited for: 5 -> 5; matrix products, arithmetic and copies ran while one was open for 0% -> 0% of each run, Pallas kernels for 24% -> 28%
where the time goes in v3:
time: 56.9 us; the launch traced here: 56.6 us
  Pallas kernels  20 us (35%)
  starting transfers between devices  20 us (35%)
  waiting for transfers between devices  15.6 us (27%)
  between operations  0.89 us (2%)
    ppermute x10, starting transfers between devices, on_device(): got[key] = lax.ppermute(send, 'ctx', links(turn, even_links))  20 us
    ppermute x10, waiting for transfers between devices, on_device(): got[key] = lax.ppermute(send, 'ctx', links(turn, even_links))  15.6 us
    pallas_call x2, Pallas kernels, local_states(): pl.pallas_call(partial(local_kernel, first=first, last=last, per_group=pe...  7.55 us
    pallas_call x4, Pallas kernels, carried(): pl.pallas_call(partial(carried_kernel, chunk=chunk, per_group=per_group,...  6.51 us
    pallas_call x2, Pallas kernels, within(): pl.pallas_call(partial(within_kernel, group=group, per_group=per_group, s...  5.09 us
  transfers between devices with their start and end apart: 10, of which 5 were waited for; matrix products, arithmetic and copies ran while one was open for 0% of the time, Pallas kernels for 28%

profile of v3, /device:TPU:0, one launch (start us, length us, event | category | flops | bytes accessed | tf_op | source)
XLA Modules:
  0.0 56.6 jit_solution(15781170975775350906)
XLA Ops:
  0.6 2.6 %states_0.1 = (bf16[512,512]{1,0:T(8,128)(2,1)S(1)}, bf16[512,512]{1,0:T(8,128)(2,1)S(1)}, f32[1,2,256,512]{3,2,1,0:T(8,128)S(1)}, f32[1,1,512]{2,1,0:T(1,128)S(...) custom-call(bf16[32,512]{1,0:T(8,128)(2,1)} %bitcast.5, ...), custom_call_target="tpu_custom_call" | custom-call | flops 805306368 | bytes 1572864 | tf_op jit(solution)/shard_map/states_0/pallas_call | solution.py:247
  3.3 4.9 %collective-permute-start = (bf16[256,512]{1,0:T(8,128)(2,1)S(1)}, bf16[256,512]{1,0:T(8,128)(2,1)S(1)}, u32[]{:S(2)}, u32[]{:S(2)}) collective-permute-start(bf16[256,512]{1,0:T(8,128)(2,1)S(1)} %get-tuple-element.43), channel_id=1, source_target_pairs={{0,4},{12,8},{1,5},{13,9},{2,6},{14,10},{3,7},{15,11},{16,20},{28,... | collective-permute-start | bytes 786440 | tf_op jit(solution)/shard_map/ppermute | solution.py:412
  8.2 4.9 %states_1.1 = (bf16[512,1536]{1,0:T(8,128)(2,1)S(1)}, bf16[512,1536]{1,0:T(8,128)(2,1)S(1)}, f32[3,2,256,512]{3,2,1,0:T(8,128)S(1)}, f32[3,1,512]{2,1,0:T(1,128)S(1)}) custom-call(bf16[2,32,512]{2,1,0:T(8,128)(2,1)S(1)} %get-tuple-element.46.refs_0_, bf16[2,32,512]{2,1,0:T(8,128)(2,1)S(1)} %get-tuple-element.62.refs_1_.refs_7_, bf16[512,2048]{1,0:T(8,128)(2,1)} %refs_6_.3, ...), custom_call_target="tpu_custom_call" | custom-call | flops 2415919104 | bytes 4718592 | tf_op jit(solution)/shard_map/states_1/pallas_call | solution.py:247
  13.2 1.6 %collective-permute-start.3 = (bf16[256,512]{1,0:T(8,128)(2,1)S(1)}, bf16[256,512]{1,0:T(8,128)(2,1)S(1)}, u32[]{:S(2)}, u32[]{:S(2)}) collective-permute-start(bf16[256,512]{1,0:T(8,128)(2,1)S(1)} %relay_1.3), channel_id=1, source_target_pairs={{0,4},{12,8},{1,5},{13,9},{2,6},{14,10},{3,7},{15,11},{16,20},{28,... | collective-permute-start | bytes 786440 | tf_op jit(solution)/shard_map/ppermute | solution.py:412
  14.9 0.7 %collective-permute-start.1 = (bf16[256,512]{1,0:T(8,128)(2,1)S(1)}, bf16[256,512]{1,0:T(8,128)(2,1)S(1)}, u32[]{:S(2)}, u32[]{:S(2)}) collective-permute-start(bf16[256,512]{1,0:T(8,128)(2,1)S(1)} %relay_1.2), channel_id=1, source_target_pairs={{4,8},{8,4},{5,9},{9,5},{6,10},{10,6},{7,11},{11,7},{20,24},{24,20... | collective-permute-start | bytes 786440 | tf_op jit(solution)/shard_map/ppermute | solution.py:412
  15.6 2.5 %within_0.1 = (f32[512,1024]{1,0:T(8,128)S(1)}, f32[512,256]{1,0:T(8,128)S(1)}, f32[512,256]{1,0:T(8,128)S(1)}) custom-call(bf16[512,512]{1,0:T(8,128)(2,1)S(1)} %get-tuple-element.50.refs_0_.refs_3_, bf16[512,1536]{1,0:T(8,128)(2,1)S(1)} %get-tuple-element.52.refs_1_.refs_3_, bf16[512,512]{1,0:T(8,128)(2,1)S(1)} %get-tuple-element.51.refs_2_.refs_4_, ...), custom_call_target="tpu_custom_call" | custom-call | flops 1610612736 | bytes 5242880 | tf_op jit(solution)/shard_map/within_0/pallas_call | solution.py:284
  18.2 2.2 %collective-permute-done.3.refs_4_.refs_0_ = bf16[256,512]{1,0:T(8,128)(2,1)S(1)} collective-permute-done((bf16[256,512]{1,0:T(8,128)(2,1)S(1)}, bf16[256,512]{1,0:T(8,128)(2,1)S(1)}, u32[]{:S(2)}, u32[]{:S(2)}) %collective-permute-start.3) | collective-permute-done | bytes 262176 | tf_op jit(solution)/shard_map/ppermute | solution.py:412
  20.4 0.7 %collective-permute-start.4 = (bf16[256,512]{1,0:T(8,128)(2,1)S(1)}, bf16[256,512]{1,0:T(8,128)(2,1)S(1)}, u32[]{:S(2)}, u32[]{:S(2)}) collective-permute-start(bf16[256,512]{1,0:T(8,128)(2,1)S(1)} %relay_2.3), channel_id=1, source_target_pairs={{4,8},{8,4},{5,9},{9,5},{6,10},{10,6},{7,11},{11,7},{20,24},{24,20... | collective-permute-start | bytes 786440 | tf_op jit(solution)/shard_map/ppermute | solution.py:412
  21.1 0.1 relay_2.2
  21.2 5.4 %collective-permute-start.2 = (bf16[256,512]{1,0:T(8,128)(2,1)S(1)}, bf16[256,512]{1,0:T(8,128)(2,1)S(1)}, u32[]{:S(2)}, u32[]{:S(2)}) collective-permute-start(bf16[256,512]{1,0:T(8,128)(2,1)S(1)} %relay_2.2), channel_id=1, source_target_pairs={{0,4},{4,0},{8,12},{12,8},{1,5},{5,1},{9,13},{13,9},{2,6},{6,2},{1... | collective-permute-start | bytes 786440 | tf_op jit(solution)/shard_map/ppermute | solution.py:412
  26.6 2.5 %within_1.1 = (f32[512,1024]{1,0:T(8,128)S(1)}, f32[512,256]{1,0:T(8,128)S(1)}, f32[512,256]{1,0:T(8,128)S(1)}) custom-call(bf16[512,512]{1,0:T(8,128)(2,1)S(1)} %get-tuple-element.50.refs_0_.refs_3_, bf16[512,1536]{1,0:T(8,128)(2,1)S(1)} %get-tuple-element.52.refs_1_.refs_3_, bf16[512,512]{1,0:T(8,128)(2,1)S(1)} %get-tuple-element.51.refs_2_.refs_4_, ...), custom_call_target="tpu_custom_call" | custom-call | flops 1610612736 | bytes 5242880 | tf_op jit(solution)/shard_map/within_1/pallas_call | solution.py:284
  29.3 2.9 %collective-permute-start.5 = (bf16[256,512]{1,0:T(8,128)(2,1)S(1)}, bf16[256,512]{1,0:T(8,128)(2,1)S(1)}, u32[]{:S(2)}, u32[]{:S(2)}) collective-permute-start(bf16[256,512]{1,0:T(8,128)(2,1)S(1)} %relay_3.2), channel_id=1, source_target_pairs={{0,4},{4,0},{8,12},{12,8},{1,5},{5,1},{9,13},{13,9},{2,6},{6,2},{1... | collective-permute-start | bytes 786440 | tf_op jit(solution)/shard_map/ppermute | solution.py:412
  32.2 0.3 collective-permute-done.2.refs_2_.refs_4_.refs_0_
  32.6 0.7 %collective-permute-start.8 = (bf16[256,512]{1,0:T(8,128)(2,1)S(1)}, bf16[256,512]{1,0:T(8,128)(2,1)S(1)}, u32[]{:S(2)}, u32[]{:S(2)}) collective-permute-start(bf16[256,512]{1,0:T(8,128)(2,1)S(1)} %relay_3.3), channel_id=1, source_target_pairs={{4,8},{8,4},{5,9},{9,5},{6,10},{10,6},{7,11},{11,7},{20,24},{24,20... | collective-permute-start | bytes 786440 | tf_op jit(solution)/shard_map/ppermute | solution.py:412
  33.2 1.5 %carried_0.1 = (bf16[512,2048]{1,0:T(8,128)(2,1)}, f32[512,256]{1,0:T(8,128)S(1)}, f32[512,256]{1,0:T(8,128)S(1)}) custom-call(bf16[256,512]{1,0:T(8,128)(2,1)S(1)} %collective-permute-done.refs_2_.refs_0_, bf16[256,512]{1,0:T(8,128)(2,1)S(1)} %collective-permute-done.1.refs_4_.refs_1_, bf16[256,512]{1,0:T(8,128)(2,1)S(1)} %collective-permute-done.2.refs_2_.refs_4_.refs_0_, ...), custom_call_target="tpu_custom_call" | custom-call | flops 402653184 | bytes 3670016 | tf_op jit(solution)/shard_map/carried_0/pallas_call | solution.py:355
  34.8 2.6 %collective-permute-done.5.refs_2_.refs_4_.refs_0_ = bf16[256,512]{1,0:T(8,128)(2,1)S(1)} collective-permute-done((bf16[256,512]{1,0:T(8,128)(2,1)S(1)}, bf16[256,512]{1,0:T(8,128)(2,1)S(1)}, u32[]{:S(2)}, u32[]{:S(2)}) %collective-permute-start.5) | collective-permute-done | bytes 262176 | tf_op jit(solution)/shard_map/ppermute | solution.py:412
  37.5 0.7 %collective-permute-start.6 = (bf16[256,512]{1,0:T(8,128)(2,1)S(1)}, bf16[256,512]{1,0:T(8,128)(2,1)S(1)}, u32[]{:S(2)}, u32[]{:S(2)}) collective-permute-start(bf16[256,512]{1,0:T(8,128)(2,1)S(1)} %relay_4.2), channel_id=1, source_target_pairs={{4,8},{8,4},{5,9},{9,5},{6,10},{10,6},{7,11},{11,7},{20,24},{24,20... | collective-permute-start | bytes 786440 | tf_op jit(solution)/shard_map/ppermute | solution.py:412
  38.3 1.3 %collective-permute-start.9 = (bf16[256,512]{1,0:T(8,128)(2,1)S(1)}, bf16[256,512]{1,0:T(8,128)(2,1)S(1)}, u32[]{:S(2)}, u32[]{:S(2)}) collective-permute-start(bf16[256,512]{1,0:T(8,128)(2,1)S(1)} %relay_4.3), channel_id=1, source_target_pairs={{4,0},{8,12},{5,1},{9,13},{6,2},{10,14},{7,3},{11,15},{20,16},{24,... | collective-permute-start | bytes 786440 | tf_op jit(solution)/shard_map/ppermute | solution.py:412
  39.6 1.8 %carried_1.1 = (bf16[512,2048]{1,0:T(8,128)(2,1)}, bf16[512,512]{1,0:T(8,128)(2,1)}, bf16[512,512]{1,0:T(8,128)(2,1)}) custom-call(bf16[256,512]{1,0:T(8,128)(2,1)S(1)} %collective-permute-done.3.refs_4_.refs_0_, bf16[256,512]{1,0:T(8,128)(2,1)S(1)} %collective-permute-done.4.refs_4_.refs_1_, ...), custom_call_target="tpu_custom_call", output_to_operand_aliasing={{0}: (11, {})} | custom-call | flops 402653184 | bytes 3670016 | tf_op jit(solution)/shard_map/carried_1/pallas_call | solution.py:355
  41.5 1.3 %collective-permute-start.7 = (bf16[256,512]{1,0:T(8,128)(2,1)S(1)}, bf16[256,512]{1,0:T(8,128)(2,1)S(1)}, u32[]{:S(2)}, u32[]{:S(2)}) collective-permute-start(bf16[256,512]{1,0:T(8,128)(2,1)S(1)} %relay_5.1), channel_id=1, source_target_pairs={{4,0},{8,12},{5,1},{9,13},{6,2},{10,14},{7,3},{11,15},{20,16},{24,... | collective-permute-start | bytes 786440 | tf_op jit(solution)/shard_map/ppermute | solution.py:412
  42.8 7.2 %collective-permute-done.9.refs_2_ = bf16[256,512]{1,0:T(8,128)(2,1)S(1)} collective-permute-done((bf16[256,512]{1,0:T(8,128)(2,1)S(1)}, bf16[256,512]{1,0:T(8,128)(2,1)S(1)}, u32[]{:S(2)}, u32[]{:S(2)}) %collective-permute-start.9) | collective-permute-done | bytes 262176 | tf_op jit(solution)/shard_map/ppermute | solution.py:412
  50.0 1.5 %carried_2.1 = (bf16[512,2048]{1,0:T(8,128)(2,1)}, f32[512,256]{1,0:T(8,128)S(1)}, f32[512,256]{1,0:T(8,128)S(1)}) custom-call(bf16[256,512]{1,0:T(8,128)(2,1)S(1)} %collective-permute-done.2.refs_2_.refs_4_.refs_0_, bf16[256,512]{1,0:T(8,128)(2,1)S(1)} %collective-permute-done.8.refs_4_.refs_1_, ...), custom_call_target="tpu_custom_call", output_to_operand_aliasing={{0}: (11, {})} | custom-call | flops 402653184 | bytes 3670016 | tf_op jit(solution)/shard_map/carried_2/pallas_call | solution.py:355
  51.5 3.3 %collective-permute-done.7.refs_2_ = bf16[256,512]{1,0:T(8,128)(2,1)S(1)} collective-permute-done((bf16[256,512]{1,0:T(8,128)(2,1)S(1)}, bf16[256,512]{1,0:T(8,128)(2,1)S(1)}, u32[]{:S(2)}, u32[]{:S(2)}) %collective-permute-start.7) | collective-permute-done | bytes 262176 | tf_op jit(solution)/shard_map/ppermute | solution.py:412
  54.8 1.8 %carried_3.1 = (bf16[512,2048]{1,0:T(8,128)(2,1)}, bf16[512,512]{1,0:T(8,128)(2,1)}, bf16[512,512]{1,0:T(8,128)(2,1)}) custom-call(bf16[256,512]{1,0:T(8,128)(2,1)S(1)} %collective-permute-done.5.refs_2_.refs_4_.refs_0_, bf16[256,512]{1,0:T(8,128)(2,1)S(1)} %collective-permute-done.6.refs_4_.refs_1_, ...), custom_call_target="tpu_custom_call", output_to_operand_aliasing={{0}: (11, {}), {1}: (12, {}), {2}: (13, {})} | custom-call | flops 402653184 | bytes 3670016 | tf_op jit(solution)/shard_map/carried_3/pallas_call | solution.py:355
  (21 shorter events, 0.8 us)
Async XLA Ops:
  3.3 11.6 %collective-permute-start = (bf16[256,512]{1,0:T(8,128)(2,1)S(1)}, bf16[256,512]{1,0:T(8,128)(2,1)S(1)}, u32[]{:S(2)}, u32[]{:S(2)}) collective-permute-start(bf16[256,512]{1,0:T(8,128)(2,1)S(1)} %get-tuple-element.43), channel_id=1, source_target_pairs={{0,4},{12,8},{1,5},{13,9},{2,6},{14,10},{3,7},{15,11},{16,20},{28,... | collective-permute-start | bytes 786440 | tf_op jit(solution)/shard_map/ppermute | solution.py:412
  13.1 2.5 %copy-start = (bf16[512,512]{1,0:T(8,128)(2,1)S(1)}, bf16[512,512]{1,0:T(8,128)(2,1)}, u32[]{:S(2)}) copy-start(bf16[512,512]{1,0:T(8,128)(2,1)} %refs_5_.15) | copy-start | bytes 1572868
  13.1 2.5 %copy-start.1 = (bf16[512,2048]{1,0:T(8,128)(2,1)S(1)}, bf16[512,2048]{1,0:T(8,128)(2,1)}, u32[]{:S(2)}) copy-start(bf16[512,2048]{1,0:T(8,128)(2,1)} %refs_6_.3) | copy-start | bytes 6291460
  13.2 2.5 %copy-start.2 = (bf16[512,512]{1,0:T(8,128)(2,1)S(1)}, bf16[512,512]{1,0:T(8,128)(2,1)}, u32[]{:S(2)}) copy-start(bf16[512,512]{1,0:T(8,128)(2,1)} %refs_5_.12) | copy-start | bytes 1572868
  13.2 2.5 %copy-start.3 = (f32[32]{0:T(128)S(1)}, f32[32]{0:T(128)}, u32[]{:S(2)}) copy-start(f32[32]{0:T(128)} %param.13) | copy-start | bytes 388
  13.2 7.1 %collective-permute-start.3 = (bf16[256,512]{1,0:T(8,128)(2,1)S(1)}, bf16[256,512]{1,0:T(8,128)(2,1)S(1)}, u32[]{:S(2)}, u32[]{:S(2)}) collective-permute-start(bf16[256,512]{1,0:T(8,128)(2,1)S(1)} %relay_1.3), channel_id=1, source_target_pairs={{0,4},{12,8},{1,5},{13,9},{2,6},{14,10},{3,7},{15,11},{16,20},{28,... | collective-permute-start | bytes 786440 | tf_op jit(solution)/shard_map/ppermute | solution.py:412
  14.9 6.2 %collective-permute-start.1 = (bf16[256,512]{1,0:T(8,128)(2,1)S(1)}, bf16[256,512]{1,0:T(8,128)(2,1)S(1)}, u32[]{:S(2)}, u32[]{:S(2)}) collective-permute-start(bf16[256,512]{1,0:T(8,128)(2,1)S(1)} %relay_1.2), channel_id=1, source_target_pairs={{4,8},{8,4},{5,9},{9,5},{6,10},{10,6},{7,11},{11,7},{20,24},{24,20... | collective-permute-start | bytes 786440 | tf_op jit(solution)/shard_map/ppermute | solution.py:412
  20.4 8.7 %collective-permute-start.4 = (bf16[256,512]{1,0:T(8,128)(2,1)S(1)}, bf16[256,512]{1,0:T(8,128)(2,1)S(1)}, u32[]{:S(2)}, u32[]{:S(2)}) collective-permute-start(bf16[256,512]{1,0:T(8,128)(2,1)S(1)} %relay_2.3), channel_id=1, source_target_pairs={{4,8},{8,4},{5,9},{9,5},{6,10},{10,6},{7,11},{11,7},{20,24},{24,20... | collective-permute-start | bytes 786440 | tf_op jit(solution)/shard_map/ppermute | solution.py:412
  21.2 11.2 %collective-permute-start.2 = (bf16[256,512]{1,0:T(8,128)(2,1)S(1)}, bf16[256,512]{1,0:T(8,128)(2,1)S(1)}, u32[]{:S(2)}, u32[]{:S(2)}) collective-permute-start(bf16[256,512]{1,0:T(8,128)(2,1)S(1)} %relay_2.2), channel_id=1, source_target_pairs={{0,4},{4,0},{8,12},{12,8},{1,5},{5,1},{9,13},{13,9},{2,6},{6,2},{1... | collective-permute-start | bytes 786440 | tf_op jit(solution)/shard_map/ppermute | solution.py:412
  29.3 8.1 %collective-permute-start.5 = (bf16[256,512]{1,0:T(8,128)(2,1)S(1)}, bf16[256,512]{1,0:T(8,128)(2,1)S(1)}, u32[]{:S(2)}, u32[]{:S(2)}) collective-permute-start(bf16[256,512]{1,0:T(8,128)(2,1)S(1)} %relay_3.2), channel_id=1, source_target_pairs={{0,4},{4,0},{8,12},{12,8},{1,5},{5,1},{9,13},{13,9},{2,6},{6,2},{1... | collective-permute-start | bytes 786440 | tf_op jit(solution)/shard_map/ppermute | solution.py:412
  32.6 5.6 %collective-permute-start.8 = (bf16[256,512]{1,0:T(8,128)(2,1)S(1)}, bf16[256,512]{1,0:T(8,128)(2,1)S(1)}, u32[]{:S(2)}, u32[]{:S(2)}) collective-permute-start(bf16[256,512]{1,0:T(8,128)(2,1)S(1)} %relay_3.3), channel_id=1, source_target_pairs={{4,8},{8,4},{5,9},{9,5},{6,10},{10,6},{7,11},{11,7},{20,24},{24,20... | collective-permute-start | bytes 786440 | tf_op jit(solution)/shard_map/ppermute | solution.py:412
  37.5 3.9 %collective-permute-start.6 = (bf16[256,512]{1,0:T(8,128)(2,1)S(1)}, bf16[256,512]{1,0:T(8,128)(2,1)S(1)}, u32[]{:S(2)}, u32[]{:S(2)}) collective-permute-start(bf16[256,512]{1,0:T(8,128)(2,1)S(1)} %relay_4.2), channel_id=1, source_target_pairs={{4,8},{8,4},{5,9},{9,5},{6,10},{10,6},{7,11},{11,7},{20,24},{24,20... | collective-permute-start | bytes 786440 | tf_op jit(solution)/shard_map/ppermute | solution.py:412
  38.3 11.7 %collective-permute-start.9 = (bf16[256,512]{1,0:T(8,128)(2,1)S(1)}, bf16[256,512]{1,0:T(8,128)(2,1)S(1)}, u32[]{:S(2)}, u32[]{:S(2)}) collective-permute-start(bf16[256,512]{1,0:T(8,128)(2,1)S(1)} %relay_4.3), channel_id=1, source_target_pairs={{4,0},{8,12},{5,1},{9,13},{6,2},{10,14},{7,3},{11,15},{20,16},{24,... | collective-permute-start | bytes 786440 | tf_op jit(solution)/shard_map/ppermute | solution.py:412
  41.5 13.3 %collective-permute-start.7 = (bf16[256,512]{1,0:T(8,128)(2,1)S(1)}, bf16[256,512]{1,0:T(8,128)(2,1)S(1)}, u32[]{:S(2)}, u32[]{:S(2)}) collective-permute-start(bf16[256,512]{1,0:T(8,128)(2,1)S(1)} %relay_5.1), channel_id=1, source_target_pairs={{4,0},{8,12},{5,1},{9,13},{6,2},{10,14},{7,3},{11,15},{20,16},{24,... | collective-permute-start | bytes 786440 | tf_op jit(solution)/shard_map/ppermute | solution.py:412

commit v4 on v3

--- a/solution.py
+++ b/solution.py
@@ -64,11 +64,53 @@
     return forward, jnp.where(forward, rank, ranks - 1 - rank)
 
 
-def local_kernel(*refs, first, last, per_group, ranks):
+def upper_ones(tokens):
+    rows = lax.broadcasted_iota(jnp.int32, (tokens, tokens), 0)
+    cols = lax.broadcasted_iota(jnp.int32, (tokens, tokens), 1)
+    return (rows <= cols).astype(F32).astype(BF16)
+
+
+def first_kernel(step_hbm, rate_hbm, dy, x, b, c, send, step, rate, rows_in, group_in, sems, *, ranks):
+    rank = lax.axis_index("ctx")
+
+    def fetch(source, target, place):
+        if source.shape != target.shape:
+            source = source.at[:, pl.ds(0, target.shape[1])]
+        copy = pltpu.make_async_copy(source, target, sems.at[place])
+        copy.start()
+        return copy
+
+    def state(wide, narrow, weigh):
+        copies = [
+            fetch(step_hbm, step, 0),
+            fetch(rate_hbm, rate, 1),
+            fetch(wide, rows_in, 2),
+            fetch(narrow, group_in, 3),
+        ]
+        upper = upper_ones(step.shape[1])
+        copies[0].wait()
+        copies[1].wait()
+        cum = dot(step[...], upper, 1, 0) * columns(rate[...])
+        spread = head_spread(terms(weigh(cum), 2), 0)
+        copies[2].wait()
+        rows = (spread * rows_in[...].astype(F32)).astype(BF16)
+        copies[3].wait()
+        send[...] = dot(group_in[...], rows, 0, 0).astype(BF16)
+
+    @pl.when(rank == 0)
+    def _():
+        state(x, b, lambda cum: jnp.exp(cum[:, -1:] - cum) * step[...].astype(F32))
+
+    @pl.when(rank == ranks - 1)
+    def _():
+        state(dy, c, jnp.exp)
+
+
+def local_kernel(*refs, first, last, per_group):
     if first == 0:
         step_hbm, rate_hbm, dy, x, b, c = refs[:6]
-        dyw, xw, states, decay, wd, wx, send = refs[6:13]
-        step, rate, dy_in, x_in, b_in, c_in, sems = refs[13:]
+        dyw, xw, states, decay, wd, wx = refs[6:12]
+        step, rate, dy_in, x_in, b_in, c_in, sems = refs[12:]
     else:
         wd, wx, dy, x, b, c = refs[:6]
         dyw, xw, states, decay = refs[6:10]
@@ -93,9 +135,7 @@
         part(b, b_in, low_group * N, 3),
     ]
     if first == 0:
-        rows = lax.broadcasted_iota(jnp.int32, (tokens, tokens), 0)
-        cols = lax.broadcasted_iota(jnp.int32, (tokens, tokens), 1)
-        upper = (rows <= cols).astype(F32).astype(BF16)
+        upper = upper_ones(tokens)
         for copy in small:
             copy.wait()
         cum = dot(step[...], upper, 1, 0) * columns(rate[...])
@@ -115,9 +155,6 @@
         xw[:, span] = (spread * x_in[:, span].astype(F32)).astype(BF16)
         states[place, 1] = dot(c_in[:, group], dyw[:, span], 0, 0)
         states[place, 0] = dot(b_in[:, group], xw[:, span], 0, 0) * end
-    if first == 0:
-        forward, _ = heading(True, ranks)
-        send[...] = states[0, jnp.where(forward, 0, 1)].astype(BF16)
 
 
 def piece(refs, chunk, starts):
@@ -128,7 +165,7 @@
 def within_kernel(*refs, group, per_group, starts):
     count = len(starts)
     dyw, xw, refs = refs[:count], refs[count : 2 * count], refs[2 * count :]
-    b, c, dy, wx, gain, grad_x, grad_b, grad_c = refs
+    b, c, dy, wx, gain, grad_x, grad_b, grad_c, spread_out = refs
     lower = lower_mask(b.shape[0])
     own = pl.ds(group * N, N)
     chunks = range(group * per_group, (group + 1) * per_group)
@@ -144,6 +181,7 @@
         spread = head_spread((wx[0], wx[1]), chunk)
         rows = dy[:, pl.ds(chunk * CHUNK, CHUNK)].astype(F32)
         skip = head_spread(gains, chunk)[0:1, :] * rows
+        spread_out[:, pl.ds(part * CHUNK, CHUNK)] = spread
         grad_x[:, pl.ds(part * CHUNK, CHUNK)] = (
             spread * dot(scores, piece(dyw, chunk, starts), 0, 0) + skip
         )
@@ -181,7 +219,7 @@
     fwd_in = chosen(refs[: ranks - 1], rank - 1)
     back_in = chosen(refs[: ranks - 1], ranks - 2 - rank)
     refs = refs[ranks - 1 :]
-    dyw, xw, b, decay, wx, part_x, part_b, part_c = refs[:8]
+    dyw, xw, b, decay, spread, part_x, part_b, part_c = refs[:8]
     group, inside = chunk // per_group, chunk % per_group
     grad_x, grad_b, grad_c = refs[-7 if last else -5 :][:3]
     x_out = refs[-4] if last else refs[-2]
@@ -196,9 +234,9 @@
         copies[-1].start()
 
     back = (back_in.astype(F32) * decay[place]).astype(BF16)
-    spread = head_spread((wx[0], wx[1]), chunk)
-    carried = spread * dot(b[:, own], back, 1, 0)
-    x_out[...] = (part_x[:, pl.ds(inside * CHUNK, CHUNK)] + carried).astype(BF16)
+    part = pl.ds(inside * CHUNK, CHUNK)
+    carried = spread[:, part] * dot(b[:, own], back, 1, 0)
+    x_out[...] = (part_x[:, part] + carried).astype(BF16)
     send(x_out, grad_x.at[:, pl.ds(chunk * CHUNK, CHUNK)], 0)
     total_b = part_b[...] + dot(xw[:, span], back, 1, 1)
     if last:
@@ -232,7 +270,7 @@
     gain_row = skip_gain.reshape(1, head_count)
     stay = partial(pltpu.with_memory_space_constraint, memory_space=pltpu.HBM)
     sources = [stay(array) for array in (grad_out, saved_x, saved_b, saved_c)]
-    starts = [start for start in (0, 1) if start < chunks]
+    starts = [start for start in (0, 2) if start < chunks]
     stops = starts[1:] + [chunks]
 
     def local_states(first, last, inputs, in_spec, extra_shapes, extra_scratch):
@@ -245,7 +283,7 @@
         ] + extra_shapes
         tall = ((last - 1) // per_group - first // per_group + 1) * N
         return pl.pallas_call(
-            partial(local_kernel, first=first, last=last, per_group=per_group, ranks=ranks),
+            partial(local_kernel, first=first, last=last, per_group=per_group),
             in_specs=[in_spec] * 2 + [ANYWHERE] * 4,
             out_specs=[IN_VMEM] * len(out_shape),
             out_shape=out_shape,
@@ -262,13 +300,34 @@
             name=f"states_{first}",
         )(*inputs)
 
-    *head, wd, wx, first_send = local_states(
+    small_scratch = [
+        pltpu.VMEM((head_count, tokens), BF16),
+        pltpu.VMEM((1, head_count), F32),
+    ]
+    step_rows, rate_row = step_size.T, decay_rate.reshape(1, head_count)
+    first_send = pl.pallas_call(
+        partial(first_kernel, ranks=ranks),
+        in_specs=[ANYWHERE] * 6,
+        out_specs=IN_VMEM,
+        out_shape=pltpu.VMEM((N, CHUNK), BF16),
+        scratch_shapes=small_scratch
+        + [
+            pltpu.VMEM((tokens, CHUNK), BF16),
+            pltpu.VMEM((tokens, N), BF16),
+            pltpu.SemaphoreType.DMA((4,)),
+        ],
+        compiler_params=PARAMS,
+        cost_estimate=cost(2 * tokens * CHUNK * (N + 256), 4 * tokens * CHUNK),
+        name="first_state",
+    )(stay(step_rows), stay(rate_row), *sources)
+    rate_row, _ = lax.optimization_barrier((rate_row, first_send))
+    *head, wd, wx = local_states(
         0,
         stops[0],
-        [stay(step_size.T), stay(decay_rate.reshape(1, head_count))] + sources,
+        [stay(step_rows), stay(rate_row)] + sources,
         ANYWHERE,
-        [pltpu.VMEM((2, head_count, tokens), BF16)] * 2 + [pltpu.VMEM((N, CHUNK), BF16)],
-        [pltpu.VMEM((head_count, tokens), BF16), pltpu.VMEM((1, head_count), F32)],
+        [pltpu.VMEM((2, head_count, tokens), BF16)] * 2,
+        small_scratch,
     )
     pieces = [head]
 
@@ -284,11 +343,12 @@
         return pl.pallas_call(
             partial(within_kernel, group=group, per_group=per_group, starts=starts),
             in_specs=[IN_VMEM] * (2 * len(starts) + 5),
-            out_specs=[IN_VMEM] * 3,
+            out_specs=[IN_VMEM] * 4,
             out_shape=[
                 pltpu.VMEM((tokens, group_width), F32),
                 pltpu.VMEM((tokens, N), F32),
                 pltpu.VMEM((tokens, N), F32),
+                pltpu.VMEM((tokens, group_width), F32),
             ],
             compiler_params=PARAMS,
             cost_estimate=cost(
@@ -329,7 +389,7 @@
             *got,
         )
 
-    def carried(chunk, candidates, part_x, part_b, part_c, grads):
+    def carried(chunk, candidates, spread, part_x, part_b, part_c, grads):
         place = max(i for i, start in enumerate(starts) if start <= chunk)
         own = pieces[place]
         last = chunk % per_group == per_group - 1
@@ -343,7 +403,7 @@
         else:
             out_shape += [pltpu.VMEM((tokens, N), F32)] * 2
             out_specs += [IN_VMEM] * 2
-        inputs = [*candidates, own[0], own[1], saved_b, own[3], wx, part_x, part_b, part_c]
+        inputs = [*candidates, own[0], own[1], saved_b, own[3], spread, part_x, part_b, part_c]
         aliases = {}
         if grads[0] is not None:
             aliases[len(inputs)] = 0
@@ -398,15 +458,13 @@
         nonlocal sums, grads
         chunk = chunks_left.pop(0)
         candidates = [got[chunk + hop, hop % 2 == 0] for hop in range(ranks - 1)]
-        part_x, part_b, part_c = parts[chunk // per_group]
+        part_x, part_b, part_c, spread = parts[chunk // per_group]
         if chunk % per_group > 0:
             part_b, part_c = sums
-        sums, grads = carried(chunk, candidates, part_x, part_b, part_c, grads)
+        sums, grads = carried(chunk, candidates, spread, part_x, part_b, part_c, grads)
 
     for position, (turn, even_links) in enumerate(order):
         before = got.get((turn - 1, not even_links))
-        if position == 1 and len(pieces) < len(starts):
-            more_states(wd)
         send = first_send if position == 0 else relay(turn, even_links, before)
         key = (turn, even_links)
         got[key] = lax.ppermute(send, "ctx", links(turn, even_links))
@@ -419,13 +477,15 @@
                     (pieces[-1], got[following])
                 )
         elif position % 2 == 0 and position > 0:
-            if groups_left:
-                group = groups_left.pop(0)
-                parts[group] = within(group, lax.optimization_barrier((wx, before))[0])
-                parts[group], got[following] = lax.optimization_barrier(
-                    (parts[group], got[following])
-                )
-            elif chunks_left and (chunks_left[0] + ranks - 2, True) in ready:
+            if groups_left and position >= min(4, len(order) - 2):
+                held = lax.optimization_barrier((wx, before))[0]
+                while groups_left:
+                    group = groups_left.pop(0)
+                    parts[group] = within(group, held)
+                    parts[group], got[following] = lax.optimization_barrier(
+                        (parts[group], got[following])
+                    )
+            elif not groups_left and (chunks_left[0] + ranks - 2, True) in ready:
                 carry()
                 grads[0], got[following] = lax.optimization_barrier((grads[0], got[following]))
     while groups_left:

time: 56.9 us -> 54.3 us (0.954)
  starting transfers between devices: 20 us -> 17 us
  Pallas kernels: 20 us -> 20.9 us
    ppermute x10, starting transfers between devices: 20 us -> 17 us  [on_device(): got[key] = lax.ppermute(send, 'ctx', links(turn, even_links))]
    pallas_call x0 -> x1, Pallas kernels: none -> 2.04 us  [on_device(): pl.pallas_call(partial(first_kernel, ranks=ranks), in_specs=[ANYWHERE] *...]
    pallas_call x4, Pallas kernels: 6.51 us -> 5.74 us  [carried(): pl.pallas_call(partial(carried_kernel, chunk=chunk, per_group=per_group,...]
  transfers between devices with their start and end apart: 10 -> 10, of which waited for: 5 -> 4; matrix products, arithmetic and copies ran while one was open for 0% -> 0% of each run, Pallas kernels for 28% -> 32%
where the time goes in v4:
time: 54.3 us; the launch traced here: 54 us
  Pallas kernels  20.9 us (38%)
  starting transfers between devices  17 us (31%)
  waiting for transfers between devices  15.2 us (28%)
  between operations  0.87 us (2%)
    ppermute x10, starting transfers between devices, on_device(): got[key] = lax.ppermute(send, 'ctx', links(turn, even_links))  17 us
    ppermute x10, waiting for transfers between devices, on_device(): got[key] = lax.ppermute(send, 'ctx', links(turn, even_links))  15.2 us
    pallas_call x2, Pallas kernels, local_states(): pl.pallas_call(partial(local_kernel, first=first, last=last, per_group=pe...  7.2 us
    pallas_call x4, Pallas kernels, carried(): pl.pallas_call(partial(carried_kernel, chunk=chunk, per_group=per_group,...  5.74 us
    pallas_call x2, Pallas kernels, within(): pl.pallas_call(partial(within_kernel, group=group, per_group=per_group, s...  5.12 us
    pallas_call x1, Pallas kernels, on_device(): pl.pallas_call(partial(first_kernel, ranks=ranks), in_specs=[ANYWHERE] *...  2.04 us
  transfers between devices with their start and end apart: 10, of which 4 were waited for; matrix products, arithmetic and copies ran while one was open for 0% of the time, Pallas kernels for 32%

profile of v4, /device:TPU:0, one launch (start us, length us, event | category | flops | bytes accessed | tf_op | source)
XLA Modules:
  0.0 54.0 jit_solution(653155385098097445)
XLA Ops:
  0.6 2.0 %first_state.1 = bf16[256,512]{1,0:T(8,128)(2,1)S(1)} custom-call(bf16[32,512]{1,0:T(8,128)(2,1)} %bitcast.5, f32[1,32]{1,0:T(1,128)} %bitcast.7, bf16[512,2048]{1,0:T(8,128)(2,1)} %refs_6_.3, bf16[512,2048]{1,0:T(8,128)(2,1)} %refs_3_.3, bf16[512,512]{1,0:T(8,128)(2,1)} %refs_5_.15, bf16[512,512]{1,0:T(8,128)(2,1)} %refs_5_.12), custom_call_target="tpu_custom_call" | custom-call | flops 268435456 | bytes 1048576 | tf_op jit(solution)/shard_map/first_state/pallas_call | solution.py:308
  2.7 3.0 %collective-permute-start = (bf16[256,512]{1,0:T(8,128)(2,1)S(1)}, bf16[256,512]{1,0:T(8,128)(2,1)S(1)}, u32[]{:S(2)}, u32[]{:S(2)}) collective-permute-start(bf16[256,512]{1,0:T(8,128)(2,1)S(1)} %first_state.1), channel_id=1, source_target_pairs={{0,4},{12,8},{1,5},{13,9},{2,6},{14,10},{3,7},{15,11},{16,20},{28,... | collective-permute-start | bytes 786440 | tf_op jit(solution)/shard_map/ppermute | solution.py:470
  5.6 3.6 %states_0.1 = (bf16[512,1024]{1,0:T(8,128)(2,1)S(1)}, bf16[512,1024]{1,0:T(8,128)(2,1)S(1)}, f32[2,2,256,512]{3,2,1,0:T(8,128)S(1)}, f32[2,1,512]{2,1,0:T(1,128)...) custom-call(bf16[32,512]{1,0:T(8,128)(2,1)} %bitcast.6, f32[1,32]{1,0:T(1,128)} %bitcast.8, ...), custom_call_target="tpu_custom_call" | custom-call | flops 1610612736 | bytes 3145728 | tf_op jit(solution)/shard_map/states_0/pallas_call | solution.py:285
  9.3 1.3 %collective-permute-start.3 = (bf16[256,512]{1,0:T(8,128)(2,1)S(1)}, bf16[256,512]{1,0:T(8,128)(2,1)S(1)}, u32[]{:S(2)}, u32[]{:S(2)}) collective-permute-start(bf16[256,512]{1,0:T(8,128)(2,1)S(1)} %relay_1.2), channel_id=1, source_target_pairs={{0,4},{12,8},{1,5},{13,9},{2,6},{14,10},{3,7},{15,11},{16,20},{28,... | collective-permute-start | bytes 786440 | tf_op jit(solution)/shard_map/ppermute | solution.py:470
  10.6 3.6 %states_2.1 = (bf16[512,1024]{1,0:T(8,128)(2,1)S(1)}, bf16[512,1024]{1,0:T(8,128)(2,1)S(1)}, f32[2,2,256,512]{3,2,1,0:T(8,128)S(1)}, f32[2,1,512]{2,1,0:T(1,128)S(1)}) custom-call(bf16[2,32,512]{2,1,0:T(8,128)(2,1)S(1)} %get-tuple-element.56.refs_0_, bf16[2,32,512]{2,1,0:T(8,128)(2,1)S(1)} %get-tuple-element.69.refs_1_.refs_7_, bf16[512,2048]{1,0:T(8,128)(2,1)} %refs_6_.3, ...), custom_call_target="tpu_custom_call" | custom-call | flops 1610612736 | bytes 3145728 | tf_op jit(solution)/shard_map/states_2/pallas_call | solution.py:285
  14.3 0.7 %collective-permute-start.1 = (bf16[256,512]{1,0:T(8,128)(2,1)S(1)}, bf16[256,512]{1,0:T(8,128)(2,1)S(1)}, u32[]{:S(2)}, u32[]{:S(2)}) collective-permute-start(bf16[256,512]{1,0:T(8,128)(2,1)S(1)} %relay_1.3), channel_id=1, source_target_pairs={{4,8},{8,4},{5,9},{9,5},{6,10},{10,6},{7,11},{11,7},{20,24},{24,20... | collective-permute-start | bytes 786440 | tf_op jit(solution)/shard_map/ppermute | solution.py:470
  15.0 1.8 %collective-permute-done.3.refs_2_.refs_0_ = bf16[256,512]{1,0:T(8,128)(2,1)S(1)} collective-permute-done((bf16[256,512]{1,0:T(8,128)(2,1)S(1)}, bf16[256,512]{1,0:T(8,128)(2,1)S(1)}, u32[]{:S(2)}, u32[]{:S(2)}) %collective-permute-start.3) | collective-permute-done | bytes 262176 | tf_op jit(solution)/shard_map/ppermute | solution.py:470
  16.9 0.8 %collective-permute-start.4 = (bf16[256,512]{1,0:T(8,128)(2,1)S(1)}, bf16[256,512]{1,0:T(8,128)(2,1)S(1)}, u32[]{:S(2)}, u32[]{:S(2)}) collective-permute-start(bf16[256,512]{1,0:T(8,128)(2,1)S(1)} %relay_2.3), channel_id=1, source_target_pairs={{4,8},{8,4},{5,9},{9,5},{6,10},{10,6},{7,11},{11,7},{20,24},{24,20... | collective-permute-start | bytes 786440 | tf_op jit(solution)/shard_map/ppermute | solution.py:470
  17.8 0.1 relay_2.2
  17.9 6.6 %collective-permute-start.2 = (bf16[256,512]{1,0:T(8,128)(2,1)S(1)}, bf16[256,512]{1,0:T(8,128)(2,1)S(1)}, u32[]{:S(2)}, u32[]{:S(2)}) collective-permute-start(bf16[256,512]{1,0:T(8,128)(2,1)S(1)} %relay_2.2), channel_id=1, source_target_pairs={{0,4},{4,0},{8,12},{12,8},{1,5},{5,1},{9,13},{13,9},{2,6},{6,2},{1... | collective-permute-start | bytes 786440 | tf_op jit(solution)/shard_map/ppermute | solution.py:470
  24.5 2.6 %within_0.1 = (f32[512,1024]{1,0:T(8,128)S(1)}, f32[512,256]{1,0:T(8,128)S(1)}, f32[512,256]{1,0:T(8,128)S(1)}, f32[512,1024]{1,0:T(8,128)S(1)}) custom-call(bf16[512,1024]{1,0:T(8,128)(2,1)S(1)} %get-tuple-element.65.refs_0_.refs_3_, bf16[512,1024]{1,0:T(8,128)(2,1)S(1)} %get-tuple-element.67.refs_1_.refs_3_, ...), custom_call_target="tpu_custom_call" | custom-call | flops 1610612736 | bytes 5242880 | tf_op jit(solution)/shard_map/within_0/pallas_call | solution.py:343
  27.0 2.6 %within_1.1 = (f32[512,1024]{1,0:T(8,128)S(1)}, f32[512,256]{1,0:T(8,128)S(1)}, f32[512,256]{1,0:T(8,128)S(1)}, f32[512,1024]{1,0:T(8,128)S(1)}) custom-call(bf16[512,1024]{1,0:T(8,128)(2,1)S(1)} %get-tuple-element.65.refs_0_.refs_3_, bf16[512,1024]{1,0:T(8,128)(2,1)S(1)} %get-tuple-element.67.refs_1_.refs_3_, ...), custom_call_target="tpu_custom_call" | custom-call | flops 1610612736 | bytes 5242880 | tf_op jit(solution)/shard_map/within_1/pallas_call | solution.py:343
  29.7 0.7 %collective-permute-start.5 = (bf16[256,512]{1,0:T(8,128)(2,1)S(1)}, bf16[256,512]{1,0:T(8,128)(2,1)S(1)}, u32[]{:S(2)}, u32[]{:S(2)}) collective-permute-start(bf16[256,512]{1,0:T(8,128)(2,1)S(1)} %relay_3.2), channel_id=1, source_target_pairs={{0,4},{4,0},{8,12},{12,8},{1,5},{5,1},{9,13},{13,9},{2,6},{6,2},{1... | collective-permute-start | bytes 786440 | tf_op jit(solution)/shard_map/ppermute | solution.py:470
  30.6 0.7 %collective-permute-start.8 = (bf16[256,512]{1,0:T(8,128)(2,1)S(1)}, bf16[256,512]{1,0:T(8,128)(2,1)S(1)}, u32[]{:S(2)}, u32[]{:S(2)}) collective-permute-start(bf16[256,512]{1,0:T(8,128)(2,1)S(1)} %relay_3.3), channel_id=1, source_target_pairs={{4,8},{8,4},{5,9},{9,5},{6,10},{10,6},{7,11},{11,7},{20,24},{24,20... | collective-permute-start | bytes 786440 | tf_op jit(solution)/shard_map/ppermute | solution.py:470
  31.2 1.4 %carried_0.1 = (bf16[512,2048]{1,0:T(8,128)(2,1)}, f32[512,256]{1,0:T(8,128)S(1)}, f32[512,256]{1,0:T(8,128)S(1)}) custom-call(bf16[256,512]{1,0:T(8,128)(2,1)S(1)} %collective-permute-done.refs_2_.refs_0_, bf16[256,512]{1,0:T(8,128)(2,1)S(1)} %collective-permute-done.1.refs_4_.refs_1_, bf16[256,512]{1,0:T(8,128)(2,1)S(1)} %collective-permute-done.2.refs_2_.refs_4_.refs_0_, ...), custom_call_target="tpu_custom_call" | custom-call | flops 402653184 | bytes 3670016 | tf_op jit(solution)/shard_map/carried_0/pallas_call | solution.py:415
  32.6 4.4 %collective-permute-done.5.refs_2_.refs_4_.refs_0_ = bf16[256,512]{1,0:T(8,128)(2,1)S(1)} collective-permute-done((bf16[256,512]{1,0:T(8,128)(2,1)S(1)}, bf16[256,512]{1,0:T(8,128)(2,1)S(1)}, u32[]{:S(2)}, u32[]{:S(2)}) %collective-permute-start.5) | collective-permute-done | bytes 262176 | tf_op jit(solution)/shard_map/ppermute | solution.py:470
  37.1 0.7 %collective-permute-start.6 = (bf16[256,512]{1,0:T(8,128)(2,1)S(1)}, bf16[256,512]{1,0:T(8,128)(2,1)S(1)}, u32[]{:S(2)}, u32[]{:S(2)}) collective-permute-start(bf16[256,512]{1,0:T(8,128)(2,1)S(1)} %relay_4.2), channel_id=1, source_target_pairs={{4,8},{8,4},{5,9},{9,5},{6,10},{10,6},{7,11},{11,7},{20,24},{24,20... | collective-permute-start | bytes 786440 | tf_op jit(solution)/shard_map/ppermute | solution.py:470
  37.9 1.3 %collective-permute-start.9 = (bf16[256,512]{1,0:T(8,128)(2,1)S(1)}, bf16[256,512]{1,0:T(8,128)(2,1)S(1)}, u32[]{:S(2)}, u32[]{:S(2)}) collective-permute-start(bf16[256,512]{1,0:T(8,128)(2,1)S(1)} %relay_4.3), channel_id=1, source_target_pairs={{4,0},{8,12},{5,1},{9,13},{6,2},{10,14},{7,3},{11,15},{20,16},{24,... | collective-permute-start | bytes 786440 | tf_op jit(solution)/shard_map/ppermute | solution.py:470
  39.2 1.5 %carried_1.1 = (bf16[512,2048]{1,0:T(8,128)(2,1)}, bf16[512,512]{1,0:T(8,128)(2,1)}, bf16[512,512]{1,0:T(8,128)(2,1)}) custom-call(bf16[256,512]{1,0:T(8,128)(2,1)S(1)} %collective-permute-done.3.refs_2_.refs_0_, bf16[256,512]{1,0:T(8,128)(2,1)S(1)} %collective-permute-done.4.refs_4_.refs_1_, ...), custom_call_target="tpu_custom_call", output_to_operand_aliasing={{0}: (11, {})} | custom-call | flops 402653184 | bytes 3670016 | tf_op jit(solution)/shard_map/carried_1/pallas_call | solution.py:415
  40.9 1.3 %collective-permute-start.7 = (bf16[256,512]{1,0:T(8,128)(2,1)S(1)}, bf16[256,512]{1,0:T(8,128)(2,1)S(1)}, u32[]{:S(2)}, u32[]{:S(2)}) collective-permute-start(bf16[256,512]{1,0:T(8,128)(2,1)S(1)} %relay_5.1), channel_id=1, source_target_pairs={{4,0},{8,12},{5,1},{9,13},{6,2},{10,14},{7,3},{11,15},{20,16},{24,... | collective-permute-start | bytes 786440 | tf_op jit(solution)/shard_map/ppermute | solution.py:470
  42.2 5.4 %collective-permute-done.9.refs_2_ = bf16[256,512]{1,0:T(8,128)(2,1)S(1)} collective-permute-done((bf16[256,512]{1,0:T(8,128)(2,1)S(1)}, bf16[256,512]{1,0:T(8,128)(2,1)S(1)}, u32[]{:S(2)}, u32[]{:S(2)}) %collective-permute-start.9) | collective-permute-done | bytes 262176 | tf_op jit(solution)/shard_map/ppermute | solution.py:470
  47.5 1.3 %carried_2.1 = (bf16[512,2048]{1,0:T(8,128)(2,1)}, f32[512,256]{1,0:T(8,128)S(1)}, f32[512,256]{1,0:T(8,128)S(1)}) custom-call(bf16[256,512]{1,0:T(8,128)(2,1)S(1)} %collective-permute-done.2.refs_2_.refs_4_.refs_0_, bf16[256,512]{1,0:T(8,128)(2,1)S(1)} %collective-permute-done.8.refs_4_.refs_1_, ...), custom_call_target="tpu_custom_call", output_to_operand_aliasing={{0}: (11, {})} | custom-call | flops 402653184 | bytes 3670016 | tf_op jit(solution)/shard_map/carried_2/pallas_call | solution.py:415
  48.9 3.6 %collective-permute-done.7.refs_2_ = bf16[256,512]{1,0:T(8,128)(2,1)S(1)} collective-permute-done((bf16[256,512]{1,0:T(8,128)(2,1)S(1)}, bf16[256,512]{1,0:T(8,128)(2,1)S(1)}, u32[]{:S(2)}, u32[]{:S(2)}) %collective-permute-start.7) | collective-permute-done | bytes 262176 | tf_op jit(solution)/shard_map/ppermute | solution.py:470
  52.5 1.5 %carried_3.1 = (bf16[512,2048]{1,0:T(8,128)(2,1)}, bf16[512,512]{1,0:T(8,128)(2,1)}, bf16[512,512]{1,0:T(8,128)(2,1)}) custom-call(bf16[256,512]{1,0:T(8,128)(2,1)S(1)} %collective-permute-done.5.refs_2_.refs_4_.refs_0_, bf16[256,512]{1,0:T(8,128)(2,1)S(1)} %collective-permute-done.6.refs_4_.refs_1_, ...), custom_call_target="tpu_custom_call", output_to_operand_aliasing={{0}: (11, {}), {1}: (12, {}), {2}: (13, {})} | custom-call | flops 402653184 | bytes 3670016 | tf_op jit(solution)/shard_map/carried_3/pallas_call | solution.py:415
  (22 shorter events, 0.8 us)
Async XLA Ops:
  2.7 11.6 %collective-permute-start = (bf16[256,512]{1,0:T(8,128)(2,1)S(1)}, bf16[256,512]{1,0:T(8,128)(2,1)S(1)}, u32[]{:S(2)}, u32[]{:S(2)}) collective-permute-start(bf16[256,512]{1,0:T(8,128)(2,1)S(1)} %first_state.1), channel_id=1, source_target_pairs={{0,4},{12,8},{1,5},{13,9},{2,6},{14,10},{3,7},{15,11},{16,20},{28,... | collective-permute-start | bytes 786440 | tf_op jit(solution)/shard_map/ppermute | solution.py:470
  9.3 7.5 %collective-permute-start.3 = (bf16[256,512]{1,0:T(8,128)(2,1)S(1)}, bf16[256,512]{1,0:T(8,128)(2,1)S(1)}, u32[]{:S(2)}, u32[]{:S(2)}) collective-permute-start(bf16[256,512]{1,0:T(8,128)(2,1)S(1)} %relay_1.2), channel_id=1, source_target_pairs={{0,4},{12,8},{1,5},{13,9},{2,6},{14,10},{3,7},{15,11},{16,20},{28,... | collective-permute-start | bytes 786440 | tf_op jit(solution)/shard_map/ppermute | solution.py:470
  14.3 3.4 %collective-permute-start.1 = (bf16[256,512]{1,0:T(8,128)(2,1)S(1)}, bf16[256,512]{1,0:T(8,128)(2,1)S(1)}, u32[]{:S(2)}, u32[]{:S(2)}) collective-permute-start(bf16[256,512]{1,0:T(8,128)(2,1)S(1)} %relay_1.3), channel_id=1, source_target_pairs={{4,8},{8,4},{5,9},{9,5},{6,10},{10,6},{7,11},{11,7},{20,24},{24,20... | collective-permute-start | bytes 786440 | tf_op jit(solution)/shard_map/ppermute | solution.py:470
  16.9 7.6 %copy-start = (bf16[512,512]{1,0:T(8,128)(2,1)S(1)}, bf16[512,512]{1,0:T(8,128)(2,1)}, u32[]{:S(2)}) copy-start(bf16[512,512]{1,0:T(8,128)(2,1)} %refs_5_.15) | copy-start | bytes 1572868
  16.9 7.6 %copy-start.1 = (bf16[512,2048]{1,0:T(8,128)(2,1)S(1)}, bf16[512,2048]{1,0:T(8,128)(2,1)}, u32[]{:S(2)}) copy-start(bf16[512,2048]{1,0:T(8,128)(2,1)} %refs_6_.3) | copy-start | bytes 6291460
  16.9 7.6 %copy-start.2 = (bf16[512,512]{1,0:T(8,128)(2,1)S(1)}, bf16[512,512]{1,0:T(8,128)(2,1)}, u32[]{:S(2)}) copy-start(bf16[512,512]{1,0:T(8,128)(2,1)} %refs_5_.12) | copy-start | bytes 1572868
  16.9 7.6 %copy-start.3 = (f32[32]{0:T(128)S(1)}, f32[32]{0:T(128)}, u32[]{:S(2)}) copy-start(f32[32]{0:T(128)} %param.13) | copy-start | bytes 388
  16.9 12.7 %collective-permute-start.4 = (bf16[256,512]{1,0:T(8,128)(2,1)S(1)}, bf16[256,512]{1,0:T(8,128)(2,1)S(1)}, u32[]{:S(2)}, u32[]{:S(2)}) collective-permute-start(bf16[256,512]{1,0:T(8,128)(2,1)S(1)} %relay_2.3), channel_id=1, source_target_pairs={{4,8},{8,4},{5,9},{9,5},{6,10},{10,6},{7,11},{11,7},{20,24},{24,20... | collective-permute-start | bytes 786440 | tf_op jit(solution)/shard_map/ppermute | solution.py:470
  17.9 12.6 %collective-permute-start.2 = (bf16[256,512]{1,0:T(8,128)(2,1)S(1)}, bf16[256,512]{1,0:T(8,128)(2,1)S(1)}, u32[]{:S(2)}, u32[]{:S(2)}) collective-permute-start(bf16[256,512]{1,0:T(8,128)(2,1)S(1)} %relay_2.2), channel_id=1, source_target_pairs={{0,4},{4,0},{8,12},{12,8},{1,5},{5,1},{9,13},{13,9},{2,6},{6,2},{1... | collective-permute-start | bytes 786440 | tf_op jit(solution)/shard_map/ppermute | solution.py:470
  29.7 7.3 %collective-permute-start.5 = (bf16[256,512]{1,0:T(8,128)(2,1)S(1)}, bf16[256,512]{1,0:T(8,128)(2,1)S(1)}, u32[]{:S(2)}, u32[]{:S(2)}) collective-permute-start(bf16[256,512]{1,0:T(8,128)(2,1)S(1)} %relay_3.2), channel_id=1, source_target_pairs={{0,4},{4,0},{8,12},{12,8},{1,5},{5,1},{9,13},{13,9},{2,6},{6,2},{1... | collective-permute-start | bytes 786440 | tf_op jit(solution)/shard_map/ppermute | solution.py:470
  30.6 7.2 %collective-permute-start.8 = (bf16[256,512]{1,0:T(8,128)(2,1)S(1)}, bf16[256,512]{1,0:T(8,128)(2,1)S(1)}, u32[]{:S(2)}, u32[]{:S(2)}) collective-permute-start(bf16[256,512]{1,0:T(8,128)(2,1)S(1)} %relay_3.3), channel_id=1, source_target_pairs={{4,8},{8,4},{5,9},{9,5},{6,10},{10,6},{7,11},{11,7},{20,24},{24,20... | collective-permute-start | bytes 786440 | tf_op jit(solution)/shard_map/ppermute | solution.py:470
  37.1 3.7 %collective-permute-start.6 = (bf16[256,512]{1,0:T(8,128)(2,1)S(1)}, bf16[256,512]{1,0:T(8,128)(2,1)S(1)}, u32[]{:S(2)}, u32[]{:S(2)}) collective-permute-start(bf16[256,512]{1,0:T(8,128)(2,1)S(1)} %relay_4.2), channel_id=1, source_target_pairs={{4,8},{8,4},{5,9},{9,5},{6,10},{10,6},{7,11},{11,7},{20,24},{24,20... | collective-permute-start | bytes 786440 | tf_op jit(solution)/shard_map/ppermute | solution.py:470
  37.9 9.6 %collective-permute-start.9 = (bf16[256,512]{1,0:T(8,128)(2,1)S(1)}, bf16[256,512]{1,0:T(8,128)(2,1)S(1)}, u32[]{:S(2)}, u32[]{:S(2)}) collective-permute-start(bf16[256,512]{1,0:T(8,128)(2,1)S(1)} %relay_4.3), channel_id=1, source_target_pairs={{4,0},{8,12},{5,1},{9,13},{6,2},{10,14},{7,3},{11,15},{20,16},{24,... | collective-permute-start | bytes 786440 | tf_op jit(solution)/shard_map/ppermute | solution.py:470
  40.9 11.7 %collective-permute-start.7 = (bf16[256,512]{1,0:T(8,128)(2,1)S(1)}, bf16[256,512]{1,0:T(8,128)(2,1)S(1)}, u32[]{:S(2)}, u32[]{:S(2)}) collective-permute-start(bf16[256,512]{1,0:T(8,128)(2,1)S(1)} %relay_5.1), channel_id=1, source_target_pairs={{4,0},{8,12},{5,1},{9,13},{6,2},{10,14},{7,3},{11,15},{20,16},{24,... | collective-permute-start | bytes 786440 | tf_op jit(solution)/shard_map/ppermute | solution.py:470

commit v5 on v4

--- a/solution.py
+++ b/solution.py
@@ -36,13 +36,11 @@
 
 def head_spread(parts, chunk):
     head_count = parts[0].shape[0]
-    rows = lax.broadcasted_iota(jnp.int32, (head_count, CHUNK), 0)
-    cols = lax.broadcasted_iota(jnp.int32, (head_count, CHUNK), 1)
-    pick = (rows == chunk * CHUNK_HEADS + cols // P_SIZE).astype(F32).astype(BF16)
-    total = dot(parts[0], pick, 0, 0)
-    for part in parts[1:]:
-        total += dot(part, pick, 0, 0)
-    return total
+    shape = (len(parts) * head_count, CHUNK)
+    head = lax.rem(lax.broadcasted_iota(jnp.int32, shape, 0), head_count)
+    cols = lax.broadcasted_iota(jnp.int32, shape, 1)
+    pick = (head == chunk * CHUNK_HEADS + cols // P_SIZE).astype(F32).astype(BF16)
+    return dot(jnp.concatenate(parts, axis=0), pick, 0, 0)
 
 
 def lower_mask(tokens):
@@ -235,22 +233,24 @@
 
     back = (back_in.astype(F32) * decay[place]).astype(BF16)
     part = pl.ds(inside * CHUNK, CHUNK)
-    carried = spread[:, part] * dot(b[:, own], back, 1, 0)
-    x_out[...] = (part_x[:, part] + carried).astype(BF16)
-    send(x_out, grad_x.at[:, pl.ds(chunk * CHUNK, CHUNK)], 0)
-    total_b = part_b[...] + dot(xw[:, span], back, 1, 1)
-    if last:
-        b_out, c_out = refs[-3:-1]
-        b_out[...] = total_b.astype(BF16)
-        send(b_out, grad_b.at[:, own], 1)
-    else:
-        grad_b[...] = total_b
-    total_c = part_c[...] + dot(dyw[:, span], fwd_in, 1, 1)
-    if last:
-        c_out[...] = total_c.astype(BF16)
-        send(c_out, grad_c.at[:, own], 2)
-    else:
-        grad_c[...] = total_c
+    half = b.shape[0] // 2
+    for low in (0, half):
+        rows = pl.ds(low, half)
+        slot = 3 * (low > 0)
+        carried = spread[rows, part] * dot(b[rows, own], back, 1, 0)
+        x_out[rows] = (part_x[rows, part] + carried).astype(BF16)
+        send(x_out.at[rows], grad_x.at[rows, pl.ds(chunk * CHUNK, CHUNK)], slot)
+        total_b = part_b[rows] + dot(xw[rows, span], back, 1, 1)
+        total_c = part_c[rows] + dot(dyw[rows, span], fwd_in, 1, 1)
+        if last:
+            b_out, c_out = refs[-3:-1]
+            b_out[rows] = total_b.astype(BF16)
+            send(b_out.at[rows], grad_b.at[rows, own], slot + 1)
+            c_out[rows] = total_c.astype(BF16)
+            send(c_out.at[rows], grad_c.at[rows, own], slot + 2)
+        else:
+            grad_b[rows] = total_b
+            grad_c[rows] = total_c
     for copy in copies:
         copy.wait()
 
@@ -424,7 +424,7 @@
             in_specs=[IN_VMEM] * (ranks + 7) + [ANYWHERE] * len(aliases),
             out_specs=out_specs,
             out_shape=out_shape,
-            scratch_shapes=scratch + [pltpu.SemaphoreType.DMA((3,))],
+            scratch_shapes=scratch + [pltpu.SemaphoreType.DMA((6,))],
             input_output_aliases=aliases,
             compiler_params=PARAMS,
             cost_estimate=cost(6 * tokens * CHUNK * N, 14 * tokens * CHUNK),

time: 54.3 us -> 53.5 us (0.985)
  Pallas kernels: 20.9 us -> 18.7 us
  waiting for transfers between devices: 15.2 us -> 16 us
  starting transfers between devices: 17 us -> 17.6 us
    pallas_call x2, Pallas kernels: 7.2 us -> 6.1 us  [local_states(): pl.pallas_call(partial(local_kernel, first=first, last=last, per_group=pe...]
    ppermute x10, waiting for transfers between devices: 15.2 us -> 16 us  [on_device(): got[key] = lax.ppermute(send, 'ctx', links(turn, even_links))]
    pallas_call x2, Pallas kernels: 5.12 us -> 4.29 us  [within(): pl.pallas_call(partial(within_kernel, group=group, per_group=per_group, s...]
    ppermute x10, starting transfers between devices: 17 us -> 17.6 us  [on_device(): got[key] = lax.ppermute(send, 'ctx', links(turn, even_links))]
  transfers between devices with their start and end apart: 10 -> 10, of which waited for: 4 -> 4; matrix products, arithmetic and copies ran while one was open for 0% -> 0% of each run, Pallas kernels for 32% -> 29%
where the time goes in v5:
time: 53.5 us; the launch traced here: 53.2 us
  Pallas kernels  18.7 us (35%)
  starting transfers between devices  17.6 us (33%)
  waiting for transfers between devices  16 us (30%)
  between operations  0.87 us (2%)
    ppermute x10, starting transfers between devices, on_device(): got[key] = lax.ppermute(send, 'ctx', links(turn, even_links))  17.6 us
    ppermute x10, waiting for transfers between devices, on_device(): got[key] = lax.ppermute(send, 'ctx', links(turn, even_links))  16 us
    pallas_call x2, Pallas kernels, local_states(): pl.pallas_call(partial(local_kernel, first=first, last=last, per_group=pe...  6.1 us
    pallas_call x4, Pallas kernels, carried(): pl.pallas_call(partial(carried_kernel, chunk=chunk, per_group=per_group,...  5.55 us
    pallas_call x2, Pallas kernels, within(): pl.pallas_call(partial(within_kernel, group=group, per_group=per_group, s...  4.29 us
    pallas_call x1, Pallas kernels, on_device(): pl.pallas_call(partial(first_kernel, ranks=ranks), in_specs=[ANYWHERE] *...  1.91 us
  transfers between devices with their start and end apart: 10, of which 4 were waited for; matrix products, arithmetic and copies ran while one was open for 0% of the time, Pallas kernels for 29%

profile of v5, /device:TPU:0, one launch (start us, length us, event | category | flops | bytes accessed | tf_op | source)
XLA Modules:
  0.0 53.2 jit_solution(6526177042498055228)
XLA Ops:
  0.6 1.9 %first_state.1 = bf16[256,512]{1,0:T(8,128)(2,1)S(1)} custom-call(bf16[32,512]{1,0:T(8,128)(2,1)} %bitcast.5, f32[1,32]{1,0:T(1,128)} %bitcast.7, bf16[512,2048]{1,0:T(8,128)(2,1)} %refs_6_.3, bf16[512,2048]{1,0:T(8,128)(2,1)} %refs_3_.3, bf16[512,512]{1,0:T(8,128)(2,1)} %refs_5_.15, bf16[512,512]{1,0:T(8,128)(2,1)} %refs_5_.12), custom_call_target="tpu_custom_call" | custom-call | flops 268435456 | bytes 1048576 | tf_op jit(solution)/shard_map/first_state/pallas_call | solution.py:308
  2.5 3.1 %collective-permute-start = (bf16[256,512]{1,0:T(8,128)(2,1)S(1)}, bf16[256,512]{1,0:T(8,128)(2,1)S(1)}, u32[]{:S(2)}, u32[]{:S(2)}) collective-permute-start(bf16[256,512]{1,0:T(8,128)(2,1)S(1)} %first_state.1), channel_id=1, source_target_pairs={{0,4},{12,8},{1,5},{13,9},{2,6},{14,10},{3,7},{15,11},{16,20},{28,... | collective-permute-start | bytes 786440 | tf_op jit(solution)/shard_map/ppermute | solution.py:470
  5.6 3.1 %states_0.1 = (bf16[512,1024]{1,0:T(8,128)(2,1)S(1)}, bf16[512,1024]{1,0:T(8,128)(2,1)S(1)}, f32[2,2,256,512]{3,2,1,0:T(8,128)S(1)}, f32[2,1,512]{2,1,0:T(1,128)...) custom-call(bf16[32,512]{1,0:T(8,128)(2,1)} %bitcast.6, f32[1,32]{1,0:T(1,128)} %bitcast.8, ...), custom_call_target="tpu_custom_call" | custom-call | flops 1610612736 | bytes 3145728 | tf_op jit(solution)/shard_map/states_0/pallas_call | solution.py:285
  8.8 1.3 %collective-permute-start.3 = (bf16[256,512]{1,0:T(8,128)(2,1)S(1)}, bf16[256,512]{1,0:T(8,128)(2,1)S(1)}, u32[]{:S(2)}, u32[]{:S(2)}) collective-permute-start(bf16[256,512]{1,0:T(8,128)(2,1)S(1)} %relay_1.2), channel_id=1, source_target_pairs={{0,4},{12,8},{1,5},{13,9},{2,6},{14,10},{3,7},{15,11},{16,20},{28,... | collective-permute-start | bytes 786440 | tf_op jit(solution)/shard_map/ppermute | solution.py:470
  10.1 3.0 %states_2.1 = (bf16[512,1024]{1,0:T(8,128)(2,1)S(1)}, bf16[512,1024]{1,0:T(8,128)(2,1)S(1)}, f32[2,2,256,512]{3,2,1,0:T(8,128)S(1)}, f32[2,1,512]{2,1,0:T(1,128)S(1)}) custom-call(bf16[2,32,512]{2,1,0:T(8,128)(2,1)S(1)} %get-tuple-element.56.refs_0_, bf16[2,32,512]{2,1,0:T(8,128)(2,1)S(1)} %get-tuple-element.69.refs_1_.refs_7_, bf16[512,2048]{1,0:T(8,128)(2,1)} %refs_6_.3, ...), custom_call_target="tpu_custom_call" | custom-call | flops 1610612736 | bytes 3145728 | tf_op jit(solution)/shard_map/states_2/pallas_call | solution.py:285
  13.2 0.7 %collective-permute-start.1 = (bf16[256,512]{1,0:T(8,128)(2,1)S(1)}, bf16[256,512]{1,0:T(8,128)(2,1)S(1)}, u32[]{:S(2)}, u32[]{:S(2)}) collective-permute-start(bf16[256,512]{1,0:T(8,128)(2,1)S(1)} %relay_1.3), channel_id=1, source_target_pairs={{4,8},{8,4},{5,9},{9,5},{6,10},{10,6},{7,11},{11,7},{20,24},{24,20... | collective-permute-start | bytes 786440 | tf_op jit(solution)/shard_map/ppermute | solution.py:470
  13.9 2.9 %collective-permute-done.3.refs_2_.refs_0_ = bf16[256,512]{1,0:T(8,128)(2,1)S(1)} collective-permute-done((bf16[256,512]{1,0:T(8,128)(2,1)S(1)}, bf16[256,512]{1,0:T(8,128)(2,1)S(1)}, u32[]{:S(2)}, u32[]{:S(2)}) %collective-permute-start.3) | collective-permute-done | bytes 262176 | tf_op jit(solution)/shard_map/ppermute | solution.py:470
  16.9 0.8 %collective-permute-start.4 = (bf16[256,512]{1,0:T(8,128)(2,1)S(1)}, bf16[256,512]{1,0:T(8,128)(2,1)S(1)}, u32[]{:S(2)}, u32[]{:S(2)}) collective-permute-start(bf16[256,512]{1,0:T(8,128)(2,1)S(1)} %relay_2.3), channel_id=1, source_target_pairs={{4,8},{8,4},{5,9},{9,5},{6,10},{10,6},{7,11},{11,7},{20,24},{24,20... | collective-permute-start | bytes 786440 | tf_op jit(solution)/shard_map/ppermute | solution.py:470
  17.9 6.5 %collective-permute-start.2 = (bf16[256,512]{1,0:T(8,128)(2,1)S(1)}, bf16[256,512]{1,0:T(8,128)(2,1)S(1)}, u32[]{:S(2)}, u32[]{:S(2)}) collective-permute-start(bf16[256,512]{1,0:T(8,128)(2,1)S(1)} %relay_2.2), channel_id=1, source_target_pairs={{0,4},{4,0},{8,12},{12,8},{1,5},{5,1},{9,13},{13,9},{2,6},{6,2},{1... | collective-permute-start | bytes 786440 | tf_op jit(solution)/shard_map/ppermute | solution.py:470
  24.3 2.2 %within_0.1 = (f32[512,1024]{1,0:T(8,128)S(1)}, f32[512,256]{1,0:T(8,128)S(1)}, f32[512,256]{1,0:T(8,128)S(1)}, f32[512,1024]{1,0:T(8,128)S(1)}) custom-call(bf16[512,1024]{1,0:T(8,128)(2,1)S(1)} %get-tuple-element.65.refs_0_.refs_3_, bf16[512,1024]{1,0:T(8,128)(2,1)S(1)} %get-tuple-element.67.refs_1_.refs_3_, ...), custom_call_target="tpu_custom_call" | custom-call | flops 1610612736 | bytes 5242880 | tf_op jit(solution)/shard_map/within_0/pallas_call | solution.py:343
  26.5 2.1 %within_1.1 = (f32[512,1024]{1,0:T(8,128)S(1)}, f32[512,256]{1,0:T(8,128)S(1)}, f32[512,256]{1,0:T(8,128)S(1)}, f32[512,1024]{1,0:T(8,128)S(1)}) custom-call(bf16[512,1024]{1,0:T(8,128)(2,1)S(1)} %get-tuple-element.65.refs_0_.refs_3_, bf16[512,1024]{1,0:T(8,128)(2,1)S(1)} %get-tuple-element.67.refs_1_.refs_3_, ...), custom_call_target="tpu_custom_call" | custom-call | flops 1610612736 | bytes 5242880 | tf_op jit(solution)/shard_map/within_1/pallas_call | solution.py:343
  28.7 0.1 relay_3.2
  28.8 1.3 %collective-permute-start.5 = (bf16[256,512]{1,0:T(8,128)(2,1)S(1)}, bf16[256,512]{1,0:T(8,128)(2,1)S(1)}, u32[]{:S(2)}, u32[]{:S(2)}) collective-permute-start(bf16[256,512]{1,0:T(8,128)(2,1)S(1)} %relay_3.2), channel_id=1, source_target_pairs={{0,4},{4,0},{8,12},{12,8},{1,5},{5,1},{9,13},{13,9},{2,6},{6,2},{1... | collective-permute-start | bytes 786440 | tf_op jit(solution)/shard_map/ppermute | solution.py:470
  30.2 0.7 %collective-permute-start.8 = (bf16[256,512]{1,0:T(8,128)(2,1)S(1)}, bf16[256,512]{1,0:T(8,128)(2,1)S(1)}, u32[]{:S(2)}, u32[]{:S(2)}) collective-permute-start(bf16[256,512]{1,0:T(8,128)(2,1)S(1)} %relay_3.3), channel_id=1, source_target_pairs={{4,8},{8,4},{5,9},{9,5},{6,10},{10,6},{7,11},{11,7},{20,24},{24,20... | collective-permute-start | bytes 786440 | tf_op jit(solution)/shard_map/ppermute | solution.py:470
  30.8 1.3 %carried_0.1 = (bf16[512,2048]{1,0:T(8,128)(2,1)}, f32[512,256]{1,0:T(8,128)S(1)}, f32[512,256]{1,0:T(8,128)S(1)}) custom-call(bf16[256,512]{1,0:T(8,128)(2,1)S(1)} %collective-permute-done.refs_2_.refs_0_, bf16[256,512]{1,0:T(8,128)(2,1)S(1)} %collective-permute-done.1.refs_4_.refs_1_, bf16[256,512]{1,0:T(8,128)(2,1)S(1)} %collective-permute-done.2.refs_2_.refs_4_.refs_0_, ...), custom_call_target="tpu_custom_call" | custom-call | flops 402653184 | bytes 3670016 | tf_op jit(solution)/shard_map/carried_0/pallas_call | solution.py:415
  32.2 3.6 %collective-permute-done.5.refs_2_.refs_4_.refs_0_ = bf16[256,512]{1,0:T(8,128)(2,1)S(1)} collective-permute-done((bf16[256,512]{1,0:T(8,128)(2,1)S(1)}, bf16[256,512]{1,0:T(8,128)(2,1)S(1)}, u32[]{:S(2)}, u32[]{:S(2)}) %collective-permute-start.5) | collective-permute-done | bytes 262176 | tf_op jit(solution)/shard_map/ppermute | solution.py:470
  35.9 0.7 %collective-permute-start.6 = (bf16[256,512]{1,0:T(8,128)(2,1)S(1)}, bf16[256,512]{1,0:T(8,128)(2,1)S(1)}, u32[]{:S(2)}, u32[]{:S(2)}) collective-permute-start(bf16[256,512]{1,0:T(8,128)(2,1)S(1)} %relay_4.2), channel_id=1, source_target_pairs={{4,8},{8,4},{5,9},{9,5},{6,10},{10,6},{7,11},{11,7},{20,24},{24,20... | collective-permute-start | bytes 786440 | tf_op jit(solution)/shard_map/ppermute | solution.py:470
  36.7 1.3 %collective-permute-start.9 = (bf16[256,512]{1,0:T(8,128)(2,1)S(1)}, bf16[256,512]{1,0:T(8,128)(2,1)S(1)}, u32[]{:S(2)}, u32[]{:S(2)}) collective-permute-start(bf16[256,512]{1,0:T(8,128)(2,1)S(1)} %relay_4.3), channel_id=1, source_target_pairs={{4,0},{8,12},{5,1},{9,13},{6,2},{10,14},{7,3},{11,15},{20,16},{24,... | collective-permute-start | bytes 786440 | tf_op jit(solution)/shard_map/ppermute | solution.py:470
  38.0 1.5 %carried_1.1 = (bf16[512,2048]{1,0:T(8,128)(2,1)}, bf16[512,512]{1,0:T(8,128)(2,1)}, bf16[512,512]{1,0:T(8,128)(2,1)}) custom-call(bf16[256,512]{1,0:T(8,128)(2,1)S(1)} %collective-permute-done.3.refs_2_.refs_0_, bf16[256,512]{1,0:T(8,128)(2,1)S(1)} %collective-permute-done.4.refs_4_.refs_1_, ...), custom_call_target="tpu_custom_call", output_to_operand_aliasing={{0}: (11, {})} | custom-call | flops 402653184 | bytes 3670016 | tf_op jit(solution)/shard_map/carried_1/pallas_call | solution.py:415
  39.6 1.3 %collective-permute-start.7 = (bf16[256,512]{1,0:T(8,128)(2,1)S(1)}, bf16[256,512]{1,0:T(8,128)(2,1)S(1)}, u32[]{:S(2)}, u32[]{:S(2)}) collective-permute-start(bf16[256,512]{1,0:T(8,128)(2,1)S(1)} %relay_5.1), channel_id=1, source_target_pairs={{4,0},{8,12},{5,1},{9,13},{6,2},{10,14},{7,3},{11,15},{20,16},{24,... | collective-permute-start | bytes 786440 | tf_op jit(solution)/shard_map/ppermute | solution.py:470
  40.9 5.9 %collective-permute-done.9.refs_2_ = bf16[256,512]{1,0:T(8,128)(2,1)S(1)} collective-permute-done((bf16[256,512]{1,0:T(8,128)(2,1)S(1)}, bf16[256,512]{1,0:T(8,128)(2,1)S(1)}, u32[]{:S(2)}, u32[]{:S(2)}) %collective-permute-start.9) | collective-permute-done | bytes 262176 | tf_op jit(solution)/shard_map/ppermute | solution.py:470
  46.8 1.3 %carried_2.1 = (bf16[512,2048]{1,0:T(8,128)(2,1)}, f32[512,256]{1,0:T(8,128)S(1)}, f32[512,256]{1,0:T(8,128)S(1)}) custom-call(bf16[256,512]{1,0:T(8,128)(2,1)S(1)} %collective-permute-done.2.refs_2_.refs_4_.refs_0_, bf16[256,512]{1,0:T(8,128)(2,1)S(1)} %collective-permute-done.8.refs_4_.refs_1_, ...), custom_call_target="tpu_custom_call", output_to_operand_aliasing={{0}: (11, {})} | custom-call | flops 402653184 | bytes 3670016 | tf_op jit(solution)/shard_map/carried_2/pallas_call | solution.py:415
  48.1 3.6 %collective-permute-done.7.refs_2_ = bf16[256,512]{1,0:T(8,128)(2,1)S(1)} collective-permute-done((bf16[256,512]{1,0:T(8,128)(2,1)S(1)}, bf16[256,512]{1,0:T(8,128)(2,1)S(1)}, u32[]{:S(2)}, u32[]{:S(2)}) %collective-permute-start.7) | collective-permute-done | bytes 262176 | tf_op jit(solution)/shard_map/ppermute | solution.py:470
  51.7 1.4 %carried_3.1 = (bf16[512,2048]{1,0:T(8,128)(2,1)}, bf16[512,512]{1,0:T(8,128)(2,1)}, bf16[512,512]{1,0:T(8,128)(2,1)}) custom-call(bf16[256,512]{1,0:T(8,128)(2,1)S(1)} %collective-permute-done.5.refs_2_.refs_4_.refs_0_, bf16[256,512]{1,0:T(8,128)(2,1)S(1)} %collective-permute-done.6.refs_4_.refs_1_, ...), custom_call_target="tpu_custom_call", output_to_operand_aliasing={{0}: (11, {}), {1}: (12, {}), {2}: (13, {})} | custom-call | flops 402653184 | bytes 3670016 | tf_op jit(solution)/shard_map/carried_3/pallas_call | solution.py:415
  (22 shorter events, 0.8 us)
Async XLA Ops:
  2.5 10.6 %collective-permute-start = (bf16[256,512]{1,0:T(8,128)(2,1)S(1)}, bf16[256,512]{1,0:T(8,128)(2,1)S(1)}, u32[]{:S(2)}, u32[]{:S(2)}) collective-permute-start(bf16[256,512]{1,0:T(8,128)(2,1)S(1)} %first_state.1), channel_id=1, source_target_pairs={{0,4},{12,8},{1,5},{13,9},{2,6},{14,10},{3,7},{15,11},{16,20},{28,... | collective-permute-start | bytes 786440 | tf_op jit(solution)/shard_map/ppermute | solution.py:470
  8.8 8.0 %collective-permute-start.3 = (bf16[256,512]{1,0:T(8,128)(2,1)S(1)}, bf16[256,512]{1,0:T(8,128)(2,1)S(1)}, u32[]{:S(2)}, u32[]{:S(2)}) collective-permute-start(bf16[256,512]{1,0:T(8,128)(2,1)S(1)} %relay_1.2), channel_id=1, source_target_pairs={{0,4},{12,8},{1,5},{13,9},{2,6},{14,10},{3,7},{15,11},{16,20},{28,... | collective-permute-start | bytes 786440 | tf_op jit(solution)/shard_map/ppermute | solution.py:470
  13.2 4.5 %collective-permute-start.1 = (bf16[256,512]{1,0:T(8,128)(2,1)S(1)}, bf16[256,512]{1,0:T(8,128)(2,1)S(1)}, u32[]{:S(2)}, u32[]{:S(2)}) collective-permute-start(bf16[256,512]{1,0:T(8,128)(2,1)S(1)} %relay_1.3), channel_id=1, source_target_pairs={{4,8},{8,4},{5,9},{9,5},{6,10},{10,6},{7,11},{11,7},{20,24},{24,20... | collective-permute-start | bytes 786440 | tf_op jit(solution)/shard_map/ppermute | solution.py:470
  16.9 7.5 %copy-start = (bf16[512,512]{1,0:T(8,128)(2,1)S(1)}, bf16[512,512]{1,0:T(8,128)(2,1)}, u32[]{:S(2)}) copy-start(bf16[512,512]{1,0:T(8,128)(2,1)} %refs_5_.15) | copy-start | bytes 1572868
  16.9 7.4 %copy-start.1 = (bf16[512,2048]{1,0:T(8,128)(2,1)S(1)}, bf16[512,2048]{1,0:T(8,128)(2,1)}, u32[]{:S(2)}) copy-start(bf16[512,2048]{1,0:T(8,128)(2,1)} %refs_6_.3) | copy-start | bytes 6291460
  16.9 7.4 %copy-start.2 = (bf16[512,512]{1,0:T(8,128)(2,1)S(1)}, bf16[512,512]{1,0:T(8,128)(2,1)}, u32[]{:S(2)}) copy-start(bf16[512,512]{1,0:T(8,128)(2,1)} %refs_5_.12) | copy-start | bytes 1572868
  16.9 7.4 %copy-start.3 = (f32[32]{0:T(128)S(1)}, f32[32]{0:T(128)}, u32[]{:S(2)}) copy-start(f32[32]{0:T(128)} %param.13) | copy-start | bytes 388
  16.9 11.7 %collective-permute-start.4 = (bf16[256,512]{1,0:T(8,128)(2,1)S(1)}, bf16[256,512]{1,0:T(8,128)(2,1)S(1)}, u32[]{:S(2)}, u32[]{:S(2)}) collective-permute-start(bf16[256,512]{1,0:T(8,128)(2,1)S(1)} %relay_2.3), channel_id=1, source_target_pairs={{4,8},{8,4},{5,9},{9,5},{6,10},{10,6},{7,11},{11,7},{20,24},{24,20... | collective-permute-start | bytes 786440 | tf_op jit(solution)/shard_map/ppermute | solution.py:470
  17.9 12.2 %collective-permute-start.2 = (bf16[256,512]{1,0:T(8,128)(2,1)S(1)}, bf16[256,512]{1,0:T(8,128)(2,1)S(1)}, u32[]{:S(2)}, u32[]{:S(2)}) collective-permute-start(bf16[256,512]{1,0:T(8,128)(2,1)S(1)} %relay_2.2), channel_id=1, source_target_pairs={{0,4},{4,0},{8,12},{12,8},{1,5},{5,1},{9,13},{13,9},{2,6},{6,2},{1... | collective-permute-start | bytes 786440 | tf_op jit(solution)/shard_map/ppermute | solution.py:470
  28.8 7.0 %collective-permute-start.5 = (bf16[256,512]{1,0:T(8,128)(2,1)S(1)}, bf16[256,512]{1,0:T(8,128)(2,1)S(1)}, u32[]{:S(2)}, u32[]{:S(2)}) collective-permute-start(bf16[256,512]{1,0:T(8,128)(2,1)S(1)} %relay_3.2), channel_id=1, source_target_pairs={{0,4},{4,0},{8,12},{12,8},{1,5},{5,1},{9,13},{13,9},{2,6},{6,2},{1... | collective-permute-start | bytes 786440 | tf_op jit(solution)/shard_map/ppermute | solution.py:470
  30.2 6.4 %collective-permute-start.8 = (bf16[256,512]{1,0:T(8,128)(2,1)S(1)}, bf16[256,512]{1,0:T(8,128)(2,1)S(1)}, u32[]{:S(2)}, u32[]{:S(2)}) collective-permute-start(bf16[256,512]{1,0:T(8,128)(2,1)S(1)} %relay_3.3), channel_id=1, source_target_pairs={{4,8},{8,4},{5,9},{9,5},{6,10},{10,6},{7,11},{11,7},{20,24},{24,20... | collective-permute-start | bytes 786440 | tf_op jit(solution)/shard_map/ppermute | solution.py:470
  35.9 3.6 %collective-permute-start.6 = (bf16[256,512]{1,0:T(8,128)(2,1)S(1)}, bf16[256,512]{1,0:T(8,128)(2,1)S(1)}, u32[]{:S(2)}, u32[]{:S(2)}) collective-permute-start(bf16[256,512]{1,0:T(8,128)(2,1)S(1)} %relay_4.2), channel_id=1, source_target_pairs={{4,8},{8,4},{5,9},{9,5},{6,10},{10,6},{7,11},{11,7},{20,24},{24,20... | collective-permute-start | bytes 786440 | tf_op jit(solution)/shard_map/ppermute | solution.py:470
  36.7 10.1 %collective-permute-start.9 = (bf16[256,512]{1,0:T(8,128)(2,1)S(1)}, bf16[256,512]{1,0:T(8,128)(2,1)S(1)}, u32[]{:S(2)}, u32[]{:S(2)}) collective-permute-start(bf16[256,512]{1,0:T(8,128)(2,1)S(1)} %relay_4.3), channel_id=1, source_target_pairs={{4,0},{8,12},{5,1},{9,13},{6,2},{10,14},{7,3},{11,15},{20,16},{24,... | collective-permute-start | bytes 786440 | tf_op jit(solution)/shard_map/ppermute | solution.py:470
  39.6 12.1 %collective-permute-start.7 = (bf16[256,512]{1,0:T(8,128)(2,1)S(1)}, bf16[256,512]{1,0:T(8,128)(2,1)S(1)}, u32[]{:S(2)}, u32[]{:S(2)}) collective-permute-start(bf16[256,512]{1,0:T(8,128)(2,1)S(1)} %relay_5.1), channel_id=1, source_target_pairs={{4,0},{8,12},{5,1},{9,13},{6,2},{10,14},{7,3},{11,15},{20,16},{24,... | collective-permute-start | bytes 786440 | tf_op jit(solution)/shard_map/ppermute | solution.py:470

commit v6 on v5

--- a/solution.py
+++ b/solution.py
@@ -167,22 +167,39 @@
     lower = lower_mask(b.shape[0])
     own = pl.ds(group * N, N)
     chunks = range(group * per_group, (group + 1) * per_group)
-    scores = jnp.where(lower, dot(c[:, own], b[:, own], 1, 1), 0.0).astype(BF16)
-    weighted = sum(
-        dot(piece(dyw, chunk, starts), piece(xw, chunk, starts), 1, 1) for chunk in chunks
+    half = b.shape[0] // 2
+    b_own, c_own = b[:, own], c[:, own]
+
+    def triangle(lefts, rights):
+        pairs = list(zip(lefts, rights))
+        top = sum(dot(left[:half], right[:half], 1, 1) for left, right in pairs)
+        low = sum(dot(left[half:], right, 1, 1) for left, right in pairs)
+        top = jnp.where(lower[:half, :half], top, 0.0).astype(BF16)
+        return top, jnp.where(lower[half:], low, 0.0).astype(BF16)
+
+    def turned(parts, right):
+        top, low = parts
+        upper_half = dot(top, right[:half], 0, 0) + dot(low[:, :half], right[half:], 0, 0)
+        return upper_half, dot(low[:, half:], right[half:], 0, 0)
+
+    scores = triangle([c_own], [b_own])
+    weighted = triangle(
+        [piece(dyw, chunk, starts) for chunk in chunks],
+        [piece(xw, chunk, starts) for chunk in chunks],
     )
-    weighted = jnp.where(lower, weighted, 0.0).astype(BF16)
-    grad_b[...] = dot(weighted, c[:, own], 0, 0)
-    grad_c[...] = dot(weighted, b[:, own], 1, 0)
+    grad_b[:half], grad_b[half:] = turned(weighted, c_own)
+    grad_c[:half] = dot(weighted[0], b_own[:half], 1, 0)
+    grad_c[half:] = dot(weighted[1], b_own, 1, 0)
     gains = terms(jnp.broadcast_to(columns(gain[...]), (gain.shape[1], 128)), 3)
     for part, chunk in enumerate(chunks):
         spread = head_spread((wx[0], wx[1]), chunk)
         rows = dy[:, pl.ds(chunk * CHUNK, CHUNK)].astype(F32)
         skip = head_spread(gains, chunk)[0:1, :] * rows
         spread_out[:, pl.ds(part * CHUNK, CHUNK)] = spread
-        grad_x[:, pl.ds(part * CHUNK, CHUNK)] = (
-            spread * dot(scores, piece(dyw, chunk, starts), 0, 0) + skip
-        )
+        sums = turned(scores, piece(dyw, chunk, starts))
+        for low, value in zip((0, half), sums):
+            span = slice(low, low + half)
+            grad_x[span, pl.ds(part * CHUNK, CHUNK)] = spread[span] * value + skip[span]
 
 
 def relay_kernel(*refs, turn, even_links, ranks, starts):

time: 53.5 us -> 53.5 us (level)
  transfers between devices with their start and end apart: 10 -> 10, of which waited for: 4 -> 4; matrix products, arithmetic and copies ran while one was open for 0% -> 0% of each run, Pallas kernels for 29% -> 28%
where the time goes in v6:
time: 53.5 us; the launch traced here: 53.2 us
  Pallas kernels  18.5 us (35%)
  starting transfers between devices  17.7 us (33%)
  waiting for transfers between devices  16 us (30%)
  between operations  0.87 us (2%)
    ppermute x10, starting transfers between devices, on_device(): got[key] = lax.ppermute(send, 'ctx', links(turn, even_links))  17.7 us
    ppermute x10, waiting for transfers between devices, on_device(): got[key] = lax.ppermute(send, 'ctx', links(turn, even_links))  16 us
    pallas_call x2, Pallas kernels, local_states(): pl.pallas_call(partial(local_kernel, first=first, last=last, per_group=pe...  6.1 us
    pallas_call x4, Pallas kernels, carried(): pl.pallas_call(partial(carried_kernel, chunk=chunk, per_group=per_group,...  5.55 us
    pallas_call x2, Pallas kernels, within(): pl.pallas_call(partial(within_kernel, group=group, per_group=per_group, s...  4.12 us
    pallas_call x1, Pallas kernels, on_device(): pl.pallas_call(partial(first_kernel, ranks=ranks), in_specs=[ANYWHERE] *...  1.91 us
  transfers between devices with their start and end apart: 10, of which 4 were waited for; matrix products, arithmetic and copies ran while one was open for 0% of the time, Pallas kernels for 28%

profile of v6, /device:TPU:0, one launch (start us, length us, event | category | flops | bytes accessed | tf_op | source)
XLA Modules:
  0.0 53.2 jit_solution(14674023591458845236)
XLA Ops:
  0.6 1.9 %first_state.1 = bf16[256,512]{1,0:T(8,128)(2,1)S(1)} custom-call(bf16[32,512]{1,0:T(8,128)(2,1)} %bitcast.5, f32[1,32]{1,0:T(1,128)} %bitcast.7, bf16[512,2048]{1,0:T(8,128)(2,1)} %refs_6_.3, bf16[512,2048]{1,0:T(8,128)(2,1)} %refs_3_.3, bf16[512,512]{1,0:T(8,128)(2,1)} %refs_5_.15, bf16[512,512]{1,0:T(8,128)(2,1)} %refs_5_.12), custom_call_target="tpu_custom_call" | custom-call | flops 268435456 | bytes 1048576 | tf_op jit(solution)/shard_map/first_state/pallas_call | solution.py:325
  2.5 3.1 %collective-permute-start = (bf16[256,512]{1,0:T(8,128)(2,1)S(1)}, bf16[256,512]{1,0:T(8,128)(2,1)S(1)}, u32[]{:S(2)}, u32[]{:S(2)}) collective-permute-start(bf16[256,512]{1,0:T(8,128)(2,1)S(1)} %first_state.1), channel_id=1, source_target_pairs={{0,4},{12,8},{1,5},{13,9},{2,6},{14,10},{3,7},{15,11},{16,20},{28,... | collective-permute-start | bytes 786440 | tf_op jit(solution)/shard_map/ppermute | solution.py:487
  5.6 3.1 %states_0.1 = (bf16[512,1024]{1,0:T(8,128)(2,1)S(1)}, bf16[512,1024]{1,0:T(8,128)(2,1)S(1)}, f32[2,2,256,512]{3,2,1,0:T(8,128)S(1)}, f32[2,1,512]{2,1,0:T(1,128)...) custom-call(bf16[32,512]{1,0:T(8,128)(2,1)} %bitcast.6, f32[1,32]{1,0:T(1,128)} %bitcast.8, ...), custom_call_target="tpu_custom_call" | custom-call | flops 1610612736 | bytes 3145728 | tf_op jit(solution)/shard_map/states_0/pallas_call | solution.py:302
  8.8 1.3 %collective-permute-start.3 = (bf16[256,512]{1,0:T(8,128)(2,1)S(1)}, bf16[256,512]{1,0:T(8,128)(2,1)S(1)}, u32[]{:S(2)}, u32[]{:S(2)}) collective-permute-start(bf16[256,512]{1,0:T(8,128)(2,1)S(1)} %relay_1.2), channel_id=1, source_target_pairs={{0,4},{12,8},{1,5},{13,9},{2,6},{14,10},{3,7},{15,11},{16,20},{28,... | collective-permute-start | bytes 786440 | tf_op jit(solution)/shard_map/ppermute | solution.py:487
  10.1 3.0 %states_2.1 = (bf16[512,1024]{1,0:T(8,128)(2,1)S(1)}, bf16[512,1024]{1,0:T(8,128)(2,1)S(1)}, f32[2,2,256,512]{3,2,1,0:T(8,128)S(1)}, f32[2,1,512]{2,1,0:T(1,128)S(1)}) custom-call(bf16[2,32,512]{2,1,0:T(8,128)(2,1)S(1)} %get-tuple-element.56.refs_0_, bf16[2,32,512]{2,1,0:T(8,128)(2,1)S(1)} %get-tuple-element.69.refs_1_.refs_7_, bf16[512,2048]{1,0:T(8,128)(2,1)} %refs_6_.3, ...), custom_call_target="tpu_custom_call" | custom-call | flops 1610612736 | bytes 3145728 | tf_op jit(solution)/shard_map/states_2/pallas_call | solution.py:302
  13.2 0.7 %collective-permute-start.1 = (bf16[256,512]{1,0:T(8,128)(2,1)S(1)}, bf16[256,512]{1,0:T(8,128)(2,1)S(1)}, u32[]{:S(2)}, u32[]{:S(2)}) collective-permute-start(bf16[256,512]{1,0:T(8,128)(2,1)S(1)} %relay_1.3), channel_id=1, source_target_pairs={{4,8},{8,4},{5,9},{9,5},{6,10},{10,6},{7,11},{11,7},{20,24},{24,20... | collective-permute-start | bytes 786440 | tf_op jit(solution)/shard_map/ppermute | solution.py:487
  13.9 2.9 %collective-permute-done.3.refs_2_.refs_0_ = bf16[256,512]{1,0:T(8,128)(2,1)S(1)} collective-permute-done((bf16[256,512]{1,0:T(8,128)(2,1)S(1)}, bf16[256,512]{1,0:T(8,128)(2,1)S(1)}, u32[]{:S(2)}, u32[]{:S(2)}) %collective-permute-start.3) | collective-permute-done | bytes 262176 | tf_op jit(solution)/shard_map/ppermute | solution.py:487
  16.9 0.8 %collective-permute-start.4 = (bf16[256,512]{1,0:T(8,128)(2,1)S(1)}, bf16[256,512]{1,0:T(8,128)(2,1)S(1)}, u32[]{:S(2)}, u32[]{:S(2)}) collective-permute-start(bf16[256,512]{1,0:T(8,128)(2,1)S(1)} %relay_2.3), channel_id=1, source_target_pairs={{4,8},{8,4},{5,9},{9,5},{6,10},{10,6},{7,11},{11,7},{20,24},{24,20... | collective-permute-start | bytes 786440 | tf_op jit(solution)/shard_map/ppermute | solution.py:487
  17.9 6.5 %collective-permute-start.2 = (bf16[256,512]{1,0:T(8,128)(2,1)S(1)}, bf16[256,512]{1,0:T(8,128)(2,1)S(1)}, u32[]{:S(2)}, u32[]{:S(2)}) collective-permute-start(bf16[256,512]{1,0:T(8,128)(2,1)S(1)} %relay_2.2), channel_id=1, source_target_pairs={{0,4},{4,0},{8,12},{12,8},{1,5},{5,1},{9,13},{13,9},{2,6},{6,2},{1... | collective-permute-start | bytes 786440 | tf_op jit(solution)/shard_map/ppermute | solution.py:487
  24.3 2.1 %within_0.1 = (f32[512,1024]{1,0:T(8,128)S(1)}, f32[512,256]{1,0:T(8,128)S(1)}, f32[512,256]{1,0:T(8,128)S(1)}, f32[512,1024]{1,0:T(8,128)S(1)}) custom-call(bf16[512,1024]{1,0:T(8,128)(2,1)S(1)} %get-tuple-element.65.refs_0_.refs_3_, bf16[512,1024]{1,0:T(8,128)(2,1)S(1)} %get-tuple-element.67.refs_1_.refs_3_, ...), custom_call_target="tpu_custom_call" | custom-call | flops 1610612736 | bytes 5242880 | tf_op jit(solution)/shard_map/within_0/pallas_call | solution.py:360
  26.4 2.1 %within_1.1 = (f32[512,1024]{1,0:T(8,128)S(1)}, f32[512,256]{1,0:T(8,128)S(1)}, f32[512,256]{1,0:T(8,128)S(1)}, f32[512,1024]{1,0:T(8,128)S(1)}) custom-call(bf16[512,1024]{1,0:T(8,128)(2,1)S(1)} %get-tuple-element.65.refs_0_.refs_3_, bf16[512,1024]{1,0:T(8,128)(2,1)S(1)} %get-tuple-element.67.refs_1_.refs_3_, ...), custom_call_target="tpu_custom_call" | custom-call | flops 1610612736 | bytes 5242880 | tf_op jit(solution)/shard_map/within_1/pallas_call | solution.py:360
  28.6 1.4 %collective-permute-start.5 = (bf16[256,512]{1,0:T(8,128)(2,1)S(1)}, bf16[256,512]{1,0:T(8,128)(2,1)S(1)}, u32[]{:S(2)}, u32[]{:S(2)}) collective-permute-start(bf16[256,512]{1,0:T(8,128)(2,1)S(1)} %relay_3.2), channel_id=1, source_target_pairs={{0,4},{4,0},{8,12},{12,8},{1,5},{5,1},{9,13},{13,9},{2,6},{6,2},{1... | collective-permute-start | bytes 786440 | tf_op jit(solution)/shard_map/ppermute | solution.py:487
  30.2 0.7 %collective-permute-start.8 = (bf16[256,512]{1,0:T(8,128)(2,1)S(1)}, bf16[256,512]{1,0:T(8,128)(2,1)S(1)}, u32[]{:S(2)}, u32[]{:S(2)}) collective-permute-start(bf16[256,512]{1,0:T(8,128)(2,1)S(1)} %relay_3.3), channel_id=1, source_target_pairs={{4,8},{8,4},{5,9},{9,5},{6,10},{10,6},{7,11},{11,7},{20,24},{24,20... | collective-permute-start | bytes 786440 | tf_op jit(solution)/shard_map/ppermute | solution.py:487
  30.8 1.3 %carried_0.1 = (bf16[512,2048]{1,0:T(8,128)(2,1)}, f32[512,256]{1,0:T(8,128)S(1)}, f32[512,256]{1,0:T(8,128)S(1)}) custom-call(bf16[256,512]{1,0:T(8,128)(2,1)S(1)} %collective-permute-done.refs_2_.refs_0_, bf16[256,512]{1,0:T(8,128)(2,1)S(1)} %collective-permute-done.1.refs_4_.refs_1_, bf16[256,512]{1,0:T(8,128)(2,1)S(1)} %collective-permute-done.2.refs_2_.refs_4_.refs_0_, ...), custom_call_target="tpu_custom_call" | custom-call | flops 402653184 | bytes 3670016 | tf_op jit(solution)/shard_map/carried_0/pallas_call | solution.py:432
  32.2 3.4 %collective-permute-done.5.refs_2_.refs_4_.refs_0_ = bf16[256,512]{1,0:T(8,128)(2,1)S(1)} collective-permute-done((bf16[256,512]{1,0:T(8,128)(2,1)S(1)}, bf16[256,512]{1,0:T(8,128)(2,1)S(1)}, u32[]{:S(2)}, u32[]{:S(2)}) %collective-permute-start.5) | collective-permute-done | bytes 262176 | tf_op jit(solution)/shard_map/ppermute | solution.py:487
  35.7 0.7 %collective-permute-start.6 = (bf16[256,512]{1,0:T(8,128)(2,1)S(1)}, bf16[256,512]{1,0:T(8,128)(2,1)S(1)}, u32[]{:S(2)}, u32[]{:S(2)}) collective-permute-start(bf16[256,512]{1,0:T(8,128)(2,1)S(1)} %relay_4.2), channel_id=1, source_target_pairs={{4,8},{8,4},{5,9},{9,5},{6,10},{10,6},{7,11},{11,7},{20,24},{24,20... | collective-permute-start | bytes 786440 | tf_op jit(solution)/shard_map/ppermute | solution.py:487
  36.5 1.3 %collective-permute-start.9 = (bf16[256,512]{1,0:T(8,128)(2,1)S(1)}, bf16[256,512]{1,0:T(8,128)(2,1)S(1)}, u32[]{:S(2)}, u32[]{:S(2)}) collective-permute-start(bf16[256,512]{1,0:T(8,128)(2,1)S(1)} %relay_4.3), channel_id=1, source_target_pairs={{4,0},{8,12},{5,1},{9,13},{6,2},{10,14},{7,3},{11,15},{20,16},{24,... | collective-permute-start | bytes 786440 | tf_op jit(solution)/shard_map/ppermute | solution.py:487
  37.8 1.5 %carried_1.1 = (bf16[512,2048]{1,0:T(8,128)(2,1)}, bf16[512,512]{1,0:T(8,128)(2,1)}, bf16[512,512]{1,0:T(8,128)(2,1)}) custom-call(bf16[256,512]{1,0:T(8,128)(2,1)S(1)} %collective-permute-done.3.refs_2_.refs_0_, bf16[256,512]{1,0:T(8,128)(2,1)S(1)} %collective-permute-done.4.refs_4_.refs_1_, ...), custom_call_target="tpu_custom_call", output_to_operand_aliasing={{0}: (11, {})} | custom-call | flops 402653184 | bytes 3670016 | tf_op jit(solution)/shard_map/carried_1/pallas_call | solution.py:432
  39.3 0.1 relay_5.1
  39.5 1.3 %collective-permute-start.7 = (bf16[256,512]{1,0:T(8,128)(2,1)S(1)}, bf16[256,512]{1,0:T(8,128)(2,1)S(1)}, u32[]{:S(2)}, u32[]{:S(2)}) collective-permute-start(bf16[256,512]{1,0:T(8,128)(2,1)S(1)} %relay_5.1), channel_id=1, source_target_pairs={{4,0},{8,12},{5,1},{9,13},{6,2},{10,14},{7,3},{11,15},{20,16},{24,... | collective-permute-start | bytes 786440 | tf_op jit(solution)/shard_map/ppermute | solution.py:487
  40.8 6.1 %collective-permute-done.9.refs_2_ = bf16[256,512]{1,0:T(8,128)(2,1)S(1)} collective-permute-done((bf16[256,512]{1,0:T(8,128)(2,1)S(1)}, bf16[256,512]{1,0:T(8,128)(2,1)S(1)}, u32[]{:S(2)}, u32[]{:S(2)}) %collective-permute-start.9) | collective-permute-done | bytes 262176 | tf_op jit(solution)/shard_map/ppermute | solution.py:487
  46.8 1.3 %carried_2.1 = (bf16[512,2048]{1,0:T(8,128)(2,1)}, f32[512,256]{1,0:T(8,128)S(1)}, f32[512,256]{1,0:T(8,128)S(1)}) custom-call(bf16[256,512]{1,0:T(8,128)(2,1)S(1)} %collective-permute-done.2.refs_2_.refs_4_.refs_0_, bf16[256,512]{1,0:T(8,128)(2,1)S(1)} %collective-permute-done.8.refs_4_.refs_1_, ...), custom_call_target="tpu_custom_call", output_to_operand_aliasing={{0}: (11, {})} | custom-call | flops 402653184 | bytes 3670016 | tf_op jit(solution)/shard_map/carried_2/pallas_call | solution.py:432
  48.1 3.6 %collective-permute-done.7.refs_2_ = bf16[256,512]{1,0:T(8,128)(2,1)S(1)} collective-permute-done((bf16[256,512]{1,0:T(8,128)(2,1)S(1)}, bf16[256,512]{1,0:T(8,128)(2,1)S(1)}, u32[]{:S(2)}, u32[]{:S(2)}) %collective-permute-start.7) | collective-permute-done | bytes 262176 | tf_op jit(solution)/shard_map/ppermute | solution.py:487
  51.7 1.4 %carried_3.1 = (bf16[512,2048]{1,0:T(8,128)(2,1)}, bf16[512,512]{1,0:T(8,128)(2,1)}, bf16[512,512]{1,0:T(8,128)(2,1)}) custom-call(bf16[256,512]{1,0:T(8,128)(2,1)S(1)} %collective-permute-done.5.refs_2_.refs_4_.refs_0_, bf16[256,512]{1,0:T(8,128)(2,1)S(1)} %collective-permute-done.6.refs_4_.refs_1_, ...), custom_call_target="tpu_custom_call", output_to_operand_aliasing={{0}: (11, {}), {1}: (12, {}), {2}: (13, {})} | custom-call | flops 402653184 | bytes 3670016 | tf_op jit(solution)/shard_map/carried_3/pallas_call | solution.py:432
  (22 shorter events, 0.8 us)
Async XLA Ops:
  2.5 10.6 %collective-permute-start = (bf16[256,512]{1,0:T(8,128)(2,1)S(1)}, bf16[256,512]{1,0:T(8,128)(2,1)S(1)}, u32[]{:S(2)}, u32[]{:S(2)}) collective-permute-start(bf16[256,512]{1,0:T(8,128)(2,1)S(1)} %first_state.1), channel_id=1, source_target_pairs={{0,4},{12,8},{1,5},{13,9},{2,6},{14,10},{3,7},{15,11},{16,20},{28,... | collective-permute-start | bytes 786440 | tf_op jit(solution)/shard_map/ppermute | solution.py:487
  8.8 8.0 %collective-permute-start.3 = (bf16[256,512]{1,0:T(8,128)(2,1)S(1)}, bf16[256,512]{1,0:T(8,128)(2,1)S(1)}, u32[]{:S(2)}, u32[]{:S(2)}) collective-permute-start(bf16[256,512]{1,0:T(8,128)(2,1)S(1)} %relay_1.2), channel_id=1, source_target_pairs={{0,4},{12,8},{1,5},{13,9},{2,6},{14,10},{3,7},{15,11},{16,20},{28,... | collective-permute-start | bytes 786440 | tf_op jit(solution)/shard_map/ppermute | solution.py:487
  13.2 4.5 %collective-permute-start.1 = (bf16[256,512]{1,0:T(8,128)(2,1)S(1)}, bf16[256,512]{1,0:T(8,128)(2,1)S(1)}, u32[]{:S(2)}, u32[]{:S(2)}) collective-permute-start(bf16[256,512]{1,0:T(8,128)(2,1)S(1)} %relay_1.3), channel_id=1, source_target_pairs={{4,8},{8,4},{5,9},{9,5},{6,10},{10,6},{7,11},{11,7},{20,24},{24,20... | collective-permute-start | bytes 786440 | tf_op jit(solution)/shard_map/ppermute | solution.py:487
  16.9 7.5 %copy-start = (bf16[512,512]{1,0:T(8,128)(2,1)S(1)}, bf16[512,512]{1,0:T(8,128)(2,1)}, u32[]{:S(2)}) copy-start(bf16[512,512]{1,0:T(8,128)(2,1)} %refs_5_.15) | copy-start | bytes 1572868
  16.9 7.4 %copy-start.1 = (bf16[512,2048]{1,0:T(8,128)(2,1)S(1)}, bf16[512,2048]{1,0:T(8,128)(2,1)}, u32[]{:S(2)}) copy-start(bf16[512,2048]{1,0:T(8,128)(2,1)} %refs_6_.3) | copy-start | bytes 6291460
  16.9 7.4 %copy-start.2 = (bf16[512,512]{1,0:T(8,128)(2,1)S(1)}, bf16[512,512]{1,0:T(8,128)(2,1)}, u32[]{:S(2)}) copy-start(bf16[512,512]{1,0:T(8,128)(2,1)} %refs_5_.12) | copy-start | bytes 1572868
  16.9 7.4 %copy-start.3 = (f32[32]{0:T(128)S(1)}, f32[32]{0:T(128)}, u32[]{:S(2)}) copy-start(f32[32]{0:T(128)} %param.13) | copy-start | bytes 388
  16.9 11.6 %collective-permute-start.4 = (bf16[256,512]{1,0:T(8,128)(2,1)S(1)}, bf16[256,512]{1,0:T(8,128)(2,1)S(1)}, u32[]{:S(2)}, u32[]{:S(2)}) collective-permute-start(bf16[256,512]{1,0:T(8,128)(2,1)S(1)} %relay_2.3), channel_id=1, source_target_pairs={{4,8},{8,4},{5,9},{9,5},{6,10},{10,6},{7,11},{11,7},{20,24},{24,20... | collective-permute-start | bytes 786440 | tf_op jit(solution)/shard_map/ppermute | solution.py:487
  17.9 12.2 %collective-permute-start.2 = (bf16[256,512]{1,0:T(8,128)(2,1)S(1)}, bf16[256,512]{1,0:T(8,128)(2,1)S(1)}, u32[]{:S(2)}, u32[]{:S(2)}) collective-permute-start(bf16[256,512]{1,0:T(8,128)(2,1)S(1)} %relay_2.2), channel_id=1, source_target_pairs={{0,4},{4,0},{8,12},{12,8},{1,5},{5,1},{9,13},{13,9},{2,6},{6,2},{1... | collective-permute-start | bytes 786440 | tf_op jit(solution)/shard_map/ppermute | solution.py:487
  28.6 7.0 %collective-permute-start.5 = (bf16[256,512]{1,0:T(8,128)(2,1)S(1)}, bf16[256,512]{1,0:T(8,128)(2,1)S(1)}, u32[]{:S(2)}, u32[]{:S(2)}) collective-permute-start(bf16[256,512]{1,0:T(8,128)(2,1)S(1)} %relay_3.2), channel_id=1, source_target_pairs={{0,4},{4,0},{8,12},{12,8},{1,5},{5,1},{9,13},{13,9},{2,6},{6,2},{1... | collective-permute-start | bytes 786440 | tf_op jit(solution)/shard_map/ppermute | solution.py:487
  30.2 6.2 %collective-permute-start.8 = (bf16[256,512]{1,0:T(8,128)(2,1)S(1)}, bf16[256,512]{1,0:T(8,128)(2,1)S(1)}, u32[]{:S(2)}, u32[]{:S(2)}) collective-permute-start(bf16[256,512]{1,0:T(8,128)(2,1)S(1)} %relay_3.3), channel_id=1, source_target_pairs={{4,8},{8,4},{5,9},{9,5},{6,10},{10,6},{7,11},{11,7},{20,24},{24,20... | collective-permute-start | bytes 786440 | tf_op jit(solution)/shard_map/ppermute | solution.py:487
  35.7 3.6 %collective-permute-start.6 = (bf16[256,512]{1,0:T(8,128)(2,1)S(1)}, bf16[256,512]{1,0:T(8,128)(2,1)S(1)}, u32[]{:S(2)}, u32[]{:S(2)}) collective-permute-start(bf16[256,512]{1,0:T(8,128)(2,1)S(1)} %relay_4.2), channel_id=1, source_target_pairs={{4,8},{8,4},{5,9},{9,5},{6,10},{10,6},{7,11},{11,7},{20,24},{24,20... | collective-permute-start | bytes 786440 | tf_op jit(solution)/shard_map/ppermute | solution.py:487
  36.5 10.3 %collective-permute-start.9 = (bf16[256,512]{1,0:T(8,128)(2,1)S(1)}, bf16[256,512]{1,0:T(8,128)(2,1)S(1)}, u32[]{:S(2)}, u32[]{:S(2)}) collective-permute-start(bf16[256,512]{1,0:T(8,128)(2,1)S(1)} %relay_4.3), channel_id=1, source_target_pairs={{4,0},{8,12},{5,1},{9,13},{6,2},{10,14},{7,3},{11,15},{20,16},{24,... | collective-permute-start | bytes 786440 | tf_op jit(solution)/shard_map/ppermute | solution.py:487
  39.5 12.3 %collective-permute-start.7 = (bf16[256,512]{1,0:T(8,128)(2,1)S(1)}, bf16[256,512]{1,0:T(8,128)(2,1)S(1)}, u32[]{:S(2)}, u32[]{:S(2)}) collective-permute-start(bf16[256,512]{1,0:T(8,128)(2,1)S(1)} %relay_5.1), channel_id=1, source_target_pairs={{4,0},{8,12},{5,1},{9,13},{6,2},{10,14},{7,3},{11,15},{20,16},{24,... | collective-permute-start | bytes 786440 | tf_op jit(solution)/shard_map/ppermute | solution.py:487

commit v7 on v5

--- a/solution.py
+++ b/solution.py
@@ -79,21 +79,26 @@
         return copy
 
     def state(wide, narrow, weigh):
-        copies = [
-            fetch(step_hbm, step, 0),
-            fetch(rate_hbm, rate, 1),
-            fetch(wide, rows_in, 2),
-            fetch(narrow, group_in, 3),
-        ]
-        upper = upper_ones(step.shape[1])
+        tokens = step.shape[1]
+        halves = [pl.ds(0, tokens // 2), pl.ds(tokens // 2, tokens // 2)]
+        copies = [fetch(step_hbm, step, 0), fetch(rate_hbm, rate, 1)]
+        copies.append(fetch(narrow, group_in, 2))
+        for place, half in enumerate(halves):
+            copies.append(fetch(wide.at[half], rows_in.at[half], 3 + place))
+        upper = upper_ones(tokens)
         copies[0].wait()
         copies[1].wait()
         cum = dot(step[...], upper, 1, 0) * columns(rate[...])
         spread = head_spread(terms(weigh(cum), 2), 0)
         copies[2].wait()
-        rows = (spread * rows_in[...].astype(F32)).astype(BF16)
-        copies[3].wait()
-        send[...] = dot(group_in[...], rows, 0, 0).astype(BF16)
+        total = None
+        for place, half in enumerate(halves):
+            copies[3 + place].wait()
+            low, high = place * (tokens // 2), (place + 1) * (tokens // 2)
+            rows = (spread[low:high] * rows_in[half].astype(F32)).astype(BF16)
+            part = dot(group_in[half], rows, 0, 0)
+            total = part if total is None else total + part
+        send[...] = total.astype(BF16)
 
     @pl.when(rank == 0)
     def _():
@@ -314,7 +319,7 @@
         + [
             pltpu.VMEM((tokens, CHUNK), BF16),
             pltpu.VMEM((tokens, N), BF16),
-            pltpu.SemaphoreType.DMA((4,)),
+            pltpu.SemaphoreType.DMA((5,)),
         ],
         compiler_params=PARAMS,
         cost_estimate=cost(2 * tokens * CHUNK * (N + 256), 4 * tokens * CHUNK),

time: 53.5 us -> 53.4 us (level)
  no operation moved by 1% of the time
where the time goes in v7:
time: 53.4 us; the launch traced here: 53.1 us
  Pallas kernels  18.6 us (35%)
  starting transfers between devices  17.6 us (33%)
  waiting for transfers between devices  16 us (30%)
  between operations  0.87 us (2%)
    ppermute x10, starting transfers between devices, on_device(): got[key] = lax.ppermute(send, 'ctx', links(turn, even_links))  17.6 us
    ppermute x10, waiting for transfers between devices, on_device(): got[key] = lax.ppermute(send, 'ctx', links(turn, even_links))  16 us
    pallas_call x2, Pallas kernels, local_states(): pl.pallas_call(partial(local_kernel, first=first, last=last, per_group=pe...  6.1 us
    pallas_call x4, Pallas kernels, carried(): pl.pallas_call(partial(carried_kernel, chunk=chunk, per_group=per_group,...  5.55 us
    pallas_call x2, Pallas kernels, within(): pl.pallas_call(partial(within_kernel, group=group, per_group=per_group, s...  4.29 us
    pallas_call x1, Pallas kernels, on_device(): pl.pallas_call(partial(first_kernel, ranks=ranks), in_specs=[ANYWHERE] *...  1.84 us
  transfers between devices with their start and end apart: 10, of which 4 were waited for; matrix products, arithmetic and copies ran while one was open for 0% of the time, Pallas kernels for 29%

profile of v7, /device:TPU:0, one launch (start us, length us, event | category | flops | bytes accessed | tf_op | source)
XLA Modules:
  0.0 53.1 jit_solution(1561582835606519699)
XLA Ops:
  0.6 1.8 %first_state.1 = bf16[256,512]{1,0:T(8,128)(2,1)S(1)} custom-call(bf16[32,512]{1,0:T(8,128)(2,1)} %bitcast.5, f32[1,32]{1,0:T(1,128)} %bitcast.7, bf16[512,2048]{1,0:T(8,128)(2,1)} %refs_6_.3, bf16[512,2048]{1,0:T(8,128)(2,1)} %refs_3_.3, bf16[512,512]{1,0:T(8,128)(2,1)} %refs_5_.15, bf16[512,512]{1,0:T(8,128)(2,1)} %refs_5_.12), custom_call_target="tpu_custom_call" | custom-call | flops 268435456 | bytes 1048576 | tf_op jit(solution)/shard_map/first_state/pallas_call | solution.py:313
  2.5 3.2 %collective-permute-start = (bf16[256,512]{1,0:T(8,128)(2,1)S(1)}, bf16[256,512]{1,0:T(8,128)(2,1)S(1)}, u32[]{:S(2)}, u32[]{:S(2)}) collective-permute-start(bf16[256,512]{1,0:T(8,128)(2,1)S(1)} %first_state.1), channel_id=1, source_target_pairs={{0,4},{12,8},{1,5},{13,9},{2,6},{14,10},{3,7},{15,11},{16,20},{28,... | collective-permute-start | bytes 786440 | tf_op jit(solution)/shard_map/ppermute | solution.py:475
  5.7 3.1 %states_0.1 = (bf16[512,1024]{1,0:T(8,128)(2,1)S(1)}, bf16[512,1024]{1,0:T(8,128)(2,1)S(1)}, f32[2,2,256,512]{3,2,1,0:T(8,128)S(1)}, f32[2,1,512]{2,1,0:T(1,128)...) custom-call(bf16[32,512]{1,0:T(8,128)(2,1)} %bitcast.6, f32[1,32]{1,0:T(1,128)} %bitcast.8, ...), custom_call_target="tpu_custom_call" | custom-call | flops 1610612736 | bytes 3145728 | tf_op jit(solution)/shard_map/states_0/pallas_call | solution.py:290
  8.8 1.3 %collective-permute-start.3 = (bf16[256,512]{1,0:T(8,128)(2,1)S(1)}, bf16[256,512]{1,0:T(8,128)(2,1)S(1)}, u32[]{:S(2)}, u32[]{:S(2)}) collective-permute-start(bf16[256,512]{1,0:T(8,128)(2,1)S(1)} %relay_1.2), channel_id=1, source_target_pairs={{0,4},{12,8},{1,5},{13,9},{2,6},{14,10},{3,7},{15,11},{16,20},{28,... | collective-permute-start | bytes 786440 | tf_op jit(solution)/shard_map/ppermute | solution.py:475
  10.1 3.0 %states_2.1 = (bf16[512,1024]{1,0:T(8,128)(2,1)S(1)}, bf16[512,1024]{1,0:T(8,128)(2,1)S(1)}, f32[2,2,256,512]{3,2,1,0:T(8,128)S(1)}, f32[2,1,512]{2,1,0:T(1,128)S(1)}) custom-call(bf16[2,32,512]{2,1,0:T(8,128)(2,1)S(1)} %get-tuple-element.56.refs_0_, bf16[2,32,512]{2,1,0:T(8,128)(2,1)S(1)} %get-tuple-element.69.refs_1_.refs_7_, bf16[512,2048]{1,0:T(8,128)(2,1)} %refs_6_.3, ...), custom_call_target="tpu_custom_call" | custom-call | flops 1610612736 | bytes 3145728 | tf_op jit(solution)/shard_map/states_2/pallas_call | solution.py:290
  13.2 0.7 %collective-permute-start.1 = (bf16[256,512]{1,0:T(8,128)(2,1)S(1)}, bf16[256,512]{1,0:T(8,128)(2,1)S(1)}, u32[]{:S(2)}, u32[]{:S(2)}) collective-permute-start(bf16[256,512]{1,0:T(8,128)(2,1)S(1)} %relay_1.3), channel_id=1, source_target_pairs={{4,8},{8,4},{5,9},{9,5},{6,10},{10,6},{7,11},{11,7},{20,24},{24,20... | collective-permute-start | bytes 786440 | tf_op jit(solution)/shard_map/ppermute | solution.py:475
  13.9 2.9 %collective-permute-done.3.refs_2_.refs_0_ = bf16[256,512]{1,0:T(8,128)(2,1)S(1)} collective-permute-done((bf16[256,512]{1,0:T(8,128)(2,1)S(1)}, bf16[256,512]{1,0:T(8,128)(2,1)S(1)}, u32[]{:S(2)}, u32[]{:S(2)}) %collective-permute-start.3) | collective-permute-done | bytes 262176 | tf_op jit(solution)/shard_map/ppermute | solution.py:475
  16.9 0.8 %collective-permute-start.4 = (bf16[256,512]{1,0:T(8,128)(2,1)S(1)}, bf16[256,512]{1,0:T(8,128)(2,1)S(1)}, u32[]{:S(2)}, u32[]{:S(2)}) collective-permute-start(bf16[256,512]{1,0:T(8,128)(2,1)S(1)} %relay_2.3), channel_id=1, source_target_pairs={{4,8},{8,4},{5,9},{9,5},{6,10},{10,6},{7,11},{11,7},{20,24},{24,20... | collective-permute-start | bytes 786440 | tf_op jit(solution)/shard_map/ppermute | solution.py:475
  17.8 0.1 relay_2.2
  17.9 6.4 %collective-permute-start.2 = (bf16[256,512]{1,0:T(8,128)(2,1)S(1)}, bf16[256,512]{1,0:T(8,128)(2,1)S(1)}, u32[]{:S(2)}, u32[]{:S(2)}) collective-permute-start(bf16[256,512]{1,0:T(8,128)(2,1)S(1)} %relay_2.2), channel_id=1, source_target_pairs={{0,4},{4,0},{8,12},{12,8},{1,5},{5,1},{9,13},{13,9},{2,6},{6,2},{1... | collective-permute-start | bytes 786440 | tf_op jit(solution)/shard_map/ppermute | solution.py:475
  24.3 2.2 %within_0.1 = (f32[512,1024]{1,0:T(8,128)S(1)}, f32[512,256]{1,0:T(8,128)S(1)}, f32[512,256]{1,0:T(8,128)S(1)}, f32[512,1024]{1,0:T(8,128)S(1)}) custom-call(bf16[512,1024]{1,0:T(8,128)(2,1)S(1)} %get-tuple-element.65.refs_0_.refs_3_, bf16[512,1024]{1,0:T(8,128)(2,1)S(1)} %get-tuple-element.67.refs_1_.refs_3_, ...), custom_call_target="tpu_custom_call" | custom-call | flops 1610612736 | bytes 5242880 | tf_op jit(solution)/shard_map/within_0/pallas_call | solution.py:348
  26.4 2.1 %within_1.1 = (f32[512,1024]{1,0:T(8,128)S(1)}, f32[512,256]{1,0:T(8,128)S(1)}, f32[512,256]{1,0:T(8,128)S(1)}, f32[512,1024]{1,0:T(8,128)S(1)}) custom-call(bf16[512,1024]{1,0:T(8,128)(2,1)S(1)} %get-tuple-element.65.refs_0_.refs_3_, bf16[512,1024]{1,0:T(8,128)(2,1)S(1)} %get-tuple-element.67.refs_1_.refs_3_, ...), custom_call_target="tpu_custom_call" | custom-call | flops 1610612736 | bytes 5242880 | tf_op jit(solution)/shard_map/within_1/pallas_call | solution.py:348
  28.7 1.3 %collective-permute-start.5 = (bf16[256,512]{1,0:T(8,128)(2,1)S(1)}, bf16[256,512]{1,0:T(8,128)(2,1)S(1)}, u32[]{:S(2)}, u32[]{:S(2)}) collective-permute-start(bf16[256,512]{1,0:T(8,128)(2,1)S(1)} %relay_3.2), channel_id=1, source_target_pairs={{0,4},{4,0},{8,12},{12,8},{1,5},{5,1},{9,13},{13,9},{2,6},{6,2},{1... | collective-permute-start | bytes 786440 | tf_op jit(solution)/shard_map/ppermute | solution.py:475
  30.1 0.7 %collective-permute-start.8 = (bf16[256,512]{1,0:T(8,128)(2,1)S(1)}, bf16[256,512]{1,0:T(8,128)(2,1)S(1)}, u32[]{:S(2)}, u32[]{:S(2)}) collective-permute-start(bf16[256,512]{1,0:T(8,128)(2,1)S(1)} %relay_3.3), channel_id=1, source_target_pairs={{4,8},{8,4},{5,9},{9,5},{6,10},{10,6},{7,11},{11,7},{20,24},{24,20... | collective-permute-start | bytes 786440 | tf_op jit(solution)/shard_map/ppermute | solution.py:475
  30.8 1.3 %carried_0.1 = (bf16[512,2048]{1,0:T(8,128)(2,1)}, f32[512,256]{1,0:T(8,128)S(1)}, f32[512,256]{1,0:T(8,128)S(1)}) custom-call(bf16[256,512]{1,0:T(8,128)(2,1)S(1)} %collective-permute-done.refs_2_.refs_0_, bf16[256,512]{1,0:T(8,128)(2,1)S(1)} %collective-permute-done.1.refs_4_.refs_1_, bf16[256,512]{1,0:T(8,128)(2,1)S(1)} %collective-permute-done.2.refs_2_.refs_4_.refs_0_, ...), custom_call_target="tpu_custom_call" | custom-call | flops 402653184 | bytes 3670016 | tf_op jit(solution)/shard_map/carried_0/pallas_call | solution.py:420
  32.1 3.6 %collective-permute-done.5.refs_2_.refs_4_.refs_0_ = bf16[256,512]{1,0:T(8,128)(2,1)S(1)} collective-permute-done((bf16[256,512]{1,0:T(8,128)(2,1)S(1)}, bf16[256,512]{1,0:T(8,128)(2,1)S(1)}, u32[]{:S(2)}, u32[]{:S(2)}) %collective-permute-start.5) | collective-permute-done | bytes 262176 | tf_op jit(solution)/shard_map/ppermute | solution.py:475
  35.8 0.7 %collective-permute-start.6 = (bf16[256,512]{1,0:T(8,128)(2,1)S(1)}, bf16[256,512]{1,0:T(8,128)(2,1)S(1)}, u32[]{:S(2)}, u32[]{:S(2)}) collective-permute-start(bf16[256,512]{1,0:T(8,128)(2,1)S(1)} %relay_4.2), channel_id=1, source_target_pairs={{4,8},{8,4},{5,9},{9,5},{6,10},{10,6},{7,11},{11,7},{20,24},{24,20... | collective-permute-start | bytes 786440 | tf_op jit(solution)/shard_map/ppermute | solution.py:475
  36.6 1.3 %collective-permute-start.9 = (bf16[256,512]{1,0:T(8,128)(2,1)S(1)}, bf16[256,512]{1,0:T(8,128)(2,1)S(1)}, u32[]{:S(2)}, u32[]{:S(2)}) collective-permute-start(bf16[256,512]{1,0:T(8,128)(2,1)S(1)} %relay_4.3), channel_id=1, source_target_pairs={{4,0},{8,12},{5,1},{9,13},{6,2},{10,14},{7,3},{11,15},{20,16},{24,... | collective-permute-start | bytes 786440 | tf_op jit(solution)/shard_map/ppermute | solution.py:475
  37.9 1.5 %carried_1.1 = (bf16[512,2048]{1,0:T(8,128)(2,1)}, bf16[512,512]{1,0:T(8,128)(2,1)}, bf16[512,512]{1,0:T(8,128)(2,1)}) custom-call(bf16[256,512]{1,0:T(8,128)(2,1)S(1)} %collective-permute-done.3.refs_2_.refs_0_, bf16[256,512]{1,0:T(8,128)(2,1)S(1)} %collective-permute-done.4.refs_4_.refs_1_, ...), custom_call_target="tpu_custom_call", output_to_operand_aliasing={{0}: (11, {})} | custom-call | flops 402653184 | bytes 3670016 | tf_op jit(solution)/shard_map/carried_1/pallas_call | solution.py:420
  39.5 1.3 %collective-permute-start.7 = (bf16[256,512]{1,0:T(8,128)(2,1)S(1)}, bf16[256,512]{1,0:T(8,128)(2,1)S(1)}, u32[]{:S(2)}, u32[]{:S(2)}) collective-permute-start(bf16[256,512]{1,0:T(8,128)(2,1)S(1)} %relay_5.1), channel_id=1, source_target_pairs={{4,0},{8,12},{5,1},{9,13},{6,2},{10,14},{7,3},{11,15},{20,16},{24,... | collective-permute-start | bytes 786440 | tf_op jit(solution)/shard_map/ppermute | solution.py:475
  40.8 5.9 %collective-permute-done.9.refs_2_ = bf16[256,512]{1,0:T(8,128)(2,1)S(1)} collective-permute-done((bf16[256,512]{1,0:T(8,128)(2,1)S(1)}, bf16[256,512]{1,0:T(8,128)(2,1)S(1)}, u32[]{:S(2)}, u32[]{:S(2)}) %collective-permute-start.9) | collective-permute-done | bytes 262176 | tf_op jit(solution)/shard_map/ppermute | solution.py:475
  46.7 1.3 %carried_2.1 = (bf16[512,2048]{1,0:T(8,128)(2,1)}, f32[512,256]{1,0:T(8,128)S(1)}, f32[512,256]{1,0:T(8,128)S(1)}) custom-call(bf16[256,512]{1,0:T(8,128)(2,1)S(1)} %collective-permute-done.2.refs_2_.refs_4_.refs_0_, bf16[256,512]{1,0:T(8,128)(2,1)S(1)} %collective-permute-done.8.refs_4_.refs_1_, ...), custom_call_target="tpu_custom_call", output_to_operand_aliasing={{0}: (11, {})} | custom-call | flops 402653184 | bytes 3670016 | tf_op jit(solution)/shard_map/carried_2/pallas_call | solution.py:420
  48.0 3.6 %collective-permute-done.7.refs_2_ = bf16[256,512]{1,0:T(8,128)(2,1)S(1)} collective-permute-done((bf16[256,512]{1,0:T(8,128)(2,1)S(1)}, bf16[256,512]{1,0:T(8,128)(2,1)S(1)}, u32[]{:S(2)}, u32[]{:S(2)}) %collective-permute-start.7) | collective-permute-done | bytes 262176 | tf_op jit(solution)/shard_map/ppermute | solution.py:475
  51.7 1.4 %carried_3.1 = (bf16[512,2048]{1,0:T(8,128)(2,1)}, bf16[512,512]{1,0:T(8,128)(2,1)}, bf16[512,512]{1,0:T(8,128)(2,1)}) custom-call(bf16[256,512]{1,0:T(8,128)(2,1)S(1)} %collective-permute-done.5.refs_2_.refs_4_.refs_0_, bf16[256,512]{1,0:T(8,128)(2,1)S(1)} %collective-permute-done.6.refs_4_.refs_1_, ...), custom_call_target="tpu_custom_call", output_to_operand_aliasing={{0}: (11, {}), {1}: (12, {}), {2}: (13, {})} | custom-call | flops 402653184 | bytes 3670016 | tf_op jit(solution)/shard_map/carried_3/pallas_call | solution.py:420
  (22 shorter events, 0.8 us)
Async XLA Ops:
  2.5 10.7 %collective-permute-start = (bf16[256,512]{1,0:T(8,128)(2,1)S(1)}, bf16[256,512]{1,0:T(8,128)(2,1)S(1)}, u32[]{:S(2)}, u32[]{:S(2)}) collective-permute-start(bf16[256,512]{1,0:T(8,128)(2,1)S(1)} %first_state.1), channel_id=1, source_target_pairs={{0,4},{12,8},{1,5},{13,9},{2,6},{14,10},{3,7},{15,11},{16,20},{28,... | collective-permute-start | bytes 786440 | tf_op jit(solution)/shard_map/ppermute | solution.py:475
  8.8 8.0 %collective-permute-start.3 = (bf16[256,512]{1,0:T(8,128)(2,1)S(1)}, bf16[256,512]{1,0:T(8,128)(2,1)S(1)}, u32[]{:S(2)}, u32[]{:S(2)}) collective-permute-start(bf16[256,512]{1,0:T(8,128)(2,1)S(1)} %relay_1.2), channel_id=1, source_target_pairs={{0,4},{12,8},{1,5},{13,9},{2,6},{14,10},{3,7},{15,11},{16,20},{28,... | collective-permute-start | bytes 786440 | tf_op jit(solution)/shard_map/ppermute | solution.py:475
  13.2 4.5 %collective-permute-start.1 = (bf16[256,512]{1,0:T(8,128)(2,1)S(1)}, bf16[256,512]{1,0:T(8,128)(2,1)S(1)}, u32[]{:S(2)}, u32[]{:S(2)}) collective-permute-start(bf16[256,512]{1,0:T(8,128)(2,1)S(1)} %relay_1.3), channel_id=1, source_target_pairs={{4,8},{8,4},{5,9},{9,5},{6,10},{10,6},{7,11},{11,7},{20,24},{24,20... | collective-permute-start | bytes 786440 | tf_op jit(solution)/shard_map/ppermute | solution.py:475
  16.9 7.4 %copy-start = (bf16[512,512]{1,0:T(8,128)(2,1)S(1)}, bf16[512,512]{1,0:T(8,128)(2,1)}, u32[]{:S(2)}) copy-start(bf16[512,512]{1,0:T(8,128)(2,1)} %refs_5_.15) | copy-start | bytes 1572868
  16.9 7.4 %copy-start.1 = (bf16[512,2048]{1,0:T(8,128)(2,1)S(1)}, bf16[512,2048]{1,0:T(8,128)(2,1)}, u32[]{:S(2)}) copy-start(bf16[512,2048]{1,0:T(8,128)(2,1)} %refs_6_.3) | copy-start | bytes 6291460
  16.9 7.4 %copy-start.2 = (bf16[512,512]{1,0:T(8,128)(2,1)S(1)}, bf16[512,512]{1,0:T(8,128)(2,1)}, u32[]{:S(2)}) copy-start(bf16[512,512]{1,0:T(8,128)(2,1)} %refs_5_.12) | copy-start | bytes 1572868
  16.9 7.4 %copy-start.3 = (f32[32]{0:T(128)S(1)}, f32[32]{0:T(128)}, u32[]{:S(2)}) copy-start(f32[32]{0:T(128)} %param.13) | copy-start | bytes 388
  16.9 11.6 %collective-permute-start.4 = (bf16[256,512]{1,0:T(8,128)(2,1)S(1)}, bf16[256,512]{1,0:T(8,128)(2,1)S(1)}, u32[]{:S(2)}, u32[]{:S(2)}) collective-permute-start(bf16[256,512]{1,0:T(8,128)(2,1)S(1)} %relay_2.3), channel_id=1, source_target_pairs={{4,8},{8,4},{5,9},{9,5},{6,10},{10,6},{7,11},{11,7},{20,24},{24,20... | collective-permute-start | bytes 786440 | tf_op jit(solution)/shard_map/ppermute | solution.py:475
  17.9 12.1 %collective-permute-start.2 = (bf16[256,512]{1,0:T(8,128)(2,1)S(1)}, bf16[256,512]{1,0:T(8,128)(2,1)S(1)}, u32[]{:S(2)}, u32[]{:S(2)}) collective-permute-start(bf16[256,512]{1,0:T(8,128)(2,1)S(1)} %relay_2.2), channel_id=1, source_target_pairs={{0,4},{4,0},{8,12},{12,8},{1,5},{5,1},{9,13},{13,9},{2,6},{6,2},{1... | collective-permute-start | bytes 786440 | tf_op jit(solution)/shard_map/ppermute | solution.py:475
  28.7 7.0 %collective-permute-start.5 = (bf16[256,512]{1,0:T(8,128)(2,1)S(1)}, bf16[256,512]{1,0:T(8,128)(2,1)S(1)}, u32[]{:S(2)}, u32[]{:S(2)}) collective-permute-start(bf16[256,512]{1,0:T(8,128)(2,1)S(1)} %relay_3.2), channel_id=1, source_target_pairs={{0,4},{4,0},{8,12},{12,8},{1,5},{5,1},{9,13},{13,9},{2,6},{6,2},{1... | collective-permute-start | bytes 786440 | tf_op jit(solution)/shard_map/ppermute | solution.py:475
  30.1 6.4 %collective-permute-start.8 = (bf16[256,512]{1,0:T(8,128)(2,1)S(1)}, bf16[256,512]{1,0:T(8,128)(2,1)S(1)}, u32[]{:S(2)}, u32[]{:S(2)}) collective-permute-start(bf16[256,512]{1,0:T(8,128)(2,1)S(1)} %relay_3.3), channel_id=1, source_target_pairs={{4,8},{8,4},{5,9},{9,5},{6,10},{10,6},{7,11},{11,7},{20,24},{24,20... | collective-permute-start | bytes 786440 | tf_op jit(solution)/shard_map/ppermute | solution.py:475
  35.8 3.6 %collective-permute-start.6 = (bf16[256,512]{1,0:T(8,128)(2,1)S(1)}, bf16[256,512]{1,0:T(8,128)(2,1)S(1)}, u32[]{:S(2)}, u32[]{:S(2)}) collective-permute-start(bf16[256,512]{1,0:T(8,128)(2,1)S(1)} %relay_4.2), channel_id=1, source_target_pairs={{4,8},{8,4},{5,9},{9,5},{6,10},{10,6},{7,11},{11,7},{20,24},{24,20... | collective-permute-start | bytes 786440 | tf_op jit(solution)/shard_map/ppermute | solution.py:475
  36.6 10.1 %collective-permute-start.9 = (bf16[256,512]{1,0:T(8,128)(2,1)S(1)}, bf16[256,512]{1,0:T(8,128)(2,1)S(1)}, u32[]{:S(2)}, u32[]{:S(2)}) collective-permute-start(bf16[256,512]{1,0:T(8,128)(2,1)S(1)} %relay_4.3), channel_id=1, source_target_pairs={{4,0},{8,12},{5,1},{9,13},{6,2},{10,14},{7,3},{11,15},{20,16},{24,... | collective-permute-start | bytes 786440 | tf_op jit(solution)/shard_map/ppermute | solution.py:475
  39.5 12.1 %collective-permute-start.7 = (bf16[256,512]{1,0:T(8,128)(2,1)S(1)}, bf16[256,512]{1,0:T(8,128)(2,1)S(1)}, u32[]{:S(2)}, u32[]{:S(2)}) collective-permute-start(bf16[256,512]{1,0:T(8,128)(2,1)S(1)} %relay_5.1), channel_id=1, source_target_pairs={{4,0},{8,12},{5,1},{9,13},{6,2},{10,14},{7,3},{11,15},{20,16},{24,... | collective-permute-start | bytes 786440 | tf_op jit(solution)/shard_map/ppermute | solution.py:475
